TPU v7x, 512 devices: a whole 4x4x16 slice. The times are simulated.
512 devices in a mesh: wide: 64 (over y, z), narrow: 8 (over x, core).
Axes of the slice: x: 4, y: 4, z: 16, core: 2. Of those that a mesh axis runs over, the one named last changes fastest.
Arguments:
- right_side: float32 [16384, 1024], P(('wide', 'narrow')), may hold values from -6 to 6
- start_guess: float32 [16384, 1024], P(('wide', 'narrow')), may hold values from -6 to 6
- block_diag: float32 [16384, 4096], P(('wide', 'narrow')), may hold values from -0.375 to 0.375
- face_lift: float32 [6, 64, 64], replicated, may hold values from -0.75 to 0.75
- face_scale: float32 [16384, 6], P(('wide', 'narrow')), may hold values from 0.05 to 0.2
- neighbors: int32 [16384, 6], P(('wide', 'narrow')), may hold values from 0 to 40, as said below
- ghost_send: int32 [512, 8], P(('wide', 'narrow')), may hold values from 0 to 31, as said below
Outputs:
- solution: float32 [16384, 1024], P(('wide', 'narrow'))
- new_residual: float32 [16384, 1024], P(('wide', 'narrow'))
Inputs may be any that keep to these rules, and one draw needn't show every extreme that they name: `neighbors`: values below 32 name the device's own elements, 32 + k the k-th ghost from the previous device, 36 + k the k-th ghost from the next device, 40 the zero row; the first device names no ghost of a previous device and the last none of a next device. `ghost_send`: each row holds 8 distinct own elements of that device.
All inputs are finite; a program needn't handle non-finite values.
Results may differ from a plain program's by a relative error of at most 0.0003.
Values sent between devices are 32-bit elements; how exact they have to be, the bound alone decides.
No kernel may reach another device: no remote copies, remote signals or barrier semaphores. Data moves between devices by JAX's collectives and lax.ppermute only.
A program may use at most 64 MiB of HBM per device.

v0:
```python
import functools

import jax
import jax.numpy as jnp
from jax import lax
from jax.experimental import pallas as pl
from jax.experimental.pallas import tpu as pltpu
from jax.sharding import Mesh, PartitionSpec as P

STEPS = 4
GAIN = 1.5
RHS = 16
NODES = 64
FACES = 6
ELEMS = 32
GHOST = 4
F32 = jnp.float32
BF16 = jnp.bfloat16


VMEM = pl.BlockSpec(memory_space=pltpu.VMEM)
SMEM = pl.BlockSpec(memory_space=pltpu.SMEM)
PARAMS = pltpu.CompilerParams(vmem_limit_bytes=32 * 1024 * 1024)


def tiles(count):
    return jax.ShapeDtypeStruct((count, 8, 128), F32)


def dot_nt(left, right):
    return lax.dot_general(left, right, (((1,), (1,)), ((), ())), preferred_element_type=F32)


def split(value):
    high = value.astype(BF16)
    low = (value - high.astype(F32)).astype(BF16)
    return high, low


def swap(value):
    return pltpu.roll(value, 64, 1)


def left_half(shape):
    return lax.broadcasted_iota(jnp.int32, shape, len(shape) - 1) < 64


def to_tiles(ref, out):
    for t in range(8):
        out[:, t, :] = ref[:, t * 128 : (t + 1) * 128]


def send_rows(send, source, to_prev, to_next):
    for k in range(GHOST):
        to_prev[k] = source[send[k]]
        to_next[k] = source[send[GHOST + k]]


def pack_kernel(send, guess, tiled, to_prev, to_next):
    to_tiles(guess, tiled)
    send_rows(send, tiled, to_prev, to_next)


def prep_kernel(blocks, lift, right, block_parts, lift_parts, right_tiled):
    high, low = split(blocks[...])
    block_parts[:, :128] = high
    block_parts[:, 128:] = low
    high, low = split(lift[...])
    lift_parts[:, :128] = high
    lift_parts[:, 128:256] = high
    lift_parts[:, 256:] = low
    to_tiles(right, right_tiled)


def lifted(vector, lift_parts):
    high, low = split(vector)
    return dot_nt(jnp.concatenate([high, low, high], 1), lift_parts[...])


def gather_faces(total, element, neighbors, scale, source, place):
    for f in range(FACES):
        row = element * FACES + f
        total = total + scale[row] * source[f, place(neighbors[row])]
    return total


def dense(vector):
    upper, lower = [], []
    mask = left_half((8, 128))
    for pair in range(ELEMS // 2):
        first, second = vector[2 * pair], vector[2 * pair + 1]
        upper.append(jnp.where(mask, first, swap(second)))
        lower.append(jnp.where(mask, swap(first), second))
    return jnp.concatenate([jnp.concatenate(upper, 1), jnp.concatenate(lower, 1)], 0)


def own_part(vector, block_parts, lift_parts, neighbors, scale, out, own_lifted):
    value = vector[...].reshape(ELEMS * 8, 128)
    product = lifted(value, lift_parts)
    for f in range(FACES):
        own_lifted[f, :ELEMS] = product[:, f * 128 : (f + 1) * 128].reshape(ELEMS, 8, 128)
        own_lifted[f, ELEMS] = jnp.zeros((8, 128), F32)
    mask = left_half((ELEMS * 8, 128))
    high, low = split(value)
    high, low = high.astype(F32), low.astype(F32)
    turned_high, turned_low = swap(high), swap(low)
    first = jnp.where(mask, low, turned_high).astype(BF16)
    second = jnp.where(mask, turned_low, high).astype(BF16)
    first_rest = jnp.where(mask, high, 0.0).astype(BF16)
    second_rest = jnp.where(mask, 0.0, high).astype(BF16)
    first = jnp.concatenate([first, first_rest], 1)
    second = jnp.concatenate([second, second_rest], 1)
    mask = left_half((8, 128))
    for group in range(ELEMS // 4):
        rows = slice(group * 32, (group + 1) * 32)
        both = jnp.concatenate([first[rows], second[rows]], 0)
        result = dot_nt(both, block_parts[group * 256 : (group + 1) * 256, :])
        for part in range(4):
            lanes = slice((part // 2) * 128, (part // 2) * 128 + 128)
            top = result[part * 8 : part * 8 + 8, lanes]
            bottom = result[32 + part * 8 : 40 + part * 8, lanes]
            if part % 2 == 0:
                total = jnp.where(mask, top, swap(bottom))
            else:
                total = jnp.where(mask, swap(top), bottom)
            element = group * 4 + part
            out[element] = gather_faces(
                total, element, neighbors, scale, own_lifted, lambda n: jnp.minimum(n, ELEMS)
            )


def gram_rows(stack_high, stack_low, newest, count):
    high, low = split(newest)
    left = jnp.concatenate([high, high, low], 1)
    right = jnp.concatenate([stack_high, stack_low, stack_high], 1)
    return dot_nt(left, right)


def first_own_kernel(neighbors, scale, vector, block_parts, lift_parts, out, own_lifted):
    own_part(vector, block_parts, lift_parts, neighbors, scale, out, own_lifted)


def own_kernel(index, neighbors, scale, vector, block_parts, lift_parts, *rest):
    if index:
        old_high, old_low, out, gram, high_out, low_out, own_lifted = rest
    else:
        out, gram, high_out, low_out, own_lifted = rest
    own_part(vector, block_parts, lift_parts, neighbors, scale, out, own_lifted)
    new_gram(index, vector, old_high if index else None, old_low if index else None, gram, high_out, low_out)


def new_gram(index, vector, old_high, old_low, gram, high_out, low_out):
    newest = dense(vector)
    high, low = split(newest)
    if index:
        high_out[: 16 * index] = old_high[...]
        low_out[: 16 * index] = old_low[...]
    high_out[16 * index :] = high
    low_out[16 * index :] = low
    gram[...] = gram_rows(high_out[...], low_out[...], newest, index + 1)


def ghost_total(own, from_prev, from_next, lift_parts, neighbors, scale, ghost_lifted):
    ghosts = jnp.concatenate([from_prev[...], from_next[...]], 0).reshape(2 * GHOST * 8, 128)
    product = lifted(ghosts, lift_parts)
    for f in range(FACES):
        ghost_lifted[f, : 2 * GHOST] = product[:, f * 128 : (f + 1) * 128].reshape(2 * GHOST, 8, 128)
        ghost_lifted[f, 2 * GHOST] = jnp.zeros((8, 128), F32)
    place = lambda n: jnp.where(n >= ELEMS, n - ELEMS, 2 * GHOST)
    for element in range(ELEMS):
        yield element, gather_faces(own[element], element, neighbors, scale, ghost_lifted, place)


def first_ghost_kernel(
    neighbors, scale, send, own, from_prev, from_next, lift_parts, right, guess,
    out, to_prev, to_next, ghost_lifted,
):
    for element, total in ghost_total(own, from_prev, from_next, lift_parts, neighbors, scale, ghost_lifted):
        out[element] = right[element] - (guess[element] + total)
    send_rows(send, out, to_prev, to_next)


def ghost_kernel(
    neighbors, scale, send, own, from_prev, from_next, lift_parts,
    out, to_prev, to_next, ghost_lifted,
):
    for element, total in ghost_total(own, from_prev, from_next, lift_parts, neighbors, scale, ghost_lifted):
        out[element] = GAIN * total
    send_rows(send, out, to_prev, to_next)


def last_kernel(
    neighbors, scale, own, from_prev, from_next, lift_parts, old_high, old_low,
    gram0, gram1, gram2, gram3, high_out, low_out, packed, ghost_lifted, newest, gram4,
):
    for element, total in ghost_total(own, from_prev, from_next, lift_parts, neighbors, scale, ghost_lifted):
        newest[element] = GAIN * total
    new_gram(STEPS, newest, old_high, old_low, gram4, high_out, low_out)
    packed[0:16] = jnp.concatenate([gram4[...], gram1[...], gram0[...]], 1)
    packed[16:32] = jnp.concatenate([gram3[...], gram2[...], jnp.zeros((16, 16), F32)], 1)


def solve_spd(system):
    size, block = 64, 4
    row_id = lax.broadcasted_iota(jnp.int32, (size, 128), 0)
    for start in range(0, size, block):
        columns = [jnp.broadcast_to(system[:, start + j : start + j + 1], (size, 128)) for j in range(block)]
        rows = [system[start + i : start + i + 1, :] for i in range(block)]
        pivots = [[columns[j][start + i : start + i + 1, :] for j in range(block)] for i in range(block)]
        for j in range(block):
            inverse = 1.0 / pivots[j][j]
            rows[j] = rows[j] * inverse
            for l in range(j + 1, block):
                pivots[j][l] = pivots[j][l] * inverse
            for i in range(block):
                if i != j:
                    factor = pivots[i][j]
                    rows[i] = rows[i] - factor * rows[j]
                    for l in range(j + 1, block):
                        pivots[i][l] = pivots[i][l] - factor * pivots[j][l]
        update = system
        for j in range(block):
            update = update - columns[j] * rows[j]
        for j in range(block):
            update = jnp.where(row_id == start + j, rows[j], update)
        system = update
    return system


def solve_kernel(packed, high, low, first, guess, solution, residual, gram_low, tiled):
    total = jnp.sum(packed[...], 0)
    upper, lower = total[:16], total[16:]
    lane = lax.broadcasted_iota(jnp.int32, (16, 128), 1)
    pieces = [
        (pltpu.roll(upper, 16, 1), 16),
        (pltpu.roll(upper, 48, 1), 32),
        (pltpu.roll(lower, 64, 1), 48),
        (lower, 64),
        (upper, 80),
    ]
    for a, (piece, width) in enumerate(pieces):
        gram_low[16 * a : 16 * a + 16, :] = jnp.where(lane < width, piece, 0.0)
    gram_low[80:, :] = jnp.zeros((48, 128), F32)
    lower_part = gram_low[...]
    row = lax.broadcasted_iota(jnp.int32, (128, 128), 0) // 16
    column = lax.broadcasted_iota(jnp.int32, (128, 128), 1) // 16
    gram = jnp.where(row >= column, lower_part, lower_part.T)
    weighted = gram[:64] + gram[16:80] * (1.0 / GAIN)
    lane = lax.broadcasted_iota(jnp.int32, (64, 128), 1)
    normal = weighted + pltpu.roll(weighted, 112, 1) * (1.0 / GAIN)
    system = jnp.where(lane < 64, normal, pltpu.roll(weighted, 64, 1))
    system = jnp.where(lane < 80, system, 0.0)
    coeffs = pltpu.roll(solve_spd(system), 64, 1)
    empty = jnp.zeros((16, 128), F32)
    padded = jnp.concatenate([coeffs, empty], 0)
    mixed = padded + jnp.concatenate([empty, coeffs], 0) * (1.0 / GAIN)
    lane = lax.broadcasted_iota(jnp.int32, (80, 128), 1)
    both = jnp.where(lane < 16, padded, pltpu.roll(mixed, 16, 1))
    both = jnp.where(lane < 32, both, 0.0)
    both = jnp.concatenate([both, jnp.zeros((48, 128), F32)], 0).T[:32]
    mask_high, mask_low = split(both)
    change = jnp.dot(mask_high[:, :80], high[...], preferred_element_type=F32)
    change = change + jnp.dot(mask_high[:, :80], low[...], preferred_element_type=F32)
    change = change + jnp.dot(mask_low[:, :80], high[...], preferred_element_type=F32)
    mask = left_half((8, 128))
    for pair in range(ELEMS // 2):
        lanes = slice(pair * 128, pair * 128 + 128)
        top, bottom = change[0:8, lanes], change[8:16, lanes]
        tiled[0, 2 * pair] = jnp.where(mask, top, swap(bottom))
        tiled[0, 2 * pair + 1] = jnp.where(mask, swap(top), bottom)
        top, bottom = change[16:24, lanes], change[24:32, lanes]
        tiled[1, 2 * pair] = first[2 * pair] - jnp.where(mask, top, swap(bottom))
        tiled[1, 2 * pair + 1] = first[2 * pair + 1] - jnp.where(mask, swap(top), bottom)
    for t in range(8):
        lanes = slice(t * 128, t * 128 + 128)
        solution[:, lanes] = guess[:, lanes] + tiled[0, :, t, :]
        residual[:, lanes] = tiled[1, :, t, :]


def call(kernel, outs, scratch, specs):
    return pl.pallas_call(
        kernel,
        out_shape=outs,
        in_specs=specs,
        out_specs=[VMEM] * len(outs),
        scratch_shapes=scratch,
        compiler_params=PARAMS,
    )


def shifted(block, axes, distance):
    devices = range(lax.axis_size(axes))
    route = [(i - distance, i) for i in devices if i - distance in devices]
    return lax.ppermute(block, axes, route)


def spread(value, axis):
    count = lax.axis_size(axis)
    return lax.all_to_all(jnp.broadcast_to(value[None], (count,) + value.shape), axis, 0, 0)


def local(right_side, start_guess, block_diag, face_lift, face_scale, neighbors, ghost_send, axes):
    send = ghost_send.reshape(2 * GHOST)
    near = neighbors.reshape(ELEMS * FACES)
    scale = face_scale.reshape(ELEMS * FACES)
    sent = [tiles(GHOST), tiles(GHOST)]
    guess, to_prev, to_next = call(pack_kernel, [tiles(ELEMS)] + sent, [], [SMEM, VMEM])(send, start_guess)

    def exchange(to_prev, to_next):
        return shifted(to_next, axes, 1), shifted(to_prev, axes, -1)

    from_prev, from_next = exchange(to_prev, to_next)
    matrices = block_diag.reshape(ELEMS * NODES, NODES)
    matrices = jnp.concatenate([matrices, matrices], 1)
    lift = jnp.concatenate(
        [jnp.pad(face_lift, ((0, 0), (0, 0), (0, 64))), jnp.pad(face_lift, ((0, 0), (0, 0), (64, 0)))], 1
    ).reshape(FACES * 128, 128)
    block_parts, lift_parts, right = call(
        prep_kernel,
        [
            jax.ShapeDtypeStruct((ELEMS * NODES, 256), BF16),
            jax.ShapeDtypeStruct((FACES * 128, 384), BF16),
            tiles(ELEMS),
        ],
        [],
        [VMEM] * 3,
    )(matrices, lift, right_side)
    own_scratch = [pltpu.VMEM((FACES, ELEMS + 1, 8, 128), F32)]
    ghost_scratch = [pltpu.VMEM((FACES, 2 * GHOST + 1, 8, 128), F32)]
    own = call(first_own_kernel, [tiles(ELEMS)], own_scratch, [SMEM] * 2 + [VMEM] * 3)(
        near, scale, guess, block_parts, lift_parts
    )[0]
    first, to_prev, to_next = call(
        first_ghost_kernel, [tiles(ELEMS)] + sent, ghost_scratch, [SMEM] * 3 + [VMEM] * 6
    )(near, scale, send, own, from_prev, from_next, lift_parts, right, guess)
    vector = first
    grams, stacks = [], []
    for index in range(STEPS):
        from_prev, from_next = exchange(to_prev, to_next)
        rows = 16 * (index + 1)
        stack_shape = jax.ShapeDtypeStruct((rows, ELEMS * NODES), BF16)
        own, gram, *stacks = call(
            functools.partial(own_kernel, index),
            [tiles(ELEMS), jax.ShapeDtypeStruct((16, rows), F32), stack_shape, stack_shape],
            own_scratch,
            [SMEM] * 2 + [VMEM] * (3 + len(stacks)),
        )(near, scale, vector, block_parts, lift_parts, *stacks)
        grams.append(gram)
        if index < STEPS - 1:
            vector, to_prev, to_next = call(
                ghost_kernel, [tiles(ELEMS)] + sent, ghost_scratch, [SMEM] * 3 + [VMEM] * 4
            )(near, scale, send, own, from_prev, from_next, lift_parts)
    rows = 16 * (STEPS + 1)
    stack_shape = jax.ShapeDtypeStruct((rows, ELEMS * NODES), BF16)
    high, low, packed = call(
        last_kernel,
        [stack_shape, stack_shape, jax.ShapeDtypeStruct((32, 128), F32)],
        ghost_scratch + [pltpu.VMEM((ELEMS, 8, 128), F32), pltpu.VMEM((16, rows), F32)],
        [SMEM] * 2 + [VMEM] * 10,
    )(near, scale, own, from_prev, from_next, lift_parts, *stacks, *grams)
    packed = spread(packed, axes[2]).sum(0)
    packed = spread(packed, axes[0]).sum(0)
    packed = spread(packed, axes[1])
    result = jax.ShapeDtypeStruct((ELEMS, RHS * NODES), F32)
    return tuple(
        call(
            solve_kernel,
            [result, result],
            [pltpu.VMEM((128, 128), F32), pltpu.VMEM((2, ELEMS, 8, 128), F32)],
            [VMEM] * 5,
        )(packed, high, low, first, start_guess)
    )


def solution(mesh):
    wide, narrow = mesh.devices.shape
    inner = 16 if wide % 16 == 0 else 2
    axes = ("outer", "inner", "narrow")
    split_mesh = Mesh(mesh.devices.reshape(wide // inner, inner, narrow), axes)
    rows = P(axes, None)
    return jax.shard_map(
        functools.partial(local, axes=axes),
        mesh=split_mesh,
        in_specs=(rows, rows, rows, P(), rows, rows, rows),
        out_specs=(rows, rows),
        check_vma=False,
    )
```

profile of v0, /device:TPU:32, one launch (start us, length us, event | category | flops | bytes accessed | tf_op | source)
XLA Modules:
  0.0 122.6 jit_solution(17235267647045773667)
XLA Ops:
  0.6 0.0 copy-start.3
  0.6 0.6 copy-done.3
  1.3 0.0 copy-start
  1.3 0.9 copy-done
  2.2 0.6 shard_map.86
  2.8 1.9 %collective-permute-start = (f32[4,8,128]{2,1,0:T(8,128)S(1)}, f32[4,8,128]{2,1,0:T(8,128)S(1)}, u32[]{:S(2)}, u32[]{:S(2)}) collective-permute-start(f32[4,8,128]{2,1,0:T(8,128)S(1)} %get-tuple-element.42), channel_id=1, source_target_pairs={{0,1},{1,2},{2,3},{3,4},{4,5},{5,6},{6,7},{7,8},{8,9},{9,10},{10,1... | collective-permute-start | bytes 49160 | tf_op jit(solution)/shard_map/ppermute | solution.py:294
  4.7 5.8 %collective-permute-start.1 = (f32[4,8,128]{2,1,0:T(8,128)S(1)}, f32[4,8,128]{2,1,0:T(8,128)S(1)}, u32[]{:S(2)}, u32[]{:S(2)}) collective-permute-start(f32[4,8,128]{2,1,0:T(8,128)S(1)} %get-tuple-element.43), channel_id=1, source_target_pairs={{1,0},{2,1},{3,2},{4,3},{5,4},{6,5},{7,6},{8,7},{9,8},{10,9},{11,1... | collective-permute-start | bytes 49160 | tf_op jit(solution)/shard_map/ppermute | solution.py:294
  10.5 1.5 %reshape.25 = f32[2048,64]{1,0:T(8,128)S(1)} reshape(f32[32,4096]{1,0:T(8,128)} %param.9) | data formatting | bytes 1048576 | tf_op jit(solution)/shard_map/reshape | solution.py:313
  12.0 0.0 copy-start.4
  12.0 0.3 pad_maximum_fusion.blocks
  12.3 0.6 copy-done.4
  12.9 0.0 copy-start.5
  12.9 0.0 copy-start.2
  12.9 0.1 select_maximum_fusion
  13.0 0.6 copy-done.5
  13.6 0.1 copy.11
  13.7 0.0 copy-start.6
  13.7 0.1 reshape.22.neighbors
  13.8 0.6 copy-done.6
  14.4 0.1 copy.12
  14.5 0.1 reshape.23.scale
  14.6 0.0 copy-done.2
  14.6 0.4 shard_map.87
  14.9 1.4 %shard_map.88.own = f32[32,8,128]{2,1,0:T(8,128)S(1)} custom-call(s32[192]{0:T(256)S(1)} %reshape.22.neighbors, f32[192]{0:T(256)S(1)} %reshape.23.scale, f32[32,8,128]{2,1,0:T(8,128)S(1)} %get-tuple-element.39.vector.guess, bf16[2048,256]{1,0:T(8,128)(2,1)S(1)} %get-tuple-element.40.block_parts, bf16[768,384]{1,0:T(8,128)(2,1)S(1)} %get-tuple-element.41.lift_parts), custom_call_target="tpu_custom_call" | custom-call | tf_op jit(solution)/shard_map/pallas_call | solution.py:330
  16.3 0.0 collective-permute-done.from_prev
  16.3 0.0 collective-permute-done.1.from_next
  16.3 1.2 shard_map.89
  17.5 1.9 %collective-permute-start.2 = (f32[4,8,128]{2,1,0:T(8,128)S(1)}, f32[4,8,128]{2,1,0:T(8,128)S(1)}, u32[]{:S(2)}, u32[]{:S(2)}) collective-permute-start(f32[4,8,128]{2,1,0:T(8,128)S(1)} %get-tuple-element.47), channel_id=1, source_target_pairs={{0,1},{1,2},{2,3},{3,4},{4,5},{5,6},{6,7},{7,8},{8,9},{9,10},{10,1... | collective-permute-start | bytes 49160 | tf_op jit(solution)/shard_map/ppermute | solution.py:294
  19.5 5.8 %collective-permute-start.3 = (f32[4,8,128]{2,1,0:T(8,128)S(1)}, f32[4,8,128]{2,1,0:T(8,128)S(1)}, u32[]{:S(2)}, u32[]{:S(2)}) collective-permute-start(f32[4,8,128]{2,1,0:T(8,128)S(1)} %get-tuple-element.48), channel_id=1, source_target_pairs={{1,0},{2,1},{3,2},{4,3},{5,4},{6,5},{7,6},{8,7},{9,8},{10,9},{11,1... | collective-permute-start | bytes 49160 | tf_op jit(solution)/shard_map/ppermute | solution.py:294
  25.2 1.3 %shard_map.90 = (f32[32,8,128]{2,1,0:T(8,128)S(1)}, f32[16,16]{1,0:T(8,128)S(1)}, bf16[16,2048]{1,0:T(8,128)(2,1)S(1)}, bf16[16,2048]{1,0:T(8,128)(2,1)S(1)}) custom-call(s32[192]{0:T(256)S(1)} %reshape.22.neighbors, f32[192]{0:T(256)S(1)} %reshape.23.scale, f32[32,8,128]{2,1,0:T(8,128)S(1)} %get-tuple-element.45.vector.first, ...), custom_call_target="tpu_custom_call" | custom-call | tf_op jit(solution)/shard_map/pallas_call | solution.py:342
  26.6 0.0 collective-permute-done.2.from_prev
  26.6 0.1 collective-permute-done.3.from_next
  26.7 1.2 shard_map.91
  27.9 1.9 %collective-permute-start.4 = (f32[4,8,128]{2,1,0:T(8,128)S(1)}, f32[4,8,128]{2,1,0:T(8,128)S(1)}, u32[]{:S(2)}, u32[]{:S(2)}) collective-permute-start(f32[4,8,128]{2,1,0:T(8,128)S(1)} %get-tuple-element.53), channel_id=1, source_target_pairs={{0,1},{1,2},{2,3},{3,4},{4,5},{5,6},{6,7},{7,8},{8,9},{9,10},{10,1... | collective-permute-start | bytes 49160 | tf_op jit(solution)/shard_map/ppermute | solution.py:294
  29.8 5.8 %collective-permute-start.5 = (f32[4,8,128]{2,1,0:T(8,128)S(1)}, f32[4,8,128]{2,1,0:T(8,128)S(1)}, u32[]{:S(2)}, u32[]{:S(2)}) collective-permute-start(f32[4,8,128]{2,1,0:T(8,128)S(1)} %get-tuple-element.54), channel_id=1, source_target_pairs={{1,0},{2,1},{3,2},{4,3},{5,4},{6,5},{7,6},{8,7},{9,8},{10,9},{11,1... | collective-permute-start | bytes 49160 | tf_op jit(solution)/shard_map/ppermute | solution.py:294
  35.6 1.4 %shard_map.92 = (f32[32,8,128]{2,1,0:T(8,128)S(1)}, f32[16,32]{1,0:T(8,128)S(1)}, bf16[32,2048]{1,0:T(8,128)(2,1)S(1)}, bf16[32,2048]{1,0:T(8,128)(2,1)S(1)}) custom-call(s32[192]{0:T(256)S(1)} %reshape.22.neighbors, f32[192]{0:T(256)S(1)} %reshape.23.scale, f32[32,8,128]{2,1,0:T(8,128)S(1)} %get-tuple-element.49.vector, ...), custom_call_target="tpu_custom_call" | custom-call | tf_op jit(solution)/shard_map/pallas_call | solution.py:342
  36.9 0.0 collective-permute-done.4.from_prev
  36.9 0.0 collective-permute-done.5.from_next
  37.0 1.2 shard_map.93
  38.2 1.9 %collective-permute-start.6 = (f32[4,8,128]{2,1,0:T(8,128)S(1)}, f32[4,8,128]{2,1,0:T(8,128)S(1)}, u32[]{:S(2)}, u32[]{:S(2)}) collective-permute-start(f32[4,8,128]{2,1,0:T(8,128)S(1)} %get-tuple-element.59), channel_id=1, source_target_pairs={{0,1},{1,2},{2,3},{3,4},{4,5},{5,6},{6,7},{7,8},{8,9},{9,10},{10,1... | collective-permute-start | bytes 49160 | tf_op jit(solution)/shard_map/ppermute | solution.py:294
  40.1 5.8 %collective-permute-start.7 = (f32[4,8,128]{2,1,0:T(8,128)S(1)}, f32[4,8,128]{2,1,0:T(8,128)S(1)}, u32[]{:S(2)}, u32[]{:S(2)}) collective-permute-start(f32[4,8,128]{2,1,0:T(8,128)S(1)} %get-tuple-element.60), channel_id=1, source_target_pairs={{1,0},{2,1},{3,2},{4,3},{5,4},{6,5},{7,6},{8,7},{9,8},{10,9},{11,1... | collective-permute-start | bytes 49160 | tf_op jit(solution)/shard_map/ppermute | solution.py:294
  45.9 1.5 %shard_map.94 = (f32[32,8,128]{2,1,0:T(8,128)S(1)}, f32[16,48]{1,0:T(8,128)S(1)}, bf16[48,2048]{1,0:T(8,128)(2,1)S(1)}, bf16[48,2048]{1,0:T(8,128)(2,1)S(1)}) custom-call(s32[192]{0:T(256)S(1)} %reshape.22.neighbors, f32[192]{0:T(256)S(1)} %reshape.23.scale, f32[32,8,128]{2,1,0:T(8,128)S(1)} %get-tuple-element.55.vector, ...), custom_call_target="tpu_custom_call" | custom-call | tf_op jit(solution)/shard_map/pallas_call | solution.py:342
  47.3 0.0 collective-permute-done.6.from_prev
  47.3 0.0 collective-permute-done.7.from_next
  47.4 1.2 shard_map.95
  48.6 1.9 %collective-permute-start.8 = (f32[4,8,128]{2,1,0:T(8,128)S(1)}, f32[4,8,128]{2,1,0:T(8,128)S(1)}, u32[]{:S(2)}, u32[]{:S(2)}) collective-permute-start(f32[4,8,128]{2,1,0:T(8,128)S(1)} %get-tuple-element.65), channel_id=1, source_target_pairs={{0,1},{1,2},{2,3},{3,4},{4,5},{5,6},{6,7},{7,8},{8,9},{9,10},{10,1... | collective-permute-start | bytes 49160 | tf_op jit(solution)/shard_map/ppermute | solution.py:294
  50.5 5.8 %collective-permute-start.9 = (f32[4,8,128]{2,1,0:T(8,128)S(1)}, f32[4,8,128]{2,1,0:T(8,128)S(1)}, u32[]{:S(2)}, u32[]{:S(2)}) collective-permute-start(f32[4,8,128]{2,1,0:T(8,128)S(1)} %get-tuple-element.66), channel_id=1, source_target_pairs={{1,0},{2,1},{3,2},{4,3},{5,4},{6,5},{7,6},{8,7},{9,8},{10,9},{11,1... | collective-permute-start | bytes 49160 | tf_op jit(solution)/shard_map/ppermute | solution.py:294
  56.3 1.5 %shard_map.96 = (f32[32,8,128]{2,1,0:T(8,128)S(1)}, f32[16,64]{1,0:T(8,128)S(1)}, bf16[64,2048]{1,0:T(8,128)(2,1)S(1)}, bf16[64,2048]{1,0:T(8,128)(2,1)S(1)}) custom-call(s32[192]{0:T(256)S(1)} %reshape.22.neighbors, f32[192]{0:T(256)S(1)} %reshape.23.scale, f32[32,8,128]{2,1,0:T(8,128)S(1)} %get-tuple-element.61.vector, ...), custom_call_target="tpu_custom_call" | custom-call | tf_op jit(solution)/shard_map/pallas_call | solution.py:342
  57.8 0.0 collective-permute-done.8.from_prev
  57.8 0.0 collective-permute-done.9.from_next
  57.8 1.8 %shard_map.97 = (bf16[80,2048]{1,0:T(8,128)(2,1)S(1)}, bf16[80,2048]{1,0:T(8,128)(2,1)S(1)}, f32[32,128]{1,0:T(8,128)S(1)}) custom-call(s32[192]{0:T(256)S(1)} %reshape.22.neighbors, f32[192]{0:T(256)S(1)} %reshape.23.scale, f32[32,8,128]{2,1,0:T(8,128)S(1)} %get-tuple-element.64.own, f32[4,8,128]{2,1,0:T(8,128)S(1)} %collective-permute-done.8.from_prev, ...), custom_call_target="tpu_custom_call" | custom-call | tf_op jit(solution)/shard_map/pallas_call | solution.py:355
  59.6 11.4 %all_to_all.15 = f32[8,32,128]{2,1,0:T(8,128)S(1)} all-to-all(f32[8,32,128]{2,1,0:T(8,128)S(1)} %broadcast_in_dim.6), channel_id=1, replica_groups=mesh['outer'=4,'inner'=16,'narrow'=8] {'narrow'}, dimensions={0} | all-to-all | bytes 262144 | tf_op jit(solution)/shard_map/all_to_all | solution.py:299
  71.0 9.9 %all_to_all.16 = f32[4,32,128]{2,1,0:T(8,128)S(1)} all-to-all(f32[4,32,128]{2,1,0:T(8,128)S(1)} %broadcast_in_dim.7), channel_id=1, replica_groups=mesh['outer'=4,'inner'=16,'narrow'=8] {'outer'}, dimensions={0} | all-to-all | bytes 131072 | tf_op jit(solution)/shard_map/all_to_all | solution.py:299
  81.0 0.0 copy-start.1
  81.0 37.4 %all_to_all.17.packed = f32[16,32,128]{2,1,0:T(8,128)S(1)} all-to-all(f32[16,32,128]{2,1,0:T(8,128)S(1)} %broadcast_in_dim.8), channel_id=1, replica_groups=mesh['outer'=4,'inner'=16,'narrow'=8] {'inner'}, dimensions={0} | all-to-all | bytes 524288 | tf_op jit(solution)/shard_map/all_to_all | solution.py:299
  118.4 0.0 copy-done.1
  118.4 4.3 %shard_map.98 = (f32[32,1024]{1,0:T(8,128)}, f32[32,1024]{1,0:T(8,128)}) custom-call(f32[16,32,128]{2,1,0:T(8,128)S(1)} %all_to_all.17.packed, bf16[80,2048]{1,0:T(8,128)(2,1)S(1)} %get-tuple-element.74.high, bf16[80,2048]{1,0:T(8,128)(2,1)S(1)} %get-tuple-element.75.low, f32[32,8,128]{2,1,0:T(8,128)S(1)} %get-tuple-element.45.vector.first, ...), custom_call_target="tpu_custom_call" | custom-call | tf_op jit(solution)/shard_map/pallas_call | solution.py:366
  (5 shorter events, 0.1 us)
Async XLA Ops:
  0.6 0.7 copy-start.3
  1.3 0.9 copy-start
  2.8 13.5 %collective-permute-start = (f32[4,8,128]{2,1,0:T(8,128)S(1)}, f32[4,8,128]{2,1,0:T(8,128)S(1)}, u32[]{:S(2)}, u32[]{:S(2)}) collective-permute-start(f32[4,8,128]{2,1,0:T(8,128)S(1)} %get-tuple-element.42), channel_id=1, source_target_pairs={{0,1},{1,2},{2,3},{3,4},{4,5},{5,6},{6,7},{7,8},{8,9},{9,10},{10,1... | collective-permute-start | bytes 49160 | tf_op jit(solution)/shard_map/ppermute | solution.py:294
  4.7 11.6 %collective-permute-start.1 = (f32[4,8,128]{2,1,0:T(8,128)S(1)}, f32[4,8,128]{2,1,0:T(8,128)S(1)}, u32[]{:S(2)}, u32[]{:S(2)}) collective-permute-start(f32[4,8,128]{2,1,0:T(8,128)S(1)} %get-tuple-element.43), channel_id=1, source_target_pairs={{1,0},{2,1},{3,2},{4,3},{5,4},{6,5},{7,6},{8,7},{9,8},{10,9},{11,1... | collective-permute-start | bytes 49160 | tf_op jit(solution)/shard_map/ppermute | solution.py:294
  12.0 0.9 copy-start.4
  12.9 0.7 copy-start.5
  12.9 1.7 %copy-start.2 = (f32[32,1024]{1,0:T(8,128)S(1)}, f32[32,1024]{1,0:T(8,128)}, u32[]{:S(2)}) copy-start(f32[32,1024]{1,0:T(8,128)} %right.1) | copy-start | bytes 393220
  13.7 0.7 copy-start.6
  17.5 9.0 %collective-permute-start.2 = (f32[4,8,128]{2,1,0:T(8,128)S(1)}, f32[4,8,128]{2,1,0:T(8,128)S(1)}, u32[]{:S(2)}, u32[]{:S(2)}) collective-permute-start(f32[4,8,128]{2,1,0:T(8,128)S(1)} %get-tuple-element.47), channel_id=1, source_target_pairs={{0,1},{1,2},{2,3},{3,4},{4,5},{5,6},{6,7},{7,8},{8,9},{9,10},{10,1... | collective-permute-start | bytes 49160 | tf_op jit(solution)/shard_map/ppermute | solution.py:294
  19.5 7.2 %collective-permute-start.3 = (f32[4,8,128]{2,1,0:T(8,128)S(1)}, f32[4,8,128]{2,1,0:T(8,128)S(1)}, u32[]{:S(2)}, u32[]{:S(2)}) collective-permute-start(f32[4,8,128]{2,1,0:T(8,128)S(1)} %get-tuple-element.48), channel_id=1, source_target_pairs={{1,0},{2,1},{3,2},{4,3},{5,4},{6,5},{7,6},{8,7},{9,8},{10,9},{11,1... | collective-permute-start | bytes 49160 | tf_op jit(solution)/shard_map/ppermute | solution.py:294
  27.9 9.1 %collective-permute-start.4 = (f32[4,8,128]{2,1,0:T(8,128)S(1)}, f32[4,8,128]{2,1,0:T(8,128)S(1)}, u32[]{:S(2)}, u32[]{:S(2)}) collective-permute-start(f32[4,8,128]{2,1,0:T(8,128)S(1)} %get-tuple-element.53), channel_id=1, source_target_pairs={{0,1},{1,2},{2,3},{3,4},{4,5},{5,6},{6,7},{7,8},{8,9},{9,10},{10,1... | collective-permute-start | bytes 49160 | tf_op jit(solution)/shard_map/ppermute | solution.py:294
  29.8 7.2 %collective-permute-start.5 = (f32[4,8,128]{2,1,0:T(8,128)S(1)}, f32[4,8,128]{2,1,0:T(8,128)S(1)}, u32[]{:S(2)}, u32[]{:S(2)}) collective-permute-start(f32[4,8,128]{2,1,0:T(8,128)S(1)} %get-tuple-element.54), channel_id=1, source_target_pairs={{1,0},{2,1},{3,2},{4,3},{5,4},{6,5},{7,6},{8,7},{9,8},{10,9},{11,1... | collective-permute-start | bytes 49160 | tf_op jit(solution)/shard_map/ppermute | solution.py:294
  38.2 9.2 %collective-permute-start.6 = (f32[4,8,128]{2,1,0:T(8,128)S(1)}, f32[4,8,128]{2,1,0:T(8,128)S(1)}, u32[]{:S(2)}, u32[]{:S(2)}) collective-permute-start(f32[4,8,128]{2,1,0:T(8,128)S(1)} %get-tuple-element.59), channel_id=1, source_target_pairs={{0,1},{1,2},{2,3},{3,4},{4,5},{5,6},{6,7},{7,8},{8,9},{9,10},{10,1... | collective-permute-start | bytes 49160 | tf_op jit(solution)/shard_map/ppermute | solution.py:294
  40.1 7.2 %collective-permute-start.7 = (f32[4,8,128]{2,1,0:T(8,128)S(1)}, f32[4,8,128]{2,1,0:T(8,128)S(1)}, u32[]{:S(2)}, u32[]{:S(2)}) collective-permute-start(f32[4,8,128]{2,1,0:T(8,128)S(1)} %get-tuple-element.60), channel_id=1, source_target_pairs={{1,0},{2,1},{3,2},{4,3},{5,4},{6,5},{7,6},{8,7},{9,8},{10,9},{11,1... | collective-permute-start | bytes 49160 | tf_op jit(solution)/shard_map/ppermute | solution.py:294
  48.6 9.2 %collective-permute-start.8 = (f32[4,8,128]{2,1,0:T(8,128)S(1)}, f32[4,8,128]{2,1,0:T(8,128)S(1)}, u32[]{:S(2)}, u32[]{:S(2)}) collective-permute-start(f32[4,8,128]{2,1,0:T(8,128)S(1)} %get-tuple-element.65), channel_id=1, source_target_pairs={{0,1},{1,2},{2,3},{3,4},{4,5},{5,6},{6,7},{7,8},{8,9},{9,10},{10,1... | collective-permute-start | bytes 49160 | tf_op jit(solution)/shard_map/ppermute | solution.py:294
  50.5 7.3 %collective-permute-start.9 = (f32[4,8,128]{2,1,0:T(8,128)S(1)}, f32[4,8,128]{2,1,0:T(8,128)S(1)}, u32[]{:S(2)}, u32[]{:S(2)}) collective-permute-start(f32[4,8,128]{2,1,0:T(8,128)S(1)} %get-tuple-element.66), channel_id=1, source_target_pairs={{1,0},{2,1},{3,2},{4,3},{5,4},{6,5},{7,6},{8,7},{9,8},{10,9},{11,1... | collective-permute-start | bytes 49160 | tf_op jit(solution)/shard_map/ppermute | solution.py:294
  81.0 37.4 %copy-start.1 = (f32[32,1024]{1,0:T(8,128)S(1)}, f32[32,1024]{1,0:T(8,128)}, u32[]{:S(2)}) copy-start(f32[32,1024]{1,0:T(8,128)} %guess.3) | copy-start | bytes 393220
where the time goes:
time: 123 us
  blocking collectives  58.6 us (48%)
  starting transfers between devices  38.4 us (31%)
  Pallas kernels  18.9 us (15%)
  local copies, waits for them, and re-layouts  5.18 us (4%)
    all_to_all x3, blocking collectives, spread(): lax.all_to_all(jnp.broadcast_to(value[None], (count,) + value.shape), axi...  58.6 us
    ppermute x10, starting transfers between devices, shifted(): return lax.ppermute(block, axes, route)  38.4 us
    pallas_call x4, Pallas kernels, local(): call(functools.partial(own_kernel, index), [tiles(ELEMS), jax.ShapeDtypeS...  5.7 us
    pallas_call x1, Pallas kernels, local(): call(solve_kernel, [result, result], [pltpu.VMEM((128, 128), F32), pltpu....  4.27 us
    pallas_call x3, Pallas kernels, local(): call(ghost_kernel, [tiles(ELEMS)] + sent, ghost_scratch, [SMEM] * 3 + [VM...  3.6 us
    unnamed x16, local copies, waits for them, and re-layouts  3.47 us
  transfers between devices with their start and end apart: 10, of which 1 were waited for; matrix products, arithmetic and copies ran while one was open for 2% of the time, Pallas kernels for 6%

commit v1 on v0

--- a/solution.py
+++ b/solution.py
@@ -20,6 +20,7 @@
 
 VMEM = pl.BlockSpec(memory_space=pltpu.VMEM)
 SMEM = pl.BlockSpec(memory_space=pltpu.SMEM)
+HBM = pl.BlockSpec(memory_space=pltpu.HBM)
 PARAMS = pltpu.CompilerParams(vmem_limit_bytes=32 * 1024 * 1024)
 
 
@@ -50,26 +51,70 @@
         out[:, t, :] = ref[:, t * 128 : (t + 1) * 128]
 
 
-def send_rows(send, source, to_prev, to_next):
+def sides():
+    odd = lax.rem(lax.axis_index("narrow"), 2)
+    return GHOST * (1 - odd), GHOST * odd
+
+
+def send_rows(send, source, to_other, to_pair):
+    pair, other = sides()
     for k in range(GHOST):
-        to_prev[k] = source[send[k]]
-        to_next[k] = source[send[GHOST + k]]
-
-
-def pack_kernel(send, guess, tiled, to_prev, to_next):
+        to_other[k] = source[send[0, other + k]]
+        to_pair[k] = source[send[0, pair + k]]
+
+
+def pack_kernel(
+    send_in, guess_in, near_in, scale_in, tiled, to_other, to_pair, send_out, near_out, scale_out,
+    send, guess, done,
+):
+    pairs = [
+        (guess_in, guess),
+        (send_in, send),
+        (send_in, send_out),
+        (near_in, near_out),
+        (scale_in, scale_out),
+    ]
+    copies = [pltpu.make_async_copy(a, b, done.at[i]) for i, (a, b) in enumerate(pairs)]
+    for copy in copies:
+        copy.start()
+    copies[0].wait()
     to_tiles(guess, tiled)
-    send_rows(send, tiled, to_prev, to_next)
-
-
-def prep_kernel(blocks, lift, right, block_parts, lift_parts, right_tiled):
-    high, low = split(blocks[...])
-    block_parts[:, :128] = high
-    block_parts[:, 128:] = low
-    high, low = split(lift[...])
-    lift_parts[:, :128] = high
-    lift_parts[:, 128:256] = high
-    lift_parts[:, 256:] = low
+    copies[1].wait()
+    send_rows(send, tiled, to_other, to_pair)
+    for copy in copies[2:]:
+        copy.wait()
+
+
+def prep_kernel(
+    blocks_in, lift_in, right_in, block_parts, lift_parts, right_tiled,
+    blocks, lift, right, spread_blocks, done,
+):
+    pairs = [(lift_in, lift), (right_in, right), (blocks_in, blocks)]
+    copies = [pltpu.make_async_copy(a, b, done.at[i]) for i, (a, b) in enumerate(pairs)]
+    for copy in copies:
+        copy.start()
+    copies[0].wait()
+    for f in range(FACES):
+        upper = jnp.concatenate([lift[f], jnp.zeros((NODES, NODES), F32)], 1)
+        high, low = split(jnp.concatenate([upper, swap(upper)], 0))
+        rows = slice(f * 128, f * 128 + 128)
+        lift_parts[rows, :128] = high
+        lift_parts[rows, 128:256] = high
+        lift_parts[rows, 256:] = low
+    copies[1].wait()
     to_tiles(right, right_tiled)
+    copies[2].wait()
+    mask = left_half((ELEMS, 128))
+    for pair in range(NODES // 2):
+        two = blocks[:, pair * 128 : pair * 128 + 128]
+        turned = swap(two)
+        spread_blocks[:, 2 * pair, :] = jnp.where(mask, two, turned)
+        spread_blocks[:, 2 * pair + 1, :] = jnp.where(mask, turned, two)
+    for element in range(ELEMS):
+        high, low = split(spread_blocks[element])
+        rows = slice(element * NODES, (element + 1) * NODES)
+        block_parts[rows, :128] = high
+        block_parts[rows, 128:] = low
 
 
 def lifted(vector, lift_parts):
@@ -79,8 +124,7 @@
 
 def gather_faces(total, element, neighbors, scale, source, place):
     for f in range(FACES):
-        row = element * FACES + f
-        total = total + scale[row] * source[f, place(neighbors[row])]
+        total = total + scale[f, element] * source[f, place(neighbors[f, element])]
     return total
 
 
@@ -160,11 +204,14 @@
     gram[...] = gram_rows(high_out[...], low_out[...], newest, index + 1)
 
 
-def ghost_total(own, from_prev, from_next, lift_parts, neighbors, scale, ghost_lifted):
-    ghosts = jnp.concatenate([from_prev[...], from_next[...]], 0).reshape(2 * GHOST * 8, 128)
+def ghost_total(own, from_other, from_pair, lift_parts, neighbors, scale, ghost_lifted):
+    ghosts = jnp.concatenate([from_other[...], from_pair[...]], 0).reshape(2 * GHOST * 8, 128)
     product = lifted(ghosts, lift_parts)
+    pair, other = sides()
     for f in range(FACES):
-        ghost_lifted[f, : 2 * GHOST] = product[:, f * 128 : (f + 1) * 128].reshape(2 * GHOST, 8, 128)
+        both = product[:, f * 128 : (f + 1) * 128].reshape(2 * GHOST, 8, 128)
+        ghost_lifted[f, pl.ds(other, GHOST)] = both[:GHOST]
+        ghost_lifted[f, pl.ds(pair, GHOST)] = both[GHOST:]
         ghost_lifted[f, 2 * GHOST] = jnp.zeros((8, 128), F32)
     place = lambda n: jnp.where(n >= ELEMS, n - ELEMS, 2 * GHOST)
     for element in range(ELEMS):
@@ -172,28 +219,28 @@
 
 
 def first_ghost_kernel(
-    neighbors, scale, send, own, from_prev, from_next, lift_parts, right, guess,
-    out, to_prev, to_next, ghost_lifted,
+    neighbors, scale, send, own, from_other, from_pair, lift_parts, right, guess,
+    out, to_other, to_pair, ghost_lifted,
 ):
-    for element, total in ghost_total(own, from_prev, from_next, lift_parts, neighbors, scale, ghost_lifted):
+    for element, total in ghost_total(own, from_other, from_pair, lift_parts, neighbors, scale, ghost_lifted):
         out[element] = right[element] - (guess[element] + total)
-    send_rows(send, out, to_prev, to_next)
+    send_rows(send, out, to_other, to_pair)
 
 
 def ghost_kernel(
-    neighbors, scale, send, own, from_prev, from_next, lift_parts,
-    out, to_prev, to_next, ghost_lifted,
+    neighbors, scale, send, own, from_other, from_pair, lift_parts,
+    out, to_other, to_pair, ghost_lifted,
 ):
-    for element, total in ghost_total(own, from_prev, from_next, lift_parts, neighbors, scale, ghost_lifted):
+    for element, total in ghost_total(own, from_other, from_pair, lift_parts, neighbors, scale, ghost_lifted):
         out[element] = GAIN * total
-    send_rows(send, out, to_prev, to_next)
+    send_rows(send, out, to_other, to_pair)
 
 
 def last_kernel(
-    neighbors, scale, own, from_prev, from_next, lift_parts, old_high, old_low,
+    neighbors, scale, own, from_other, from_pair, lift_parts, old_high, old_low,
     gram0, gram1, gram2, gram3, high_out, low_out, packed, ghost_lifted, newest, gram4,
 ):
-    for element, total in ghost_total(own, from_prev, from_next, lift_parts, neighbors, scale, ghost_lifted):
+    for element, total in ghost_total(own, from_other, from_pair, lift_parts, neighbors, scale, ghost_lifted):
         newest[element] = GAIN * total
     new_gram(STEPS, newest, old_high, old_low, gram4, high_out, low_out)
     packed[0:16] = jnp.concatenate([gram4[...], gram1[...], gram0[...]], 1)
@@ -201,7 +248,7 @@
 
 
 def solve_spd(system):
-    size, block = 64, 4
+    size, block = 64, 8
     row_id = lax.broadcasted_iota(jnp.int32, (size, 128), 0)
     for start in range(0, size, block):
         columns = [jnp.broadcast_to(system[:, start + j : start + j + 1], (size, 128)) for j in range(block)]
@@ -277,21 +324,21 @@
         residual[:, lanes] = tiled[1, :, t, :]
 
 
-def call(kernel, outs, scratch, specs):
+def call(kernel, outs, scratch, specs, limit=32 * 1024, cost=None):
     return pl.pallas_call(
         kernel,
         out_shape=outs,
         in_specs=specs,
         out_specs=[VMEM] * len(outs),
         scratch_shapes=scratch,
-        compiler_params=PARAMS,
+        compiler_params=pltpu.CompilerParams(vmem_limit_bytes=limit * 1024),
+        cost_estimate=cost,
     )
 
 
-def shifted(block, axes, distance):
-    devices = range(lax.axis_size(axes))
-    route = [(i - distance, i) for i in devices if i - distance in devices]
-    return lax.ppermute(block, axes, route)
+def swapped(block, axes, first):
+    lower = range(first, lax.axis_size(axes) - 1, 2)
+    return lax.ppermute(block, axes, [(i, i + 1) for i in lower] + [(i + 1, i) for i in lower])
 
 
 def spread(value, axis):
@@ -300,21 +347,31 @@
 
 
 def local(right_side, start_guess, block_diag, face_lift, face_scale, neighbors, ghost_send, axes):
-    send = ghost_send.reshape(2 * GHOST)
-    near = neighbors.reshape(ELEMS * FACES)
-    scale = face_scale.reshape(ELEMS * FACES)
     sent = [tiles(GHOST), tiles(GHOST)]
-    guess, to_prev, to_next = call(pack_kernel, [tiles(ELEMS)] + sent, [], [SMEM, VMEM])(send, start_guess)
-
-    def exchange(to_prev, to_next):
-        return shifted(to_next, axes, 1), shifted(to_prev, axes, -1)
-
-    from_prev, from_next = exchange(to_prev, to_next)
-    matrices = block_diag.reshape(ELEMS * NODES, NODES)
-    matrices = jnp.concatenate([matrices, matrices], 1)
-    lift = jnp.concatenate(
-        [jnp.pad(face_lift, ((0, 0), (0, 0), (0, 64))), jnp.pad(face_lift, ((0, 0), (0, 0), (64, 0)))], 1
-    ).reshape(FACES * 128, 128)
+    guess, to_other, to_pair, send, near, scale = call(
+        pack_kernel,
+        [tiles(ELEMS)]
+        + sent
+        + [
+            jax.ShapeDtypeStruct((1, 2 * GHOST), jnp.int32),
+            jax.ShapeDtypeStruct((FACES, ELEMS), jnp.int32),
+            jax.ShapeDtypeStruct((FACES, ELEMS), F32),
+        ],
+        [
+            pltpu.SMEM((1, 2 * GHOST), jnp.int32),
+            pltpu.VMEM((ELEMS, RHS * NODES), F32),
+            pltpu.SemaphoreType.DMA((5,)),
+        ],
+        [HBM] * 4,
+        64512,
+        pl.CostEstimate(flops=0, bytes_accessed=16_000_000, transcendentals=0),
+    )(ghost_send, start_guess, neighbors.T, face_scale.T)
+
+    def exchange(to_other, to_pair):
+        from_other = swapped(to_other, axes, 1)
+        return from_other, swapped(to_pair, axes, 0)
+
+    from_other, from_pair = exchange(to_other, to_pair)
     block_parts, lift_parts, right = call(
         prep_kernel,
         [
@@ -322,21 +379,27 @@
             jax.ShapeDtypeStruct((FACES * 128, 384), BF16),
             tiles(ELEMS),
         ],
-        [],
-        [VMEM] * 3,
-    )(matrices, lift, right_side)
+        [
+            pltpu.VMEM((ELEMS, NODES * NODES), F32),
+            pltpu.VMEM((FACES, NODES, NODES), F32),
+            pltpu.VMEM((ELEMS, RHS * NODES), F32),
+            pltpu.VMEM((ELEMS, NODES, 128), F32),
+            pltpu.SemaphoreType.DMA((3,)),
+        ],
+        [HBM] * 3,
+    )(block_diag, face_lift, right_side)
     own_scratch = [pltpu.VMEM((FACES, ELEMS + 1, 8, 128), F32)]
     ghost_scratch = [pltpu.VMEM((FACES, 2 * GHOST + 1, 8, 128), F32)]
     own = call(first_own_kernel, [tiles(ELEMS)], own_scratch, [SMEM] * 2 + [VMEM] * 3)(
         near, scale, guess, block_parts, lift_parts
     )[0]
-    first, to_prev, to_next = call(
+    first, to_other, to_pair = call(
         first_ghost_kernel, [tiles(ELEMS)] + sent, ghost_scratch, [SMEM] * 3 + [VMEM] * 6
-    )(near, scale, send, own, from_prev, from_next, lift_parts, right, guess)
+    )(near, scale, send, own, from_other, from_pair, lift_parts, right, guess)
     vector = first
     grams, stacks = [], []
     for index in range(STEPS):
-        from_prev, from_next = exchange(to_prev, to_next)
+        from_other, from_pair = exchange(to_other, to_pair)
         rows = 16 * (index + 1)
         stack_shape = jax.ShapeDtypeStruct((rows, ELEMS * NODES), BF16)
         own, gram, *stacks = call(
@@ -347,9 +410,9 @@
         )(near, scale, vector, block_parts, lift_parts, *stacks)
         grams.append(gram)
         if index < STEPS - 1:
-            vector, to_prev, to_next = call(
+            vector, to_other, to_pair = call(
                 ghost_kernel, [tiles(ELEMS)] + sent, ghost_scratch, [SMEM] * 3 + [VMEM] * 4
-            )(near, scale, send, own, from_prev, from_next, lift_parts)
+            )(near, scale, send, own, from_other, from_pair, lift_parts)
     rows = 16 * (STEPS + 1)
     stack_shape = jax.ShapeDtypeStruct((rows, ELEMS * NODES), BF16)
     high, low, packed = call(
@@ -357,9 +420,8 @@
         [stack_shape, stack_shape, jax.ShapeDtypeStruct((32, 128), F32)],
         ghost_scratch + [pltpu.VMEM((ELEMS, 8, 128), F32), pltpu.VMEM((16, rows), F32)],
         [SMEM] * 2 + [VMEM] * 10,
-    )(near, scale, own, from_prev, from_next, lift_parts, *stacks, *grams)
-    packed = spread(packed, axes[2]).sum(0)
-    packed = spread(packed, axes[0]).sum(0)
+    )(near, scale, own, from_other, from_pair, lift_parts, *stacks, *grams)
+    packed = spread(packed, (axes[0], axes[2])).sum(0)
     packed = spread(packed, axes[1])
     result = jax.ShapeDtypeStruct((ELEMS, RHS * NODES), F32)
     return tuple(

time: 123 us -> 111 us (0.902)
  starting transfers between devices: 38.4 us -> 28.7 us
  Pallas kernels: 18.9 us -> 22 us
  blocking collectives: 58.6 us -> 55.7 us
  local copies, waits for them, and re-layouts: 5.18 us -> 3.35 us
    ppermute x10, starting transfers between devices: 38.4 us -> 28.7 us  [swapped(): lax.ppermute(block, axes, [(i, i + 1) for i in lower] + [(i + 1, i) for i...]
    all_to_all x3 -> x2, blocking collectives: 58.6 us -> 55.7 us  [spread(): lax.all_to_all(jnp.broadcast_to(value[None], (count,) + value.shape), axi...]
    reshape x3 -> x0, local copies, waits for them, and re-layouts: 1.66 us -> none  [the longest x1 1.45 us: local(): matrices = block_diag.reshape(ELEMS * NODES, NODES)]
    pallas_call x1, Pallas kernels: 0.37 us -> 1.67 us  [local(): call(prep_kernel, [jax.ShapeDtypeStruct((ELEMS * NODES, 256), BF16), jax....]
  transfers between devices with their start and end apart: 10 -> 10, of which waited for: 1 -> 0; matrix products, arithmetic and copies ran while one was open for 2% -> 0% of each run, Pallas kernels for 6% -> 8%
where the time goes in v1:
time: 111 us
  blocking collectives  55.7 us (50%)
  starting transfers between devices  28.7 us (26%)
  Pallas kernels  22 us (20%)
  local copies, waits for them, and re-layouts  3.35 us (3%)
    all_to_all x2, blocking collectives, spread(): lax.all_to_all(jnp.broadcast_to(value[None], (count,) + value.shape), axi...  55.7 us
    ppermute x10, starting transfers between devices, swapped(): lax.ppermute(block, axes, [(i, i + 1) for i in lower] + [(i + 1, i) for i...  28.7 us
    pallas_call x4, Pallas kernels, local(): call(functools.partial(own_kernel, index), [tiles(ELEMS), jax.ShapeDtypeS...  6.09 us
    pallas_call x3, Pallas kernels, local(): call(ghost_kernel, [tiles(ELEMS)] + sent, ghost_scratch, [SMEM] * 3 + [VM...  3.95 us
    pallas_call x1, Pallas kernels, local(): call(solve_kernel, [result, result], [pltpu.VMEM((128, 128), F32), pltpu....  3.8 us
    unnamed x16, local copies, waits for them, and re-layouts  3.25 us
  transfers between devices with their start and end apart: 10, of which 0 were waited for; matrix products, arithmetic and copies ran while one was open for 0% of the time, Pallas kernels for 8%

profile of v1, /device:TPU:32, one launch (start us, length us, event | category | flops | bytes accessed | tf_op | source)
XLA Modules:
  0.0 110.8 jit_solution(3298035315491961701)
XLA Ops:
  0.6 0.0 copy-start.6
  0.6 1.8 %shard_map.86 = (f32[32,8,128]{2,1,0:T(8,128)}, f32[4,8,128]{2,1,0:T(8,128)}, f32[4,8,128]{2,1,0:T(8,128)}, s32[1,8]{1,0:T(1,128)}, s32[6,32]{1,0:T(8,128)}, /*index=5*/f32[6,32]{1,0:T(8,128)}) custom-call(s32[1,8]{1,0:T(1,128)} %send_in.1, f32[32,1024]{1,0:T(8,128)} %guess.1, s32[6,32]{1,0:T(8,128)} %bitcast.2, f32[6,32]{1,0:T(8,128)} %bitcast.3), custom_call_target="tpu_custom_call" | custom-call | bytes 16000000 | tf_op jit(solution)/shard_map/pallas_call | solution.py:351
  2.4 3.7 %collective-permute-start = (f32[4,8,128]{2,1,0:T(8,128)}, f32[4,8,128]{2,1,0:T(8,128)S(1)}, u32[]{:S(2)}, u32[]{:S(2)}) collective-permute-start(f32[4,8,128]{2,1,0:T(8,128)} %get-tuple-element.48), channel_id=1, source_target_pairs={{1,2},{3,4},{5,6},{7,8},{9,10},{11,12},{13,14},{15,16},{17,18},{19... | collective-permute-start | bytes 49160 | tf_op jit(solution)/shard_map/ppermute | solution.py:341
  6.1 1.9 %collective-permute-start.1 = (f32[4,8,128]{2,1,0:T(8,128)}, f32[4,8,128]{2,1,0:T(8,128)S(1)}, u32[]{:S(2)}, u32[]{:S(2)}) collective-permute-start(f32[4,8,128]{2,1,0:T(8,128)} %get-tuple-element.49), channel_id=1, source_target_pairs={{0,1},{2,3},{4,5},{6,7},{8,9},{10,11},{12,13},{14,15},{16,17},{18,... | collective-permute-start | bytes 49160 | tf_op jit(solution)/shard_map/ppermute | solution.py:341
  8.0 0.0 copy-done.6
  8.0 0.0 copy-start.1
  8.0 1.0 copy-done.1
  9.1 0.0 copy-start.5
  9.1 0.9 copy-done.5
  10.0 0.0 copy-start.2
  10.0 1.7 %shard_map.87 = (bf16[2048,256]{1,0:T(8,128)(2,1)S(1)}, bf16[768,384]{1,0:T(8,128)(2,1)S(1)}, f32[32,8,128]{2,1,0:T(8,128)S(1)}) custom-call(f32[32,4096]{1,0:T(8,128)S(1)} %copy-done.1, f32[6,64,64]{2,1,0:T(8,128)S(1)} %copy-done.5, f32[32,1024]{1,0:T(8,128)S(1)} %copy-done.6), custom_call_target="tpu_custom_call" | custom-call | tf_op jit(solution)/shard_map/pallas_call | solution.py:375
  11.7 0.0 copy-start.4
  11.7 0.0 copy-start.3
  11.7 0.0 copy-done.2
  11.7 0.7 copy-done.4
  12.3 0.0 copy-done.3
  12.3 1.5 %shard_map.88.own = f32[32,8,128]{2,1,0:T(8,128)S(1)} custom-call(s32[6,32]{1,0:T(8,128)S(1)} %copy-done.3, f32[6,32]{1,0:T(8,128)S(1)} %copy-done.4, f32[32,8,128]{2,1,0:T(8,128)S(1)} %copy-done.2, bf16[2048,256]{1,0:T(8,128)(2,1)S(1)} %get-tuple-element.46.block_parts, bf16[768,384]{1,0:T(8,128)(2,1)S(1)} %get-tuple-element.47.lift_parts), custom_call_target="tpu_custom_call" | custom-call | tf_op jit(solution)/shard_map/pallas_call | solution.py:393
  13.8 0.0 collective-permute-done.from_other
  13.8 0.0 collective-permute-done.1.from_pair
  13.8 0.0 copy-start.7
  13.8 0.6 copy-done.7
  14.5 1.3 %shard_map.89 = (f32[32,8,128]{2,1,0:T(8,128)S(1)}, f32[4,8,128]{2,1,0:T(8,128)S(1)}, f32[4,8,128]{2,1,0:T(8,128)S(1)}) custom-call(s32[6,32]{1,0:T(8,128)S(1)} %copy-done.3, f32[6,32]{1,0:T(8,128)S(1)} %copy-done.4, s32[1,8]{1,0:T(1,128)S(1)} %copy-done.7, f32[32,8,128]{2,1,0:T(8,128)S(1)} %shard_map.88.own, ...), custom_call_target="tpu_custom_call" | custom-call | tf_op jit(solution)/shard_map/pallas_call | solution.py:396
  15.8 4.0 %collective-permute-start.2 = (f32[4,8,128]{2,1,0:T(8,128)S(1)}, f32[4,8,128]{2,1,0:T(8,128)S(1)}, u32[]{:S(2)}, u32[]{:S(2)}) collective-permute-start(f32[4,8,128]{2,1,0:T(8,128)S(1)} %get-tuple-element.53), channel_id=1, source_target_pairs={{1,2},{3,4},{5,6},{7,8},{9,10},{11,12},{13,14},{15,16},{17,18},{19... | collective-permute-start | bytes 49160 | tf_op jit(solution)/shard_map/ppermute | solution.py:341
  19.8 1.9 %collective-permute-start.3 = (f32[4,8,128]{2,1,0:T(8,128)S(1)}, f32[4,8,128]{2,1,0:T(8,128)S(1)}, u32[]{:S(2)}, u32[]{:S(2)}) collective-permute-start(f32[4,8,128]{2,1,0:T(8,128)S(1)} %get-tuple-element.54), channel_id=1, source_target_pairs={{0,1},{2,3},{4,5},{6,7},{8,9},{10,11},{12,13},{14,15},{16,17},{18,... | collective-permute-start | bytes 49160 | tf_op jit(solution)/shard_map/ppermute | solution.py:341
  21.7 1.4 %shard_map.90 = (f32[32,8,128]{2,1,0:T(8,128)S(1)}, f32[16,16]{1,0:T(8,128)S(1)}, bf16[16,2048]{1,0:T(8,128)(2,1)S(1)}, bf16[16,2048]{1,0:T(8,128)(2,1)S(1)}) custom-call(s32[6,32]{1,0:T(8,128)S(1)} %copy-done.3, f32[6,32]{1,0:T(8,128)S(1)} %copy-done.4, f32[32,8,128]{2,1,0:T(8,128)S(1)} %get-tuple-element.51.vector.first, ...), custom_call_target="tpu_custom_call" | custom-call | tf_op jit(solution)/shard_map/pallas_call | solution.py:405
  23.2 0.0 collective-permute-done.2.from_other
  23.2 0.0 collective-permute-done.3.from_pair
  23.2 1.3 %shard_map.91 = (f32[32,8,128]{2,1,0:T(8,128)S(1)}, f32[4,8,128]{2,1,0:T(8,128)S(1)}, f32[4,8,128]{2,1,0:T(8,128)S(1)}) custom-call(s32[6,32]{1,0:T(8,128)S(1)} %copy-done.3, f32[6,32]{1,0:T(8,128)S(1)} %copy-done.4, s32[1,8]{1,0:T(1,128)S(1)} %copy-done.7, f32[32,8,128]{2,1,0:T(8,128)S(1)} %get-tuple-element.52.own, ...), custom_call_target="tpu_custom_call" | custom-call | tf_op jit(solution)/shard_map/pallas_call | solution.py:413
  24.5 3.8 %collective-permute-start.4 = (f32[4,8,128]{2,1,0:T(8,128)S(1)}, f32[4,8,128]{2,1,0:T(8,128)S(1)}, u32[]{:S(2)}, u32[]{:S(2)}) collective-permute-start(f32[4,8,128]{2,1,0:T(8,128)S(1)} %get-tuple-element.59), channel_id=1, source_target_pairs={{1,2},{3,4},{5,6},{7,8},{9,10},{11,12},{13,14},{15,16},{17,18},{19... | collective-permute-start | bytes 49160 | tf_op jit(solution)/shard_map/ppermute | solution.py:341
  28.3 1.9 %collective-permute-start.5 = (f32[4,8,128]{2,1,0:T(8,128)S(1)}, f32[4,8,128]{2,1,0:T(8,128)S(1)}, u32[]{:S(2)}, u32[]{:S(2)}) collective-permute-start(f32[4,8,128]{2,1,0:T(8,128)S(1)} %get-tuple-element.60), channel_id=1, source_target_pairs={{0,1},{2,3},{4,5},{6,7},{8,9},{10,11},{12,13},{14,15},{16,17},{18,... | collective-permute-start | bytes 49160 | tf_op jit(solution)/shard_map/ppermute | solution.py:341
  30.2 1.5 %shard_map.92 = (f32[32,8,128]{2,1,0:T(8,128)S(1)}, f32[16,32]{1,0:T(8,128)S(1)}, bf16[32,2048]{1,0:T(8,128)(2,1)S(1)}, bf16[32,2048]{1,0:T(8,128)(2,1)S(1)}) custom-call(s32[6,32]{1,0:T(8,128)S(1)} %copy-done.3, f32[6,32]{1,0:T(8,128)S(1)} %copy-done.4, f32[32,8,128]{2,1,0:T(8,128)S(1)} %get-tuple-element.55.vector, ...), custom_call_target="tpu_custom_call" | custom-call | tf_op jit(solution)/shard_map/pallas_call | solution.py:405
  31.7 0.0 collective-permute-done.4.from_other
  31.7 0.0 collective-permute-done.5.from_pair
  31.7 1.3 %shard_map.93 = (f32[32,8,128]{2,1,0:T(8,128)S(1)}, f32[4,8,128]{2,1,0:T(8,128)S(1)}, f32[4,8,128]{2,1,0:T(8,128)S(1)}) custom-call(s32[6,32]{1,0:T(8,128)S(1)} %copy-done.3, f32[6,32]{1,0:T(8,128)S(1)} %copy-done.4, s32[1,8]{1,0:T(1,128)S(1)} %copy-done.7, f32[32,8,128]{2,1,0:T(8,128)S(1)} %get-tuple-element.58.own, ...), custom_call_target="tpu_custom_call" | custom-call | tf_op jit(solution)/shard_map/pallas_call | solution.py:413
  33.1 3.9 %collective-permute-start.6 = (f32[4,8,128]{2,1,0:T(8,128)S(1)}, f32[4,8,128]{2,1,0:T(8,128)S(1)}, u32[]{:S(2)}, u32[]{:S(2)}) collective-permute-start(f32[4,8,128]{2,1,0:T(8,128)S(1)} %get-tuple-element.65), channel_id=1, source_target_pairs={{1,2},{3,4},{5,6},{7,8},{9,10},{11,12},{13,14},{15,16},{17,18},{19... | collective-permute-start | bytes 49160 | tf_op jit(solution)/shard_map/ppermute | solution.py:341
  37.0 1.9 %collective-permute-start.7 = (f32[4,8,128]{2,1,0:T(8,128)S(1)}, f32[4,8,128]{2,1,0:T(8,128)S(1)}, u32[]{:S(2)}, u32[]{:S(2)}) collective-permute-start(f32[4,8,128]{2,1,0:T(8,128)S(1)} %get-tuple-element.66), channel_id=1, source_target_pairs={{0,1},{2,3},{4,5},{6,7},{8,9},{10,11},{12,13},{14,15},{16,17},{18,... | collective-permute-start | bytes 49160 | tf_op jit(solution)/shard_map/ppermute | solution.py:341
  38.9 1.6 %shard_map.94 = (f32[32,8,128]{2,1,0:T(8,128)S(1)}, f32[16,48]{1,0:T(8,128)S(1)}, bf16[48,2048]{1,0:T(8,128)(2,1)S(1)}, bf16[48,2048]{1,0:T(8,128)(2,1)S(1)}) custom-call(s32[6,32]{1,0:T(8,128)S(1)} %copy-done.3, f32[6,32]{1,0:T(8,128)S(1)} %copy-done.4, f32[32,8,128]{2,1,0:T(8,128)S(1)} %get-tuple-element.61.vector, ...), custom_call_target="tpu_custom_call" | custom-call | tf_op jit(solution)/shard_map/pallas_call | solution.py:405
  40.5 0.0 collective-permute-done.6.from_other
  40.5 0.0 collective-permute-done.7.from_pair
  40.5 1.3 %shard_map.95 = (f32[32,8,128]{2,1,0:T(8,128)S(1)}, f32[4,8,128]{2,1,0:T(8,128)S(1)}, f32[4,8,128]{2,1,0:T(8,128)S(1)}) custom-call(s32[6,32]{1,0:T(8,128)S(1)} %copy-done.3, f32[6,32]{1,0:T(8,128)S(1)} %copy-done.4, s32[1,8]{1,0:T(1,128)S(1)} %copy-done.7, f32[32,8,128]{2,1,0:T(8,128)S(1)} %get-tuple-element.64.own, ...), custom_call_target="tpu_custom_call" | custom-call | tf_op jit(solution)/shard_map/pallas_call | solution.py:413
  41.8 3.8 %collective-permute-start.8 = (f32[4,8,128]{2,1,0:T(8,128)S(1)}, f32[4,8,128]{2,1,0:T(8,128)S(1)}, u32[]{:S(2)}, u32[]{:S(2)}) collective-permute-start(f32[4,8,128]{2,1,0:T(8,128)S(1)} %get-tuple-element.71), channel_id=1, source_target_pairs={{1,2},{3,4},{5,6},{7,8},{9,10},{11,12},{13,14},{15,16},{17,18},{19... | collective-permute-start | bytes 49160 | tf_op jit(solution)/shard_map/ppermute | solution.py:341
  45.6 1.9 %collective-permute-start.9 = (f32[4,8,128]{2,1,0:T(8,128)S(1)}, f32[4,8,128]{2,1,0:T(8,128)S(1)}, u32[]{:S(2)}, u32[]{:S(2)}) collective-permute-start(f32[4,8,128]{2,1,0:T(8,128)S(1)} %get-tuple-element.72), channel_id=1, source_target_pairs={{0,1},{2,3},{4,5},{6,7},{8,9},{10,11},{12,13},{14,15},{16,17},{18,... | collective-permute-start | bytes 49160 | tf_op jit(solution)/shard_map/ppermute | solution.py:341
  47.5 1.6 %shard_map.96 = (f32[32,8,128]{2,1,0:T(8,128)S(1)}, f32[16,64]{1,0:T(8,128)S(1)}, bf16[64,2048]{1,0:T(8,128)(2,1)S(1)}, bf16[64,2048]{1,0:T(8,128)(2,1)S(1)}) custom-call(s32[6,32]{1,0:T(8,128)S(1)} %copy-done.3, f32[6,32]{1,0:T(8,128)S(1)} %copy-done.4, f32[32,8,128]{2,1,0:T(8,128)S(1)} %get-tuple-element.67.vector, ...), custom_call_target="tpu_custom_call" | custom-call | tf_op jit(solution)/shard_map/pallas_call | solution.py:405
  49.1 0.0 collective-permute-done.8.from_other
  49.2 0.0 collective-permute-done.9.from_pair
  49.2 1.9 %shard_map.97 = (bf16[80,2048]{1,0:T(8,128)(2,1)S(1)}, bf16[80,2048]{1,0:T(8,128)(2,1)S(1)}, f32[32,128]{1,0:T(8,128)S(1)}) custom-call(s32[6,32]{1,0:T(8,128)S(1)} %copy-done.3, f32[6,32]{1,0:T(8,128)S(1)} %copy-done.4, f32[32,8,128]{2,1,0:T(8,128)S(1)} %get-tuple-element.70.own, f32[4,8,128]{2,1,0:T(8,128)S(1)} %collective-permute-done.8.from_other, ...), custom_call_target="tpu_custom_call" | custom-call | tf_op jit(solution)/shard_map/pallas_call | solution.py:418
  51.1 0.1 broadcast_in_dim.4
  51.2 22.7 %all_to_all.10 = f32[32,32,128]{2,1,0:T(8,128)S(1)} all-to-all(f32[32,32,128]{2,1,0:T(8,128)S(1)} %broadcast_in_dim.4), channel_id=1, replica_groups=mesh['outer'=4,'inner'=16,'narrow'=8] {'outer','narrow'}, dimensions={0} | all-to-all | bytes 1048576 | tf_op jit(solution)/shard_map/all_to_all | solution.py:346
  73.9 0.0 copy-start
  73.9 33.0 %all_to_all.11.packed = f32[16,32,128]{2,1,0:T(8,128)S(1)} all-to-all(f32[16,32,128]{2,1,0:T(8,128)S(1)} %broadcast_in_dim.5), channel_id=1, replica_groups=mesh['outer'=4,'inner'=16,'narrow'=8] {'inner'}, dimensions={0} | all-to-all | bytes 524288 | tf_op jit(solution)/shard_map/all_to_all | solution.py:346
  107.0 0.0 copy-done
  107.0 3.8 %shard_map.98 = (f32[32,1024]{1,0:T(8,128)}, f32[32,1024]{1,0:T(8,128)}) custom-call(f32[16,32,128]{2,1,0:T(8,128)S(1)} %all_to_all.11.packed, bf16[80,2048]{1,0:T(8,128)(2,1)S(1)} %get-tuple-element.80.high, bf16[80,2048]{1,0:T(8,128)(2,1)S(1)} %get-tuple-element.81.low, f32[32,8,128]{2,1,0:T(8,128)S(1)} %get-tuple-element.51.vector.first, ...), custom_call_target="tpu_custom_call" | custom-call | tf_op jit(solution)/shard_map/pallas_call | solution.py:428
  (2 shorter events, 0.1 us)
Async XLA Ops:
  0.6 7.4 %copy-start.6 = (f32[32,1024]{1,0:T(8,128)S(1)}, f32[32,1024]{1,0:T(8,128)}, u32[]{:S(2)}) copy-start(f32[32,1024]{1,0:T(8,128)} %right_in.1) | copy-start | bytes 393220
  2.4 11.4 %collective-permute-start = (f32[4,8,128]{2,1,0:T(8,128)}, f32[4,8,128]{2,1,0:T(8,128)S(1)}, u32[]{:S(2)}, u32[]{:S(2)}) collective-permute-start(f32[4,8,128]{2,1,0:T(8,128)} %get-tuple-element.48), channel_id=1, source_target_pairs={{1,2},{3,4},{5,6},{7,8},{9,10},{11,12},{13,14},{15,16},{17,18},{19... | collective-permute-start | bytes 49160 | tf_op jit(solution)/shard_map/ppermute | solution.py:341
  6.1 7.8 %collective-permute-start.1 = (f32[4,8,128]{2,1,0:T(8,128)}, f32[4,8,128]{2,1,0:T(8,128)S(1)}, u32[]{:S(2)}, u32[]{:S(2)}) collective-permute-start(f32[4,8,128]{2,1,0:T(8,128)} %get-tuple-element.49), channel_id=1, source_target_pairs={{0,1},{2,3},{4,5},{6,7},{8,9},{10,11},{12,13},{14,15},{16,17},{18,... | collective-permute-start | bytes 49160 | tf_op jit(solution)/shard_map/ppermute | solution.py:341
  8.0 1.0 copy-start.1
  9.1 0.9 copy-start.5
  10.0 1.7 %copy-start.2 = (f32[32,8,128]{2,1,0:T(8,128)S(1)}, f32[32,8,128]{2,1,0:T(8,128)}, u32[]{:S(2)}) copy-start(f32[32,8,128]{2,1,0:T(8,128)} %get-tuple-element.45.vector.guess) | copy-start | bytes 393220
  11.7 0.7 copy-start.4
  11.7 0.7 copy-start.3
  13.8 0.6 copy-start.7
  15.8 7.4 %collective-permute-start.2 = (f32[4,8,128]{2,1,0:T(8,128)S(1)}, f32[4,8,128]{2,1,0:T(8,128)S(1)}, u32[]{:S(2)}, u32[]{:S(2)}) collective-permute-start(f32[4,8,128]{2,1,0:T(8,128)S(1)} %get-tuple-element.53), channel_id=1, source_target_pairs={{1,2},{3,4},{5,6},{7,8},{9,10},{11,12},{13,14},{15,16},{17,18},{19... | collective-permute-start | bytes 49160 | tf_op jit(solution)/shard_map/ppermute | solution.py:341
  19.8 3.4 %collective-permute-start.3 = (f32[4,8,128]{2,1,0:T(8,128)S(1)}, f32[4,8,128]{2,1,0:T(8,128)S(1)}, u32[]{:S(2)}, u32[]{:S(2)}) collective-permute-start(f32[4,8,128]{2,1,0:T(8,128)S(1)} %get-tuple-element.54), channel_id=1, source_target_pairs={{0,1},{2,3},{4,5},{6,7},{8,9},{10,11},{12,13},{14,15},{16,17},{18,... | collective-permute-start | bytes 49160 | tf_op jit(solution)/shard_map/ppermute | solution.py:341
  24.5 7.2 %collective-permute-start.4 = (f32[4,8,128]{2,1,0:T(8,128)S(1)}, f32[4,8,128]{2,1,0:T(8,128)S(1)}, u32[]{:S(2)}, u32[]{:S(2)}) collective-permute-start(f32[4,8,128]{2,1,0:T(8,128)S(1)} %get-tuple-element.59), channel_id=1, source_target_pairs={{1,2},{3,4},{5,6},{7,8},{9,10},{11,12},{13,14},{15,16},{17,18},{19... | collective-permute-start | bytes 49160 | tf_op jit(solution)/shard_map/ppermute | solution.py:341
  28.3 3.4 %collective-permute-start.5 = (f32[4,8,128]{2,1,0:T(8,128)S(1)}, f32[4,8,128]{2,1,0:T(8,128)S(1)}, u32[]{:S(2)}, u32[]{:S(2)}) collective-permute-start(f32[4,8,128]{2,1,0:T(8,128)S(1)} %get-tuple-element.60), channel_id=1, source_target_pairs={{0,1},{2,3},{4,5},{6,7},{8,9},{10,11},{12,13},{14,15},{16,17},{18,... | collective-permute-start | bytes 49160 | tf_op jit(solution)/shard_map/ppermute | solution.py:341
  33.1 7.4 %collective-permute-start.6 = (f32[4,8,128]{2,1,0:T(8,128)S(1)}, f32[4,8,128]{2,1,0:T(8,128)S(1)}, u32[]{:S(2)}, u32[]{:S(2)}) collective-permute-start(f32[4,8,128]{2,1,0:T(8,128)S(1)} %get-tuple-element.65), channel_id=1, source_target_pairs={{1,2},{3,4},{5,6},{7,8},{9,10},{11,12},{13,14},{15,16},{17,18},{19... | collective-permute-start | bytes 49160 | tf_op jit(solution)/shard_map/ppermute | solution.py:341
  37.0 3.5 %collective-permute-start.7 = (f32[4,8,128]{2,1,0:T(8,128)S(1)}, f32[4,8,128]{2,1,0:T(8,128)S(1)}, u32[]{:S(2)}, u32[]{:S(2)}) collective-permute-start(f32[4,8,128]{2,1,0:T(8,128)S(1)} %get-tuple-element.66), channel_id=1, source_target_pairs={{0,1},{2,3},{4,5},{6,7},{8,9},{10,11},{12,13},{14,15},{16,17},{18,... | collective-permute-start | bytes 49160 | tf_op jit(solution)/shard_map/ppermute | solution.py:341
  41.8 7.3 %collective-permute-start.8 = (f32[4,8,128]{2,1,0:T(8,128)S(1)}, f32[4,8,128]{2,1,0:T(8,128)S(1)}, u32[]{:S(2)}, u32[]{:S(2)}) collective-permute-start(f32[4,8,128]{2,1,0:T(8,128)S(1)} %get-tuple-element.71), channel_id=1, source_target_pairs={{1,2},{3,4},{5,6},{7,8},{9,10},{11,12},{13,14},{15,16},{17,18},{19... | collective-permute-start | bytes 49160 | tf_op jit(solution)/shard_map/ppermute | solution.py:341
  45.6 3.6 %collective-permute-start.9 = (f32[4,8,128]{2,1,0:T(8,128)S(1)}, f32[4,8,128]{2,1,0:T(8,128)S(1)}, u32[]{:S(2)}, u32[]{:S(2)}) collective-permute-start(f32[4,8,128]{2,1,0:T(8,128)S(1)} %get-tuple-element.72), channel_id=1, source_target_pairs={{0,1},{2,3},{4,5},{6,7},{8,9},{10,11},{12,13},{14,15},{16,17},{18,... | collective-permute-start | bytes 49160 | tf_op jit(solution)/shard_map/ppermute | solution.py:341
  73.9 33.0 %copy-start = (f32[32,1024]{1,0:T(8,128)S(1)}, f32[32,1024]{1,0:T(8,128)}, u32[]{:S(2)}) copy-start(f32[32,1024]{1,0:T(8,128)} %guess.1) | copy-start | bytes 393220

commit v2 on v1

v2 whole, which is shorter than its diff:
```python
import functools

import jax
import jax.numpy as jnp
from jax import lax
from jax.experimental import pallas as pl
from jax.experimental.pallas import tpu as pltpu
from jax.sharding import Mesh, PartitionSpec as P

STEPS = 4
GAIN = 1.5
RHS = 16
NODES = 64
FACES = 6
ELEMS = 32
GHOST = 4
F32 = jnp.float32
BF16 = jnp.bfloat16

OWN, FROM, SEND = (0, 576), (640, 784), (896, 992)

VMEM = pl.BlockSpec(memory_space=pltpu.VMEM)
HBM = pl.BlockSpec(memory_space=pltpu.HBM)


WIDTH = RHS * NODES
FIELD = jax.ShapeDtypeStruct((ELEMS, WIDTH), F32)


def dot_nt(left, right):
    return lax.dot_general(left, right, (((1,), (1,)), ((), ())), preferred_element_type=F32)


def split(value):
    high = value.astype(BF16)
    low = (value - high.astype(F32)).astype(BF16)
    return high, low


def swap(value):
    return pltpu.roll(value, 64, 1)


def left_half(shape):
    return lax.broadcasted_iota(jnp.int32, shape, len(shape) - 1) < 64


def slab(t):
    return slice(t * 128, t * 128 + 128)


def to_tiles(ref, out):
    for t in range(8):
        out[:, t, :] = ref[:, slab(t)]


def selection(near, scale, first, count):
    columns = []
    for f in range(FACES):
        place = first(lax.broadcasted_iota(jnp.int32, (count, ELEMS), 0))
        columns.append(jnp.where(place == near[f : f + 1, :], scale[f : f + 1, :], 0.0))
    chosen = jnp.concatenate(columns, 0)
    high = chosen.astype(BF16).astype(F32)
    return jnp.concatenate([high, high, chosen - high], 0).T


def pack_kernel(
    send_in, guess_in, near_in, scale_in, to_other, to_pair, choose,
    guess, near, scale, send_row, send, done,
):
    pairs = [(send_in, send), (guess_in, guess), (near_in, near), (scale_in, scale), (send_in, send_row)]
    copies = [pltpu.make_async_copy(a, b, done.at[i]) for i, (a, b) in enumerate(pairs)]
    for copy in copies:
        copy.start()
    for copy in copies:
        copy.wait()
    odd = lax.rem(lax.axis_index("narrow"), 2)
    for k in range(GHOST):
        to_other[k : k + 1, :] = guess[pl.ds(send[0, GHOST * odd + k], 1), :]
        to_pair[k : k + 1, :] = guess[pl.ds(send[0, GHOST * (1 - odd) + k], 1), :]
    choose[...] = jnp.zeros((ELEMS, 1024), BF16)
    choose[:, OWN[0] : OWN[1]] = selection(near, scale, lambda n: n, ELEMS).astype(BF16)
    ghosts = lambda m: ELEMS + lax.rem(m + GHOST * odd, 2 * GHOST)
    choose[:, FROM[0] : FROM[1]] = selection(near, scale, ghosts, 2 * GHOST).astype(BF16)
    row = send_row[...]
    row = jnp.where(odd == 1, jnp.concatenate([row[:, GHOST:], row[:, :GHOST]], 1), row)
    rows = (lax.broadcasted_iota(jnp.int32, (ELEMS, 2 * GHOST), 0) == row).astype(F32)
    rows = jnp.concatenate([rows, jnp.zeros((ELEMS, ELEMS - 2 * GHOST), F32)], 1)
    choose[:, SEND[0] : SEND[1]] = jnp.concatenate([rows, rows, rows], 0).T.astype(BF16)


def prep_kernel(blocks, lift, block_parts, lift_parts, spread_blocks):
    for f in range(FACES):
        upper = jnp.concatenate([lift[f], jnp.zeros((NODES, NODES), F32)], 1)
        high, low = split(jnp.concatenate([upper, swap(upper)], 0))
        rows = slice(f * 128, f * 128 + 128)
        lift_parts[rows, :128] = high
        lift_parts[rows, 128:256] = high
        lift_parts[rows, 256:] = low
    mask = left_half((ELEMS, 128))
    for pair in range(NODES // 2):
        two = blocks[:, pair * 128 : pair * 128 + 128]
        turned = swap(two)
        spread_blocks[:, 2 * pair, :] = jnp.where(mask, two, turned)
        spread_blocks[:, 2 * pair + 1, :] = jnp.where(mask, turned, two)
    for element in range(ELEMS):
        high, low = split(spread_blocks[element])
        rows = slice(element * NODES, (element + 1) * NODES)
        block_parts[rows, :128] = high
        block_parts[rows, 128:] = low


def face_sum(vector, lift_parts, choose, lanes):
    count = vector.shape[0]
    rows = jnp.concatenate([vector[:, slab(t)] for t in range(8)], 0)
    high, low = split(rows)
    moved = dot_nt(jnp.concatenate([high, low, high], 1), lift_parts[...])
    moved = jnp.concatenate(
        [
            jnp.concatenate([moved[t * count : (t + 1) * count, slab(f)] for t in range(8)], 1)
            for f in range(FACES)
        ],
        0,
    )
    high, low = split(moved)
    parts = jnp.concatenate([high, low, high], 0)
    return jnp.dot(choose[:, lanes[0] : lanes[1]], parts, preferred_element_type=F32)


def send_rows(vector, choose, to_other, to_pair):
    high = vector.astype(BF16)
    rest = vector - high.astype(F32)
    middle, low = split(rest)
    parts = jnp.concatenate([high, middle, low], 0)
    rows = jnp.dot(choose[:16, SEND[0] : SEND[1]], parts, preferred_element_type=F32)
    to_other[...] = rows[:GHOST]
    to_pair[...] = rows[GHOST : 2 * GHOST]


def dense(vector):
    upper, lower = [], []
    mask = left_half((8, 128))
    for pair in range(ELEMS // 2):
        first, second = vector[2 * pair], vector[2 * pair + 1]
        upper.append(jnp.where(mask, first, swap(second)))
        lower.append(jnp.where(mask, swap(first), second))
    return jnp.concatenate([jnp.concatenate(upper, 1), jnp.concatenate(lower, 1)], 0)


def own_part(vector, block_parts, lift_parts, choose, out, tiled, product):
    to_tiles(vector, tiled)
    value = tiled[...].reshape(ELEMS * 8, 128)
    mask = left_half((ELEMS * 8, 128))
    high, low = split(value)
    high, low = high.astype(F32), low.astype(F32)
    turned_high, turned_low = swap(high), swap(low)
    first = jnp.where(mask, low, turned_high).astype(BF16)
    second = jnp.where(mask, turned_low, high).astype(BF16)
    first_rest = jnp.where(mask, high, 0.0).astype(BF16)
    second_rest = jnp.where(mask, 0.0, high).astype(BF16)
    first = jnp.concatenate([first, first_rest], 1)
    second = jnp.concatenate([second, second_rest], 1)
    mask = left_half((8, 128))
    for group in range(ELEMS // 4):
        rows = slice(group * 32, (group + 1) * 32)
        both = jnp.concatenate([first[rows], second[rows]], 0)
        result = dot_nt(both, block_parts[group * 256 : (group + 1) * 256, :])
        for part in range(4):
            lanes = slab(part // 2)
            top = result[part * 8 : part * 8 + 8, lanes]
            bottom = result[32 + part * 8 : 40 + part * 8, lanes]
            if part % 2 == 0:
                product[group * 4 + part] = jnp.where(mask, top, swap(bottom))
            else:
                product[group * 4 + part] = jnp.where(mask, swap(top), bottom)
    faces = face_sum(vector[...], lift_parts, choose, OWN)
    for t in range(8):
        out[:, slab(t)] = faces[:, slab(t)] + product[:, t, :]


def gram_rows(stack_high, stack_low, newest, count):
    high, low = split(newest)
    left = jnp.concatenate([high, high, low], 1)
    right = jnp.concatenate([stack_high, stack_low, stack_high], 1)
    return dot_nt(left, right)


def first_own_kernel(choose, vector, block_parts, lift_parts, out, tiled, product):
    own_part(vector, block_parts, lift_parts, choose, out, tiled, product)


def own_kernel(index, choose, vector, block_parts, lift_parts, *rest):
    old_high, old_low = rest[:2] if index else (None, None)
    out, gram, high_out, low_out, tiled, product = rest[-6:]
    own_part(vector, block_parts, lift_parts, choose, out, tiled, product)
    new_gram(index, tiled, old_high, old_low, gram, high_out, low_out)


def new_gram(index, tiled, old_high, old_low, gram, high_out, low_out):
    newest = dense(tiled)
    high, low = split(newest)
    if index:
        high_out[: 16 * index] = old_high[...]
        low_out[: 16 * index] = old_low[...]
    high_out[16 * index :] = high
    low_out[16 * index :] = low
    gram[...] = gram_rows(high_out[...], low_out[...], newest, index + 1)


def ghost_part(from_other, from_pair, lift_parts, choose):
    ghosts = jnp.concatenate([from_other[...], from_pair[...]], 0)
    return face_sum(ghosts, lift_parts, choose, FROM)


def first_ghost_kernel(choose, own, from_other, from_pair, lift_parts, right, guess, out, to_other, to_pair):
    total = own[...] + ghost_part(from_other, from_pair, lift_parts, choose)
    vector = right[...] - (guess[...] + total)
    out[...] = vector
    send_rows(vector, choose, to_other, to_pair)


def ghost_kernel(choose, own, from_other, from_pair, lift_parts, out, to_other, to_pair):
    vector = GAIN * (own[...] + ghost_part(from_other, from_pair, lift_parts, choose))
    out[...] = vector
    send_rows(vector, choose, to_other, to_pair)


def last_kernel(
    choose, own, from_other, from_pair, lift_parts, old_high, old_low,
    gram0, gram1, gram2, gram3, high_out, low_out, packed, newest, tiled, gram4,
):
    newest[...] = GAIN * (own[...] + ghost_part(from_other, from_pair, lift_parts, choose))
    to_tiles(newest, tiled)
    new_gram(STEPS, tiled, old_high, old_low, gram4, high_out, low_out)
    packed[0:16] = jnp.concatenate([gram4[...], gram1[...], gram0[...]], 1)
    packed[16:32] = jnp.concatenate([gram3[...], gram2[...], jnp.zeros((16, 16), F32)], 1)


def solve_spd(system):
    size, block = 64, 8
    row_id = lax.broadcasted_iota(jnp.int32, (size, 128), 0)
    for start in range(0, size, block):
        columns = [jnp.broadcast_to(system[:, start + j : start + j + 1], (size, 128)) for j in range(block)]
        rows = [system[start + i : start + i + 1, :] for i in range(block)]
        pivots = [[columns[j][start + i : start + i + 1, :] for j in range(block)] for i in range(block)]
        for j in range(block):
            inverse = 1.0 / pivots[j][j]
            rows[j] = rows[j] * inverse
            for l in range(j + 1, block):
                pivots[j][l] = pivots[j][l] * inverse
            for i in range(block):
                if i != j:
                    factor = pivots[i][j]
                    rows[i] = rows[i] - factor * rows[j]
                    for l in range(j + 1, block):
                        pivots[i][l] = pivots[i][l] - factor * pivots[j][l]
        update = system
        for j in range(block):
            update = update - columns[j] * rows[j]
        for j in range(block):
            update = jnp.where(row_id == start + j, rows[j], update)
        system = update
    return system


def solve_kernel(packed, high, low, first, guess, solution, residual, gram_low, tiled):
    total = jnp.sum(packed[...], 0)
    upper, lower = total[:16], total[16:]
    lane = lax.broadcasted_iota(jnp.int32, (16, 128), 1)
    pieces = [
        (pltpu.roll(upper, 16, 1), 16),
        (pltpu.roll(upper, 48, 1), 32),
        (pltpu.roll(lower, 64, 1), 48),
        (lower, 64),
        (upper, 80),
    ]
    for a, (piece, width) in enumerate(pieces):
        gram_low[16 * a : 16 * a + 16, :] = jnp.where(lane < width, piece, 0.0)
    gram_low[80:, :] = jnp.zeros((48, 128), F32)
    lower_part = gram_low[...]
    row = lax.broadcasted_iota(jnp.int32, (128, 128), 0) // 16
    column = lax.broadcasted_iota(jnp.int32, (128, 128), 1) // 16
    gram = jnp.where(row >= column, lower_part, lower_part.T)
    weighted = gram[:64] + gram[16:80] * (1.0 / GAIN)
    lane = lax.broadcasted_iota(jnp.int32, (64, 128), 1)
    normal = weighted + pltpu.roll(weighted, 112, 1) * (1.0 / GAIN)
    system = jnp.where(lane < 64, normal, pltpu.roll(weighted, 64, 1))
    system = jnp.where(lane < 80, system, 0.0)
    coeffs = pltpu.roll(solve_spd(system), 64, 1)
    empty = jnp.zeros((16, 128), F32)
    padded = jnp.concatenate([coeffs, empty], 0)
    mixed = padded + jnp.concatenate([empty, coeffs], 0) * (1.0 / GAIN)
    lane = lax.broadcasted_iota(jnp.int32, (80, 128), 1)
    both = jnp.where(lane < 16, padded, pltpu.roll(mixed, 16, 1))
    both = jnp.where(lane < 32, both, 0.0)
    both = jnp.concatenate([both, jnp.zeros((48, 128), F32)], 0).T[:32]
    mask_high, mask_low = split(both)
    change = jnp.dot(mask_high[:, :80], high[...], preferred_element_type=F32)
    change = change + jnp.dot(mask_high[:, :80], low[...], preferred_element_type=F32)
    change = change + jnp.dot(mask_low[:, :80], high[...], preferred_element_type=F32)
    mask = left_half((8, 128))
    for pair in range(ELEMS // 2):
        lanes = slice(pair * 128, pair * 128 + 128)
        top, bottom = change[0:8, lanes], change[8:16, lanes]
        tiled[0, 2 * pair] = jnp.where(mask, top, swap(bottom))
        tiled[0, 2 * pair + 1] = jnp.where(mask, swap(top), bottom)
        top, bottom = change[16:24, lanes], change[24:32, lanes]
        tiled[1, 2 * pair] = jnp.where(mask, top, swap(bottom))
        tiled[1, 2 * pair + 1] = jnp.where(mask, swap(top), bottom)
    for t in range(8):
        lanes = slice(t * 128, t * 128 + 128)
        solution[:, lanes] = guess[:, lanes] + tiled[0, :, t, :]
        residual[:, lanes] = first[:, lanes] - tiled[1, :, t, :]


def call(kernel, outs, scratch, specs, limit=32 * 1024):
    return pl.pallas_call(
        kernel,
        out_shape=outs,
        in_specs=specs,
        out_specs=[VMEM] * len(outs),
        scratch_shapes=scratch,
        compiler_params=pltpu.CompilerParams(vmem_limit_bytes=limit * 1024),
    )


def swapped(block, axes, first):
    lower = range(first, lax.axis_size(axes) - 1, 2)
    return lax.ppermute(block, axes, [(i, i + 1) for i in lower] + [(i + 1, i) for i in lower])


def spread(value, axis):
    count = lax.axis_size(axis)
    return lax.all_to_all(jnp.broadcast_to(value[None], (count,) + value.shape), axis, 0, 0)


def local(right_side, start_guess, block_diag, face_lift, face_scale, neighbors, ghost_send, axes):
    sent = [jax.ShapeDtypeStruct((GHOST, WIDTH), F32)] * 2
    to_other, to_pair, choose = call(
        pack_kernel,
        sent + [jax.ShapeDtypeStruct((ELEMS, 1024), BF16)],
        [
            pltpu.VMEM((ELEMS, WIDTH), F32),
            pltpu.VMEM((FACES, ELEMS), jnp.int32),
            pltpu.VMEM((FACES, ELEMS), F32),
            pltpu.VMEM((1, 2 * GHOST), jnp.int32),
            pltpu.SMEM((1, 2 * GHOST), jnp.int32),
            pltpu.SemaphoreType.DMA((5,)),
        ],
        [HBM] * 4,
        60 * 1024,
    )(ghost_send, start_guess, neighbors.T, face_scale.T)

    def exchange(to_other, to_pair):
        from_other = swapped(to_other, axes, 1)
        return from_other, swapped(to_pair, axes, 0)

    from_other, from_pair = exchange(to_other, to_pair)
    block_parts, lift_parts = call(
        prep_kernel,
        [
            jax.ShapeDtypeStruct((ELEMS * NODES, 256), BF16),
            jax.ShapeDtypeStruct((FACES * 128, 384), BF16),
        ],
        [pltpu.VMEM((ELEMS, NODES, 128), F32)],
        [VMEM] * 2,
    )(block_diag, face_lift)
    tile_scratch = pltpu.VMEM((ELEMS, 8, 128), F32)
    own = call(first_own_kernel, [FIELD], [tile_scratch] * 2, [VMEM] * 4)(
        choose, start_guess, block_parts, lift_parts
    )[0]
    first, to_other, to_pair = call(first_ghost_kernel, [FIELD] + sent, [], [VMEM] * 7)(
        choose, own, from_other, from_pair, lift_parts, right_side, start_guess
    )
    vector = first
    grams, stacks = [], []
    for index in range(STEPS):
        from_other, from_pair = exchange(to_other, to_pair)
        rows = 16 * (index + 1)
        stack_shape = jax.ShapeDtypeStruct((rows, ELEMS * NODES), BF16)
        own, gram, *stacks = call(
            functools.partial(own_kernel, index),
            [FIELD, jax.ShapeDtypeStruct((16, rows), F32), stack_shape, stack_shape],
            [tile_scratch] * 2,
            [VMEM] * (4 + len(stacks)),
        )(choose, vector, block_parts, lift_parts, *stacks)
        grams.append(gram)
        if index < STEPS - 1:
            vector, to_other, to_pair = call(ghost_kernel, [FIELD] + sent, [], [VMEM] * 5)(
                choose, own, from_other, from_pair, lift_parts
            )
    rows = 16 * (STEPS + 1)
    stack_shape = jax.ShapeDtypeStruct((rows, ELEMS * NODES), BF16)
    high, low, packed = call(
        last_kernel,
        [stack_shape, stack_shape, jax.ShapeDtypeStruct((32, 128), F32)],
        [pltpu.VMEM((ELEMS, WIDTH), F32), tile_scratch, pltpu.VMEM((16, rows), F32)],
        [VMEM] * 11,
    )(choose, own, from_other, from_pair, lift_parts, *stacks, *grams)
    packed = spread(packed, (axes[0], axes[2])).sum(0)
    packed = spread(packed, axes[1])
    return tuple(
        call(
            solve_kernel,
            [FIELD, FIELD],
            [pltpu.VMEM((128, 128), F32), pltpu.VMEM((2, ELEMS, 8, 128), F32)],
            [VMEM] * 5,
        )(packed, high, low, first, start_guess)
    )


def solution(mesh):
    wide, narrow = mesh.devices.shape
    inner = 16 if wide % 16 == 0 else 2
    axes = ("outer", "inner", "narrow")
    split_mesh = Mesh(mesh.devices.reshape(wide // inner, inner, narrow), axes)
    rows = P(axes, None)
    return jax.shard_map(
        functools.partial(local, axes=axes),
        mesh=split_mesh,
        in_specs=(rows, rows, rows, P(), rows, rows, rows),
        out_specs=(rows, rows),
        check_vma=False,
    )
```

time: 111 us -> 105 us (0.946)
  Pallas kernels: 22 us -> 16.5 us
  local copies, waits for them, and re-layouts: 3.35 us -> 2.08 us
    pallas_call x11, Pallas kernels: 18.4 us -> 14.2 us  [the longest x4 4.91 us: local(): call(functools.partial(own_kernel, index), [FIELD, jax.ShapeDtypeStruct((...]
    unnamed x16 -> x10, local copies, waits for them, and re-layouts: 3.25 us -> 1.98 us
  transfers between devices with their start and end apart: 10 -> 10, of which waited for: 0 -> 2; matrix products, arithmetic and copies ran while one was open for 0% -> 0% of each run, Pallas kernels for 8% -> 7%
where the time goes in v2:
time: 105 us
  blocking collectives  55.9 us (53%)
  starting transfers between devices  29.4 us (28%)
  Pallas kernels  16.5 us (16%)
  local copies, waits for them, and re-layouts  2.08 us (2%)
    all_to_all x2, blocking collectives, spread(): lax.all_to_all(jnp.broadcast_to(value[None], (count,) + value.shape), axi...  55.9 us
    ppermute x10, starting transfers between devices, swapped(): lax.ppermute(block, axes, [(i, i + 1) for i in lower] + [(i + 1, i) for i...  29.4 us
    pallas_call x4, Pallas kernels, local(): call(functools.partial(own_kernel, index), [FIELD, jax.ShapeDtypeStruct((...  4.91 us
    pallas_call x1, Pallas kernels, local(): call(solve_kernel, [FIELD, FIELD], [pltpu.VMEM((128, 128), F32), pltpu.VM...  3.79 us
  transfers between devices with their start and end apart: 10, of which 2 were waited for; matrix products, arithmetic and copies ran while one was open for 0% of the time, Pallas kernels for 7%

profile of v2, /device:TPU:32, one launch (start us, length us, event | category | flops | bytes accessed | tf_op | source)
XLA Modules:
  0.0 104.9 jit_solution(241825549244214746)
XLA Ops:
  0.6 1.7 %shard_map.86 = (f32[4,1024]{1,0:T(4,128)}, f32[4,1024]{1,0:T(4,128)}, bf16[32,1024]{1,0:T(8,128)(2,1)}) custom-call(s32[1,8]{1,0:T(1,128)} %send_in.1, f32[32,1024]{1,0:T(8,128)} %guess.3, s32[6,32]{1,0:T(8,128)} %bitcast.2, f32[6,32]{1,0:T(8,128)} %bitcast.3), custom_call_target="tpu_custom_call" | custom-call | tf_op jit(solution)/shard_map/pallas_call | solution.py:339
  2.4 3.7 %collective-permute-start = (f32[4,1024]{1,0:T(4,128)}, f32[4,1024]{1,0:T(4,128)S(1)}, u32[]{:S(2)}, u32[]{:S(2)}) collective-permute-start(f32[4,1024]{1,0:T(4,128)} %get-tuple-element.41), channel_id=1, source_target_pairs={{1,2},{3,4},{5,6},{7,8},{9,10},{11,12},{13,14},{15,16},{17,18},{19... | collective-permute-start | bytes 49160 | tf_op jit(solution)/shard_map/ppermute | solution.py:329
  6.0 0.0 copy-start
  6.1 0.0 copy-start.1
  6.1 2.1 %collective-permute-start.1 = (f32[4,1024]{1,0:T(4,128)}, f32[4,1024]{1,0:T(4,128)S(1)}, u32[]{:S(2)}, u32[]{:S(2)}) collective-permute-start(f32[4,1024]{1,0:T(4,128)} %get-tuple-element.42), channel_id=1, source_target_pairs={{0,1},{2,3},{4,5},{6,7},{8,9},{10,11},{12,13},{14,15},{16,17},{18,... | collective-permute-start | bytes 49160 | tf_op jit(solution)/shard_map/ppermute | solution.py:329
  8.1 0.0 copy-start.2
  8.1 1.0 copy-done.2
  9.2 0.0 copy-start.3
  9.2 0.9 copy-done.3
  10.1 1.1 %shard_map.87 = (bf16[2048,256]{1,0:T(8,128)(2,1)S(1)}, bf16[768,384]{1,0:T(8,128)(2,1)S(1)}) custom-call(f32[32,4096]{1,0:T(8,128)S(1)} %copy-done.2, f32[6,64,64]{2,1,0:T(8,128)S(1)} %copy-done.3), custom_call_target="tpu_custom_call" | custom-call | tf_op jit(solution)/shard_map/pallas_call | solution.py:359
  11.2 0.0 copy-done
  11.2 0.0 copy-done.1
  11.2 0.0 copy-start.4
  11.2 1.1 %shard_map.88.own = f32[32,1024]{1,0:T(8,128)S(1)} custom-call(bf16[32,1024]{1,0:T(8,128)(2,1)S(1)} %copy-done, f32[32,1024]{1,0:T(8,128)S(1)} %copy-done.1, bf16[2048,256]{1,0:T(8,128)(2,1)S(1)} %get-tuple-element.39.block_parts, bf16[768,384]{1,0:T(8,128)(2,1)S(1)} %get-tuple-element.40.lift_parts), custom_call_target="tpu_custom_call" | custom-call | tf_op jit(solution)/shard_map/pallas_call | solution.py:369
  12.3 0.0 collective-permute-done.from_other
  12.3 0.0 collective-permute-done.1.from_pair
  12.3 0.0 copy-done.4
  12.3 0.7 shard_map.89
  13.0 4.0 %collective-permute-start.2 = (f32[4,1024]{1,0:T(4,128)S(1)}, f32[4,1024]{1,0:T(4,128)S(1)}, u32[]{:S(2)}, u32[]{:S(2)}) collective-permute-start(f32[4,1024]{1,0:T(4,128)S(1)} %get-tuple-element.45), channel_id=1, source_target_pairs={{1,2},{3,4},{5,6},{7,8},{9,10},{11,12},{13,14},{15,16},{17,18},{19... | collective-permute-start | bytes 49160 | tf_op jit(solution)/shard_map/ppermute | solution.py:329
  17.0 1.9 %collective-permute-start.3 = (f32[4,1024]{1,0:T(4,128)S(1)}, f32[4,1024]{1,0:T(4,128)S(1)}, u32[]{:S(2)}, u32[]{:S(2)}) collective-permute-start(f32[4,1024]{1,0:T(4,128)S(1)} %get-tuple-element.46), channel_id=1, source_target_pairs={{0,1},{2,3},{4,5},{6,7},{8,9},{10,11},{12,13},{14,15},{16,17},{18,... | collective-permute-start | bytes 49160 | tf_op jit(solution)/shard_map/ppermute | solution.py:329
  18.9 1.1 %shard_map.90 = (f32[32,1024]{1,0:T(8,128)S(1)}, f32[16,16]{1,0:T(8,128)S(1)}, bf16[16,2048]{1,0:T(8,128)(2,1)S(1)}, bf16[16,2048]{1,0:T(8,128)(2,1)S(1)}) custom-call(bf16[32,1024]{1,0:T(8,128)(2,1)S(1)} %copy-done, f32[32,1024]{1,0:T(8,128)S(1)} %get-tuple-element.43.vector.first, bf16[2048,256]{1,0:T(8,128)(2,1)S(1)} %get-tuple-element.39.block_parts, ...), custom_call_target="tpu_custom_call" | custom-call | tf_op jit(solution)/shard_map/pallas_call | solution.py:381
  20.1 0.1 collective-permute-done.2.from_other
  20.2 0.0 collective-permute-done.3.from_pair
  20.2 0.6 shard_map.91
  20.8 4.0 %collective-permute-start.4 = (f32[4,1024]{1,0:T(4,128)S(1)}, f32[4,1024]{1,0:T(4,128)S(1)}, u32[]{:S(2)}, u32[]{:S(2)}) collective-permute-start(f32[4,1024]{1,0:T(4,128)S(1)} %get-tuple-element.51), channel_id=1, source_target_pairs={{1,2},{3,4},{5,6},{7,8},{9,10},{11,12},{13,14},{15,16},{17,18},{19... | collective-permute-start | bytes 49160 | tf_op jit(solution)/shard_map/ppermute | solution.py:329
  24.8 1.9 %collective-permute-start.5 = (f32[4,1024]{1,0:T(4,128)S(1)}, f32[4,1024]{1,0:T(4,128)S(1)}, u32[]{:S(2)}, u32[]{:S(2)}) collective-permute-start(f32[4,1024]{1,0:T(4,128)S(1)} %get-tuple-element.52), channel_id=1, source_target_pairs={{0,1},{2,3},{4,5},{6,7},{8,9},{10,11},{12,13},{14,15},{16,17},{18,... | collective-permute-start | bytes 49160 | tf_op jit(solution)/shard_map/ppermute | solution.py:329
  26.8 1.1 %shard_map.92 = (f32[32,1024]{1,0:T(8,128)S(1)}, f32[16,32]{1,0:T(8,128)S(1)}, bf16[32,2048]{1,0:T(8,128)(2,1)S(1)}, bf16[32,2048]{1,0:T(8,128)(2,1)S(1)}) custom-call(bf16[32,1024]{1,0:T(8,128)(2,1)S(1)} %copy-done, f32[32,1024]{1,0:T(8,128)S(1)} %get-tuple-element.47.vector, bf16[2048,256]{1,0:T(8,128)(2,1)S(1)} %get-tuple-element.39.block_parts, ...), custom_call_target="tpu_custom_call" | custom-call | tf_op jit(solution)/shard_map/pallas_call | solution.py:381
  27.9 0.1 collective-permute-done.4.from_other
  28.0 0.0 collective-permute-done.5.from_pair
  28.0 0.6 shard_map.93
  28.6 4.0 %collective-permute-start.6 = (f32[4,1024]{1,0:T(4,128)S(1)}, f32[4,1024]{1,0:T(4,128)S(1)}, u32[]{:S(2)}, u32[]{:S(2)}) collective-permute-start(f32[4,1024]{1,0:T(4,128)S(1)} %get-tuple-element.57), channel_id=1, source_target_pairs={{1,2},{3,4},{5,6},{7,8},{9,10},{11,12},{13,14},{15,16},{17,18},{19... | collective-permute-start | bytes 49160 | tf_op jit(solution)/shard_map/ppermute | solution.py:329
  32.7 1.9 %collective-permute-start.7 = (f32[4,1024]{1,0:T(4,128)S(1)}, f32[4,1024]{1,0:T(4,128)S(1)}, u32[]{:S(2)}, u32[]{:S(2)}) collective-permute-start(f32[4,1024]{1,0:T(4,128)S(1)} %get-tuple-element.58), channel_id=1, source_target_pairs={{0,1},{2,3},{4,5},{6,7},{8,9},{10,11},{12,13},{14,15},{16,17},{18,... | collective-permute-start | bytes 49160 | tf_op jit(solution)/shard_map/ppermute | solution.py:329
  34.6 1.3 %shard_map.94 = (f32[32,1024]{1,0:T(8,128)S(1)}, f32[16,48]{1,0:T(8,128)S(1)}, bf16[48,2048]{1,0:T(8,128)(2,1)S(1)}, bf16[48,2048]{1,0:T(8,128)(2,1)S(1)}) custom-call(bf16[32,1024]{1,0:T(8,128)(2,1)S(1)} %copy-done, f32[32,1024]{1,0:T(8,128)S(1)} %get-tuple-element.53.vector, bf16[2048,256]{1,0:T(8,128)(2,1)S(1)} %get-tuple-element.39.block_parts, ...), custom_call_target="tpu_custom_call" | custom-call | tf_op jit(solution)/shard_map/pallas_call | solution.py:381
  35.9 0.0 collective-permute-done.6.from_other
  35.9 0.0 collective-permute-done.7.from_pair
  35.9 0.7 shard_map.95
  36.6 3.9 %collective-permute-start.8 = (f32[4,1024]{1,0:T(4,128)S(1)}, f32[4,1024]{1,0:T(4,128)S(1)}, u32[]{:S(2)}, u32[]{:S(2)}) collective-permute-start(f32[4,1024]{1,0:T(4,128)S(1)} %get-tuple-element.63), channel_id=1, source_target_pairs={{1,2},{3,4},{5,6},{7,8},{9,10},{11,12},{13,14},{15,16},{17,18},{19... | collective-permute-start | bytes 49160 | tf_op jit(solution)/shard_map/ppermute | solution.py:329
  40.5 1.9 %collective-permute-start.9 = (f32[4,1024]{1,0:T(4,128)S(1)}, f32[4,1024]{1,0:T(4,128)S(1)}, u32[]{:S(2)}, u32[]{:S(2)}) collective-permute-start(f32[4,1024]{1,0:T(4,128)S(1)} %get-tuple-element.64), channel_id=1, source_target_pairs={{0,1},{2,3},{4,5},{6,7},{8,9},{10,11},{12,13},{14,15},{16,17},{18,... | collective-permute-start | bytes 49160 | tf_op jit(solution)/shard_map/ppermute | solution.py:329
  42.4 1.4 %shard_map.96 = (f32[32,1024]{1,0:T(8,128)S(1)}, f32[16,64]{1,0:T(8,128)S(1)}, bf16[64,2048]{1,0:T(8,128)(2,1)S(1)}, bf16[64,2048]{1,0:T(8,128)(2,1)S(1)}) custom-call(bf16[32,1024]{1,0:T(8,128)(2,1)S(1)} %copy-done, f32[32,1024]{1,0:T(8,128)S(1)} %get-tuple-element.59.vector, bf16[2048,256]{1,0:T(8,128)(2,1)S(1)} %get-tuple-element.39.block_parts, ...), custom_call_target="tpu_custom_call" | custom-call | tf_op jit(solution)/shard_map/pallas_call | solution.py:381
  43.8 0.0 collective-permute-done.8.from_other
  43.8 0.0 collective-permute-done.9.from_pair
  43.8 1.2 %shard_map.97 = (bf16[80,2048]{1,0:T(8,128)(2,1)S(1)}, bf16[80,2048]{1,0:T(8,128)(2,1)S(1)}, f32[32,128]{1,0:T(8,128)S(1)}) custom-call(bf16[32,1024]{1,0:T(8,128)(2,1)S(1)} %copy-done, f32[32,1024]{1,0:T(8,128)S(1)} %get-tuple-element.62.own, f32[4,1024]{1,0:T(4,128)S(1)} %collective-permute-done.8.from_other, ...), custom_call_target="tpu_custom_call" | custom-call | tf_op jit(solution)/shard_map/pallas_call | solution.py:394
  45.0 0.1 broadcast_in_dim.4
  45.1 22.0 %all_to_all.10 = f32[32,32,128]{2,1,0:T(8,128)S(1)} all-to-all(f32[32,32,128]{2,1,0:T(8,128)S(1)} %broadcast_in_dim.4), channel_id=1, replica_groups=mesh['outer'=4,'inner'=16,'narrow'=8] {'outer','narrow'}, dimensions={0} | all-to-all | bytes 1048576 | tf_op jit(solution)/shard_map/all_to_all | solution.py:334
  67.2 33.9 %all_to_all.11.packed = f32[16,32,128]{2,1,0:T(8,128)S(1)} all-to-all(f32[16,32,128]{2,1,0:T(8,128)S(1)} %broadcast_in_dim.5), channel_id=1, replica_groups=mesh['outer'=4,'inner'=16,'narrow'=8] {'inner'}, dimensions={0} | all-to-all | bytes 524288 | tf_op jit(solution)/shard_map/all_to_all | solution.py:334
  101.1 3.8 %shard_map.98 = (f32[32,1024]{1,0:T(8,128)}, f32[32,1024]{1,0:T(8,128)}) custom-call(f32[16,32,128]{2,1,0:T(8,128)S(1)} %all_to_all.11.packed, bf16[80,2048]{1,0:T(8,128)(2,1)S(1)} %get-tuple-element.72.high, bf16[80,2048]{1,0:T(8,128)(2,1)S(1)} %get-tuple-element.73.low, f32[32,1024]{1,0:T(8,128)S(1)} %get-tuple-element.43.vector.first, ...), custom_call_target="tpu_custom_call" | custom-call | tf_op jit(solution)/shard_map/pallas_call | solution.py:403
  (2 shorter events, 0.1 us)
Async XLA Ops:
  2.4 9.9 %collective-permute-start = (f32[4,1024]{1,0:T(4,128)}, f32[4,1024]{1,0:T(4,128)S(1)}, u32[]{:S(2)}, u32[]{:S(2)}) collective-permute-start(f32[4,1024]{1,0:T(4,128)} %get-tuple-element.41), channel_id=1, source_target_pairs={{1,2},{3,4},{5,6},{7,8},{9,10},{11,12},{13,14},{15,16},{17,18},{19... | collective-permute-start | bytes 49160 | tf_op jit(solution)/shard_map/ppermute | solution.py:329
  6.0 5.1 %copy-start = (bf16[32,1024]{1,0:T(8,128)(2,1)S(1)}, bf16[32,1024]{1,0:T(8,128)(2,1)}, u32[]{:S(2)}) copy-start(bf16[32,1024]{1,0:T(8,128)(2,1)} %get-tuple-element.38.choose) | copy-start | bytes 196612
  6.1 5.1 %copy-start.1 = (f32[32,1024]{1,0:T(8,128)S(1)}, f32[32,1024]{1,0:T(8,128)}, u32[]{:S(2)}) copy-start(f32[32,1024]{1,0:T(8,128)} %guess.3) | copy-start | bytes 393220
  6.1 6.3 %collective-permute-start.1 = (f32[4,1024]{1,0:T(4,128)}, f32[4,1024]{1,0:T(4,128)S(1)}, u32[]{:S(2)}, u32[]{:S(2)}) collective-permute-start(f32[4,1024]{1,0:T(4,128)} %get-tuple-element.42), channel_id=1, source_target_pairs={{0,1},{2,3},{4,5},{6,7},{8,9},{10,11},{12,13},{14,15},{16,17},{18,... | collective-permute-start | bytes 49160 | tf_op jit(solution)/shard_map/ppermute | solution.py:329
  8.1 1.0 copy-start.2
  9.2 0.9 copy-start.3
  11.2 1.2 %copy-start.4 = (f32[32,1024]{1,0:T(8,128)S(1)}, f32[32,1024]{1,0:T(8,128)}, u32[]{:S(2)}) copy-start(f32[32,1024]{1,0:T(8,128)} %right.1) | copy-start | bytes 393220
  13.0 7.2 %collective-permute-start.2 = (f32[4,1024]{1,0:T(4,128)S(1)}, f32[4,1024]{1,0:T(4,128)S(1)}, u32[]{:S(2)}, u32[]{:S(2)}) collective-permute-start(f32[4,1024]{1,0:T(4,128)S(1)} %get-tuple-element.45), channel_id=1, source_target_pairs={{1,2},{3,4},{5,6},{7,8},{9,10},{11,12},{13,14},{15,16},{17,18},{19... | collective-permute-start | bytes 49160 | tf_op jit(solution)/shard_map/ppermute | solution.py:329
  17.0 3.1 %collective-permute-start.3 = (f32[4,1024]{1,0:T(4,128)S(1)}, f32[4,1024]{1,0:T(4,128)S(1)}, u32[]{:S(2)}, u32[]{:S(2)}) collective-permute-start(f32[4,1024]{1,0:T(4,128)S(1)} %get-tuple-element.46), channel_id=1, source_target_pairs={{0,1},{2,3},{4,5},{6,7},{8,9},{10,11},{12,13},{14,15},{16,17},{18,... | collective-permute-start | bytes 49160 | tf_op jit(solution)/shard_map/ppermute | solution.py:329
  20.8 7.2 %collective-permute-start.4 = (f32[4,1024]{1,0:T(4,128)S(1)}, f32[4,1024]{1,0:T(4,128)S(1)}, u32[]{:S(2)}, u32[]{:S(2)}) collective-permute-start(f32[4,1024]{1,0:T(4,128)S(1)} %get-tuple-element.51), channel_id=1, source_target_pairs={{1,2},{3,4},{5,6},{7,8},{9,10},{11,12},{13,14},{15,16},{17,18},{19... | collective-permute-start | bytes 49160 | tf_op jit(solution)/shard_map/ppermute | solution.py:329
  24.8 3.1 %collective-permute-start.5 = (f32[4,1024]{1,0:T(4,128)S(1)}, f32[4,1024]{1,0:T(4,128)S(1)}, u32[]{:S(2)}, u32[]{:S(2)}) collective-permute-start(f32[4,1024]{1,0:T(4,128)S(1)} %get-tuple-element.52), channel_id=1, source_target_pairs={{0,1},{2,3},{4,5},{6,7},{8,9},{10,11},{12,13},{14,15},{16,17},{18,... | collective-permute-start | bytes 49160 | tf_op jit(solution)/shard_map/ppermute | solution.py:329
  28.6 7.2 %collective-permute-start.6 = (f32[4,1024]{1,0:T(4,128)S(1)}, f32[4,1024]{1,0:T(4,128)S(1)}, u32[]{:S(2)}, u32[]{:S(2)}) collective-permute-start(f32[4,1024]{1,0:T(4,128)S(1)} %get-tuple-element.57), channel_id=1, source_target_pairs={{1,2},{3,4},{5,6},{7,8},{9,10},{11,12},{13,14},{15,16},{17,18},{19... | collective-permute-start | bytes 49160 | tf_op jit(solution)/shard_map/ppermute | solution.py:329
  32.7 3.2 %collective-permute-start.7 = (f32[4,1024]{1,0:T(4,128)S(1)}, f32[4,1024]{1,0:T(4,128)S(1)}, u32[]{:S(2)}, u32[]{:S(2)}) collective-permute-start(f32[4,1024]{1,0:T(4,128)S(1)} %get-tuple-element.58), channel_id=1, source_target_pairs={{0,1},{2,3},{4,5},{6,7},{8,9},{10,11},{12,13},{14,15},{16,17},{18,... | collective-permute-start | bytes 49160 | tf_op jit(solution)/shard_map/ppermute | solution.py:329
  36.6 7.2 %collective-permute-start.8 = (f32[4,1024]{1,0:T(4,128)S(1)}, f32[4,1024]{1,0:T(4,128)S(1)}, u32[]{:S(2)}, u32[]{:S(2)}) collective-permute-start(f32[4,1024]{1,0:T(4,128)S(1)} %get-tuple-element.63), channel_id=1, source_target_pairs={{1,2},{3,4},{5,6},{7,8},{9,10},{11,12},{13,14},{15,16},{17,18},{19... | collective-permute-start | bytes 49160 | tf_op jit(solution)/shard_map/ppermute | solution.py:329
  40.5 3.3 %collective-permute-start.9 = (f32[4,1024]{1,0:T(4,128)S(1)}, f32[4,1024]{1,0:T(4,128)S(1)}, u32[]{:S(2)}, u32[]{:S(2)}) collective-permute-start(f32[4,1024]{1,0:T(4,128)S(1)} %get-tuple-element.64), channel_id=1, source_target_pairs={{0,1},{2,3},{4,5},{6,7},{8,9},{10,11},{12,13},{14,15},{16,17},{18,... | collective-permute-start | bytes 49160 | tf_op jit(solution)/shard_map/ppermute | solution.py:329

commit v3 on v2

--- a/solution.py
+++ b/solution.py
@@ -59,14 +59,17 @@
     for f in range(FACES):
         place = first(lax.broadcasted_iota(jnp.int32, (count, ELEMS), 0))
         columns.append(jnp.where(place == near[f : f + 1, :], scale[f : f + 1, :], 0.0))
-    chosen = jnp.concatenate(columns, 0)
+    return jnp.concatenate(columns, 0)
+
+
+def three_parts(chosen, axis):
     high = chosen.astype(BF16).astype(F32)
-    return jnp.concatenate([high, high, chosen - high], 0).T
+    return jnp.concatenate([high, high, chosen - high], axis)
 
 
 def pack_kernel(
     send_in, guess_in, near_in, scale_in, to_other, to_pair, choose,
-    guess, near, scale, send_row, send, done,
+    guess, near, scale, send_row, terms, send, done,
 ):
     pairs = [(send_in, send), (guess_in, guess), (near_in, near), (scale_in, scale), (send_in, send_row)]
     copies = [pltpu.make_async_copy(a, b, done.at[i]) for i, (a, b) in enumerate(pairs)]
@@ -75,13 +78,19 @@
     for copy in copies:
         copy.wait()
     odd = lax.rem(lax.axis_index("narrow"), 2)
+    choose[...] = jnp.zeros((ELEMS, 1024), BF16)
+    own = selection(near, scale, lambda n: n, ELEMS)
+    choose[:, OWN[0] : OWN[1]] = three_parts(own, 0).T.astype(BF16)
+    ghosts = selection(near, scale, lambda m: ELEMS + lax.rem(m + GHOST * odd, 2 * GHOST), 2 * GHOST)
+    choose[:, FROM[0] : FROM[1]] = three_parts(ghosts, 0).T.astype(BF16)
+    terms[...] = jnp.zeros((ELEMS, 128), F32)
+    terms[:, : FACES * 2 * GHOST] = ghosts.T
+    to_other[GHOST:, :] = jnp.zeros((GHOST, WIDTH), F32)
     for k in range(GHOST):
-        to_other[k : k + 1, :] = guess[pl.ds(send[0, GHOST * odd + k], 1), :]
+        row = send[0, GHOST * odd + k]
+        to_other[k : k + 1, :] = guess[pl.ds(row, 1), :]
+        to_other[GHOST + k : GHOST + k + 1, :128] = terms[pl.ds(row, 1), :]
         to_pair[k : k + 1, :] = guess[pl.ds(send[0, GHOST * (1 - odd) + k], 1), :]
-    choose[...] = jnp.zeros((ELEMS, 1024), BF16)
-    choose[:, OWN[0] : OWN[1]] = selection(near, scale, lambda n: n, ELEMS).astype(BF16)
-    ghosts = lambda m: ELEMS + lax.rem(m + GHOST * odd, 2 * GHOST)
-    choose[:, FROM[0] : FROM[1]] = selection(near, scale, ghosts, 2 * GHOST).astype(BF16)
     row = send_row[...]
     row = jnp.where(odd == 1, jnp.concatenate([row[:, GHOST:], row[:, :GHOST]], 1), row)
     rows = (lax.broadcasted_iota(jnp.int32, (ELEMS, 2 * GHOST), 0) == row).astype(F32)
@@ -110,7 +119,7 @@
         block_parts[rows, 128:] = low
 
 
-def face_sum(vector, lift_parts, choose, lanes):
+def face_sum(vector, lift_parts, chosen):
     count = vector.shape[0]
     rows = jnp.concatenate([vector[:, slab(t)] for t in range(8)], 0)
     high, low = split(rows)
@@ -124,17 +133,22 @@
     )
     high, low = split(moved)
     parts = jnp.concatenate([high, low, high], 0)
-    return jnp.dot(choose[:, lanes[0] : lanes[1]], parts, preferred_element_type=F32)
-
-
-def send_rows(vector, choose, to_other, to_pair):
+    return jnp.dot(chosen, parts, preferred_element_type=F32)
+
+
+def from_sides(choose, lift_parts, other=None, pair=None):
+    empty = jnp.zeros((GHOST, WIDTH), F32)
+    ghosts = jnp.concatenate([empty if other is None else other, empty if pair is None else pair], 0)
+    return face_sum(ghosts, lift_parts, choose[:, FROM[0] : FROM[1]])
+
+
+def sent_rows(vector, choose):
     high = vector.astype(BF16)
     rest = vector - high.astype(F32)
     middle, low = split(rest)
     parts = jnp.concatenate([high, middle, low], 0)
     rows = jnp.dot(choose[:16, SEND[0] : SEND[1]], parts, preferred_element_type=F32)
-    to_other[...] = rows[:GHOST]
-    to_pair[...] = rows[GHOST : 2 * GHOST]
+    return rows[:GHOST], rows[GHOST : 2 * GHOST]
 
 
 def dense(vector):
@@ -147,7 +161,7 @@
     return jnp.concatenate([jnp.concatenate(upper, 1), jnp.concatenate(lower, 1)], 0)
 
 
-def own_part(vector, block_parts, lift_parts, choose, out, tiled, product):
+def own_part(vector, block_parts, lift_parts, choose, out, tiled, product, other=None):
     to_tiles(vector, tiled)
     value = tiled[...].reshape(ELEMS * 8, 128)
     mask = left_half((ELEMS * 8, 128))
@@ -173,67 +187,100 @@
                 product[group * 4 + part] = jnp.where(mask, top, swap(bottom))
             else:
                 product[group * 4 + part] = jnp.where(mask, swap(top), bottom)
-    faces = face_sum(vector[...], lift_parts, choose, OWN)
+    faces = face_sum(vector[...], lift_parts, choose[:, OWN[0] : OWN[1]])
+    if other is not None:
+        faces = faces + from_sides(choose, lift_parts, other=other[...])
     for t in range(8):
         out[:, slab(t)] = faces[:, slab(t)] + product[:, t, :]
 
 
-def gram_rows(stack_high, stack_low, newest, count):
-    high, low = split(newest)
-    left = jnp.concatenate([high, high, low], 1)
-    right = jnp.concatenate([stack_high, stack_low, stack_high], 1)
-    return dot_nt(left, right)
+def gram_of(left_high, left_low, high, low):
+    left = jnp.concatenate([left_high, left_high, left_low], 1)
+    return dot_nt(left, jnp.concatenate([high, low, high], 1))
 
 
 def first_own_kernel(choose, vector, block_parts, lift_parts, out, tiled, product):
     own_part(vector, block_parts, lift_parts, choose, out, tiled, product)
 
 
-def own_kernel(index, choose, vector, block_parts, lift_parts, *rest):
-    old_high, old_low = rest[:2] if index else (None, None)
-    out, gram, high_out, low_out, tiled, product = rest[-6:]
-    own_part(vector, block_parts, lift_parts, choose, out, tiled, product)
-    new_gram(index, tiled, old_high, old_low, gram, high_out, low_out)
-
-
-def new_gram(index, tiled, old_high, old_low, gram, high_out, low_out):
-    newest = dense(tiled)
-    high, low = split(newest)
-    if index:
-        high_out[: 16 * index] = old_high[...]
-        low_out[: 16 * index] = old_low[...]
-    high_out[16 * index :] = high
-    low_out[16 * index :] = low
-    gram[...] = gram_rows(high_out[...], low_out[...], newest, index + 1)
-
-
-def ghost_part(from_other, from_pair, lift_parts, choose):
-    ghosts = jnp.concatenate([from_other[...], from_pair[...]], 0)
-    return face_sum(ghosts, lift_parts, choose, FROM)
-
-
-def first_ghost_kernel(choose, own, from_other, from_pair, lift_parts, right, guess, out, to_other, to_pair):
-    total = own[...] + ghost_part(from_other, from_pair, lift_parts, choose)
-    vector = right[...] - (guess[...] + total)
+def second_own_kernel(choose, vector, block_parts, lift_parts, other, out, tiled, product):
+    own_part(vector, block_parts, lift_parts, choose, out, tiled, product, other)
+
+
+def dense_own_kernel(
+    choose, vector, block_parts, lift_parts, other, out, high_out, low_out, tiled, product
+):
+    own_part(vector, block_parts, lift_parts, choose, out, tiled, product, other)
+    high_out[...], low_out[...] = split(dense(tiled))
+
+
+def first_ghost_kernel(
+    choose, own, from_other, from_pair, lift_parts, right, guess, out, to_other, to_pair, terms
+):
+    faces = from_sides(choose, lift_parts, from_other[:GHOST], from_pair[...])
+    vector = right[...] - (guess[...] + (own[...] + faces))
     out[...] = vector
-    send_rows(vector, choose, to_other, to_pair)
-
-
-def ghost_kernel(choose, own, from_other, from_pair, lift_parts, out, to_other, to_pair):
-    vector = GAIN * (own[...] + ghost_part(from_other, from_pair, lift_parts, choose))
+    to_other[...], to_pair[...] = sent_rows(vector, choose)
+    partner = three_parts(from_other[GHOST:, : FACES * 2 * GHOST], 1)
+    terms[...] = jnp.concatenate([partner, jnp.zeros((16 - GHOST, partner.shape[1]), F32)], 0).astype(BF16)
+
+
+def pair_kernel(choose, own, from_pair, lift_parts, to_other, partial, message):
+    total = own[...] + from_sides(choose, lift_parts, pair=from_pair[...])
+    partial[...] = total
+    message[:GHOST] = to_other[...]
+    message[GHOST:] = sent_rows(GAIN * total, choose)[0]
+
+
+def missing_terms(terms, lift_parts, to_other, missing):
+    rows = jnp.concatenate([to_other[...], jnp.zeros((GHOST, WIDTH), F32)], 0)
+    missing[...] = GAIN * face_sum(rows, lift_parts, terms[...])[:GHOST]
+
+
+def flight_kernel(terms, lift_parts, to_other, missing):
+    missing_terms(terms, lift_parts, to_other, missing)
+
+
+def gram_flight_kernel(
+    terms, lift_parts, to_other, first, second, third, missing, high, low, gram, tiled
+):
+    missing_terms(terms, lift_parts, to_other, missing)
+    for a, vector in enumerate((first, second, third)):
+        to_tiles(vector, tiled)
+        high[16 * a : 16 * a + 16], low[16 * a : 16 * a + 16] = split(dense(tiled))
+    gram[...] = gram_of(high[...], low[...], high[...], low[...])
+
+
+def other_kernel(choose, partial, message, missing, lift_parts, out, to_pair, next_other):
+    faces = from_sides(choose, lift_parts, other=message[:GHOST])
+    vector = GAIN * (partial[...] + faces)
     out[...] = vector
-    send_rows(vector, choose, to_other, to_pair)
+    to_pair[...] = sent_rows(vector, choose)[1]
+    next_other[...] = message[GHOST:] + missing[...]
+
+
+def second_pair_kernel(choose, own, from_pair, lift_parts, out, to_other, to_pair):
+    vector = GAIN * (own[...] + from_sides(choose, lift_parts, pair=from_pair[...]))
+    out[...] = vector
+    to_other[...], to_pair[...] = sent_rows(vector, choose)
 
 
 def last_kernel(
-    choose, own, from_other, from_pair, lift_parts, old_high, old_low,
-    gram0, gram1, gram2, gram3, high_out, low_out, packed, newest, tiled, gram4,
-):
-    newest[...] = GAIN * (own[...] + ghost_part(from_other, from_pair, lift_parts, choose))
+    choose, own, from_pair, lift_parts, high, low, high3, low3, gram, high4, low4, packed, newest, tiled,
+):
+    newest[...] = GAIN * (own[...] + from_sides(choose, lift_parts, pair=from_pair[...]))
     to_tiles(newest, tiled)
-    new_gram(STEPS, tiled, old_high, old_low, gram4, high_out, low_out)
-    packed[0:16] = jnp.concatenate([gram4[...], gram1[...], gram0[...]], 1)
-    packed[16:32] = jnp.concatenate([gram3[...], gram2[...], jnp.zeros((16, 16), F32)], 1)
+    high4[...], low4[...] = split(dense(tiled))
+    left_high = jnp.concatenate([high3[...], high4[...]], 0)
+    left_low = jnp.concatenate([low3[...], low4[...]], 0)
+    rows = gram_of(
+        left_high,
+        left_low,
+        jnp.concatenate([high[...], left_high], 0),
+        jnp.concatenate([low[...], left_low], 0),
+    )
+    packed[0:16] = jnp.concatenate([rows[16:], gram[16:32, :32], gram[:16, :16]], 1)
+    packed[16:32] = jnp.concatenate([rows[:16, :64], gram[32:, :], jnp.zeros((16, 16), F32)], 1)
 
 
 def solve_spd(system):
@@ -263,9 +310,15 @@
     return system
 
 
-def solve_kernel(packed, high, low, first, guess, solution, residual, gram_low, tiled):
-    total = jnp.sum(packed[...], 0)
-    upper, lower = total[:16], total[16:]
+def solve_kernel(
+    mine, theirs, high, low, high3, low3, high4, low4, first, guess,
+    solution, residual, gram_low, tiled,
+):
+    high = jnp.concatenate([high[...], high3[...], high4[...]], 0)
+    low = jnp.concatenate([low[...], low3[...], low4[...]], 0)
+    odd = lax.rem(lax.axis_index("narrow"), 2) == 1
+    upper = jnp.where(odd, theirs[...], mine[...])
+    lower = jnp.where(odd, mine[...], theirs[...])
     lane = lax.broadcasted_iota(jnp.int32, (16, 128), 1)
     pieces = [
         (pltpu.roll(upper, 16, 1), 16),
@@ -295,9 +348,9 @@
     both = jnp.where(lane < 32, both, 0.0)
     both = jnp.concatenate([both, jnp.zeros((48, 128), F32)], 0).T[:32]
     mask_high, mask_low = split(both)
-    change = jnp.dot(mask_high[:, :80], high[...], preferred_element_type=F32)
-    change = change + jnp.dot(mask_high[:, :80], low[...], preferred_element_type=F32)
-    change = change + jnp.dot(mask_low[:, :80], high[...], preferred_element_type=F32)
+    change = jnp.dot(mask_high[:, :80], high, preferred_element_type=F32)
+    change = change + jnp.dot(mask_high[:, :80], low, preferred_element_type=F32)
+    change = change + jnp.dot(mask_low[:, :80], high, preferred_element_type=F32)
     mask = left_half((8, 128))
     for pair in range(ELEMS // 2):
         lanes = slice(pair * 128, pair * 128 + 128)
@@ -329,33 +382,26 @@
     return lax.ppermute(block, axes, [(i, i + 1) for i in lower] + [(i + 1, i) for i in lower])
 
 
-def spread(value, axis):
-    count = lax.axis_size(axis)
-    return lax.all_to_all(jnp.broadcast_to(value[None], (count,) + value.shape), axis, 0, 0)
-
-
 def local(right_side, start_guess, block_diag, face_lift, face_scale, neighbors, ghost_send, axes):
-    sent = [jax.ShapeDtypeStruct((GHOST, WIDTH), F32)] * 2
+    sent = jax.ShapeDtypeStruct((GHOST, WIDTH), F32)
+    message = jax.ShapeDtypeStruct((2 * GHOST, WIDTH), F32)
     to_other, to_pair, choose = call(
         pack_kernel,
-        sent + [jax.ShapeDtypeStruct((ELEMS, 1024), BF16)],
+        [message, sent, jax.ShapeDtypeStruct((ELEMS, 1024), BF16)],
         [
             pltpu.VMEM((ELEMS, WIDTH), F32),
             pltpu.VMEM((FACES, ELEMS), jnp.int32),
             pltpu.VMEM((FACES, ELEMS), F32),
             pltpu.VMEM((1, 2 * GHOST), jnp.int32),
+            pltpu.VMEM((ELEMS, 128), F32),
             pltpu.SMEM((1, 2 * GHOST), jnp.int32),
             pltpu.SemaphoreType.DMA((5,)),
         ],
         [HBM] * 4,
         60 * 1024,
     )(ghost_send, start_guess, neighbors.T, face_scale.T)
-
-    def exchange(to_other, to_pair):
-        from_other = swapped(to_other, axes, 1)
-        return from_other, swapped(to_pair, axes, 0)
-
-    from_other, from_pair = exchange(to_other, to_pair)
+    from_other = swapped(to_other, axes, 1)
+    from_pair = swapped(to_pair, axes, 0)
     block_parts, lift_parts = call(
         prep_kernel,
         [
@@ -366,46 +412,72 @@
         [VMEM] * 2,
     )(block_diag, face_lift)
     tile_scratch = pltpu.VMEM((ELEMS, 8, 128), F32)
-    own = call(first_own_kernel, [FIELD], [tile_scratch] * 2, [VMEM] * 4)(
-        choose, start_guess, block_parts, lift_parts
-    )[0]
-    first, to_other, to_pair = call(first_ghost_kernel, [FIELD] + sent, [], [VMEM] * 7)(
-        choose, own, from_other, from_pair, lift_parts, right_side, start_guess
-    )
-    vector = first
-    grams, stacks = [], []
-    for index in range(STEPS):
-        from_other, from_pair = exchange(to_other, to_pair)
-        rows = 16 * (index + 1)
-        stack_shape = jax.ShapeDtypeStruct((rows, ELEMS * NODES), BF16)
-        own, gram, *stacks = call(
-            functools.partial(own_kernel, index),
-            [FIELD, jax.ShapeDtypeStruct((16, rows), F32), stack_shape, stack_shape],
-            [tile_scratch] * 2,
-            [VMEM] * (4 + len(stacks)),
-        )(choose, vector, block_parts, lift_parts, *stacks)
-        grams.append(gram)
-        if index < STEPS - 1:
-            vector, to_other, to_pair = call(ghost_kernel, [FIELD] + sent, [], [VMEM] * 5)(
-                choose, own, from_other, from_pair, lift_parts
+    own_call = lambda *args: call(
+        first_own_kernel, [FIELD], [tile_scratch] * 2, [VMEM] * 4
+    )(*args)[0]
+    own = own_call(choose, start_guess, block_parts, lift_parts)
+    basis = []
+    vector, to_other, to_pair, terms = call(
+        first_ghost_kernel,
+        [FIELD, sent, sent, jax.ShapeDtypeStruct((16, 3 * FACES * 2 * GHOST), BF16)],
+        [],
+        [VMEM] * 7,
+    )(choose, own, from_other, from_pair, lift_parts, right_side, start_guess)
+    basis.append(vector)
+    stack = lambda rows: jax.ShapeDtypeStruct((rows, ELEMS * NODES), BF16)
+    for half in range(2):
+        from_pair = swapped(to_pair, axes, 0)
+        own = own_call(choose, vector, block_parts, lift_parts)
+        partial, outgoing = call(pair_kernel, [FIELD, message], [], [VMEM] * 5)(
+            choose, own, from_pair, lift_parts, to_other
+        )
+        incoming = swapped(outgoing, axes, 1)
+        if half == 0:
+            missing = call(flight_kernel, [sent], [], [VMEM] * 3)(terms, lift_parts, to_other)[0]
+        else:
+            missing, high, low, gram = call(
+                gram_flight_kernel,
+                [sent, stack(48), stack(48), jax.ShapeDtypeStruct((48, 48), F32)],
+                [tile_scratch],
+                [VMEM] * 6,
+            )(terms, lift_parts, to_other, *basis)
+        vector, to_pair, next_other = call(other_kernel, [FIELD, sent, sent], [], [VMEM] * 5)(
+            choose, partial, incoming, missing, lift_parts
+        )
+        basis.append(vector)
+        from_pair = swapped(to_pair, axes, 0)
+        if half == 0:
+            own = call(second_own_kernel, [FIELD], [tile_scratch] * 2, [VMEM] * 5)(
+                choose, vector, block_parts, lift_parts, next_other
+            )[0]
+            vector, to_other, to_pair = call(second_pair_kernel, [FIELD, sent, sent], [], [VMEM] * 4)(
+                choose, own, from_pair, lift_parts
             )
-    rows = 16 * (STEPS + 1)
-    stack_shape = jax.ShapeDtypeStruct((rows, ELEMS * NODES), BF16)
-    high, low, packed = call(
+            basis.append(vector)
+        else:
+            own, high3, low3 = call(
+                dense_own_kernel, [FIELD, stack(16), stack(16)], [tile_scratch] * 2, [VMEM] * 5
+            )(choose, vector, block_parts, lift_parts, next_other)
+    high4, low4, packed = call(
         last_kernel,
-        [stack_shape, stack_shape, jax.ShapeDtypeStruct((32, 128), F32)],
-        [pltpu.VMEM((ELEMS, WIDTH), F32), tile_scratch, pltpu.VMEM((16, rows), F32)],
-        [VMEM] * 11,
-    )(choose, own, from_other, from_pair, lift_parts, *stacks, *grams)
-    packed = spread(packed, (axes[0], axes[2])).sum(0)
-    packed = spread(packed, axes[1])
+        [stack(16), stack(16), jax.ShapeDtypeStruct((32, 128), F32)],
+        [pltpu.VMEM((ELEMS, WIDTH), F32), tile_scratch],
+        [VMEM] * 9,
+    )(choose, own, from_pair, lift_parts, high, low, high3, low3, gram)
+    outer, inner, narrow = (lax.axis_size(axis) for axis in axes)
+    halves = jnp.broadcast_to(packed.reshape(1, 2, 16, 128), (outer * narrow // 2, 2, 16, 128))
+    halves = halves.reshape(outer * narrow, 16, 128)
+    mine = lax.all_to_all(halves, (axes[0], axes[2]), 0, 0).sum(0)
+    mine = jnp.broadcast_to(mine[None], (inner, 16, 128))
+    mine = lax.all_to_all(mine, axes[1], 0, 0).sum(0)
+    theirs = swapped(mine, axes, 0)
     return tuple(
         call(
             solve_kernel,
             [FIELD, FIELD],
             [pltpu.VMEM((128, 128), F32), pltpu.VMEM((2, ELEMS, 8, 128), F32)],
-            [VMEM] * 5,
-        )(packed, high, low, first, start_guess)
+            [VMEM] * 10,
+        )(mine, theirs, high, low, high3, low3, high4, low4, basis[0], start_guess)
     )
 
 

time: 105 us -> 101 us (0.962)
  the two profiles are of different devices: /device:TPU:32 before, /device:TPU:1 now
where the time goes in v3:
time: 101 us; the launch traced here: 100 us
  blocking collectives  46 us (46%)
  starting transfers between devices  26.4 us (26%)
  Pallas kernels  19.1 us (19%)
  waiting for transfers between devices  6.01 us (6%)
  local copies, waits for them, and re-layouts  2.04 us (2%)
    all_to_all x1, blocking collectives, local(): mine = lax.all_to_all(halves, (axes[0], axes[2]), 0, 0).sum(0)  29.3 us
    ppermute x9, starting transfers between devices, swapped(): lax.ppermute(block, axes, [(i, i + 1) for i in lower] + [(i + 1, i) for i...  26.4 us
    all_to_all x1, blocking collectives, local(): mine = lax.all_to_all(mine, axes[1], 0, 0).sum(0)  16.6 us
    ppermute x9, waiting for transfers between devices, swapped(): lax.ppermute(block, axes, [(i, i + 1) for i in lower] + [(i + 1, i) for i...  6.01 us
    pallas_call x1, Pallas kernels, local(): call(solve_kernel, [FIELD, FIELD], [pltpu.VMEM((128, 128), F32), pltpu.VM...  3.77 us
    pallas_call x3, Pallas kernels, local(): call(first_own_kernel, [FIELD], [tile_scratch] * 2, [VMEM] * 4)(*args)[0]  3.31 us
  transfers between devices with their start and end apart: 9, of which 3 were waited for; matrix products, arithmetic and copies ran while one was open for 0% of the time, Pallas kernels for 8%

profile of v3, /device:TPU:1, one launch (start us, length us, event | category | flops | bytes accessed | tf_op | source)
XLA Modules:
  0.0 100.5 jit_solution(6108005953107262914)
XLA Ops:
  0.6 1.8 %shard_map.86 = (f32[8,1024]{1,0:T(8,128)}, f32[4,1024]{1,0:T(4,128)}, bf16[32,1024]{1,0:T(8,128)(2,1)}) custom-call(s32[1,8]{1,0:T(1,128)} %send_in.1, f32[32,1024]{1,0:T(8,128)} %guess.3, s32[6,32]{1,0:T(8,128)} %bitcast.6, f32[6,32]{1,0:T(8,128)} %bitcast.7), custom_call_target="tpu_custom_call" | custom-call | tf_op jit(solution)/shard_map/pallas_call | solution.py:388
  2.4 4.5 %collective-permute-start = (f32[8,1024]{1,0:T(8,128)}, f32[8,1024]{1,0:T(8,128)S(1)}, u32[]{:S(2)}, u32[]{:S(2)}) collective-permute-start(f32[8,1024]{1,0:T(8,128)} %get-tuple-element.37), channel_id=1, source_target_pairs={{1,2},{3,4},{5,6},{7,8},{9,10},{11,12},{13,14},{15,16},{17,18},{19... | collective-permute-start | bytes 98312 | tf_op jit(solution)/shard_map/ppermute | solution.py:382
  6.9 0.0 copy-start
  6.9 0.0 copy-start.1
  6.9 5.1 %collective-permute-start.1 = (f32[4,1024]{1,0:T(4,128)}, f32[4,1024]{1,0:T(4,128)S(1)}, u32[]{:S(2)}, u32[]{:S(2)}) collective-permute-start(f32[4,1024]{1,0:T(4,128)} %get-tuple-element.38), channel_id=1, source_target_pairs={{0,1},{2,3},{4,5},{6,7},{8,9},{10,11},{12,13},{14,15},{16,17},{18,... | collective-permute-start | bytes 49160 | tf_op jit(solution)/shard_map/ppermute | solution.py:382
  12.0 0.0 copy-start.2
  12.0 1.0 %copy-done.2 = f32[32,4096]{1,0:T(8,128)S(1)} copy-done((f32[32,4096]{1,0:T(8,128)S(1)}, f32[32,4096]{1,0:T(8,128)}, u32[]{:S(2)}) %copy-start.2) | copy-done | bytes 524312
  13.1 0.0 copy-start.3
  13.1 0.9 copy-done.3
  14.0 1.1 %shard_map.87 = (bf16[2048,256]{1,0:T(8,128)(2,1)S(1)}, bf16[768,384]{1,0:T(8,128)(2,1)S(1)}) custom-call(f32[32,4096]{1,0:T(8,128)S(1)} %copy-done.2, f32[6,64,64]{2,1,0:T(8,128)S(1)} %copy-done.3), custom_call_target="tpu_custom_call" | custom-call | tf_op jit(solution)/shard_map/pallas_call | solution.py:405
  15.1 0.0 copy-done
  15.1 0.0 copy-done.1
  15.1 0.0 copy-start.4
  15.1 1.1 %shard_map.88.own = f32[32,1024]{1,0:T(8,128)S(1)} custom-call(bf16[32,1024]{1,0:T(8,128)(2,1)S(1)} %copy-done, f32[32,1024]{1,0:T(8,128)S(1)} %copy-done.1, bf16[2048,256]{1,0:T(8,128)(2,1)S(1)} %get-tuple-element.35.block_parts, bf16[768,384]{1,0:T(8,128)(2,1)S(1)} %get-tuple-element.36.lift_parts), custom_call_target="tpu_custom_call" | custom-call | tf_op jit(solution)/shard_map/pallas_call | solution.py:415
  16.2 0.0 collective-permute-done.1.from_pair
  16.2 0.0 collective-permute-done.from_other
  16.2 0.0 copy-done.4
  16.2 0.7 shard_map.89
  16.9 1.9 %collective-permute-start.2 = (f32[4,1024]{1,0:T(4,128)S(1)}, f32[4,1024]{1,0:T(4,128)S(1)}, u32[]{:S(2)}, u32[]{:S(2)}) collective-permute-start(f32[4,1024]{1,0:T(4,128)S(1)} %get-tuple-element.40), channel_id=1, source_target_pairs={{0,1},{2,3},{4,5},{6,7},{8,9},{10,11},{12,13},{14,15},{16,17},{18,... | collective-permute-start | bytes 49160 | tf_op jit(solution)/shard_map/ppermute | solution.py:382
  18.8 1.1 %shard_map.90.own = f32[32,1024]{1,0:T(8,128)S(1)} custom-call(bf16[32,1024]{1,0:T(8,128)(2,1)S(1)} %copy-done, f32[32,1024]{1,0:T(8,128)S(1)} %get-tuple-element.39.vector.first, bf16[2048,256]{1,0:T(8,128)(2,1)S(1)} %get-tuple-element.35.block_parts, bf16[768,384]{1,0:T(8,128)(2,1)S(1)} %get-tuple-element.36.lift_parts), custom_call_target="tpu_custom_call" | custom-call | tf_op jit(solution)/shard_map/pallas_call | solution.py:415
  19.9 0.0 collective-permute-done.2.from_pair
  19.9 0.7 shard_map.91
  20.6 1.9 %collective-permute-start.3 = (f32[8,1024]{1,0:T(8,128)S(1)}, f32[8,1024]{1,0:T(8,128)S(1)}, u32[]{:S(2)}, u32[]{:S(2)}) collective-permute-start(f32[8,1024]{1,0:T(8,128)S(1)} %get-tuple-element.43), channel_id=1, source_target_pairs={{1,2},{3,4},{5,6},{7,8},{9,10},{11,12},{13,14},{15,16},{17,18},{19... | collective-permute-start | bytes 98312 | tf_op jit(solution)/shard_map/ppermute | solution.py:382
  22.5 0.5 shard_map.92.missing
  23.0 2.8 %collective-permute-done.3.message = f32[8,1024]{1,0:T(8,128)S(1)} collective-permute-done((f32[8,1024]{1,0:T(8,128)S(1)}, f32[8,1024]{1,0:T(8,128)S(1)}, u32[]{:S(2)}, u32[]{:S(2)}) %collective-permute-start.3) | collective-permute-done | bytes 32800 | tf_op jit(solution)/shard_map/ppermute | solution.py:382
  25.8 0.6 shard_map.93
  26.5 1.9 %collective-permute-start.4 = (f32[4,1024]{1,0:T(4,128)S(1)}, f32[4,1024]{1,0:T(4,128)S(1)}, u32[]{:S(2)}, u32[]{:S(2)}) collective-permute-start(f32[4,1024]{1,0:T(4,128)S(1)} %get-tuple-element.47), channel_id=1, source_target_pairs={{0,1},{2,3},{4,5},{6,7},{8,9},{10,11},{12,13},{14,15},{16,17},{18,... | collective-permute-start | bytes 49160 | tf_op jit(solution)/shard_map/ppermute | solution.py:382
  28.4 1.3 %shard_map.94.own = f32[32,1024]{1,0:T(8,128)S(1)} custom-call(bf16[32,1024]{1,0:T(8,128)(2,1)S(1)} %copy-done, f32[32,1024]{1,0:T(8,128)S(1)} %get-tuple-element.45.vector.second, bf16[2048,256]{1,0:T(8,128)(2,1)S(1)} %get-tuple-element.35.block_parts, bf16[768,384]{1,0:T(8,128)(2,1)S(1)} %get-tuple-element.36.lift_parts, f32[4,1024]{1,0:T(4,128)S(1)} %get-tuple-element.46.other), custom_call_target="tpu_custom_call" | custom-call | tf_op jit(solution)/shard_map/pallas_call | solution.py:450
  29.8 0.0 collective-permute-done.4.from_pair
  29.8 0.6 shard_map.95
  30.4 2.4 %collective-permute-start.5 = (f32[4,1024]{1,0:T(4,128)S(1)}, f32[4,1024]{1,0:T(4,128)S(1)}, u32[]{:S(2)}, u32[]{:S(2)}) collective-permute-start(f32[4,1024]{1,0:T(4,128)S(1)} %get-tuple-element.49), channel_id=1, source_target_pairs={{0,1},{2,3},{4,5},{6,7},{8,9},{10,11},{12,13},{14,15},{16,17},{18,... | collective-permute-start | bytes 49160 | tf_op jit(solution)/shard_map/ppermute | solution.py:382
  32.8 1.1 %shard_map.96.own = f32[32,1024]{1,0:T(8,128)S(1)} custom-call(bf16[32,1024]{1,0:T(8,128)(2,1)S(1)} %copy-done, f32[32,1024]{1,0:T(8,128)S(1)} %get-tuple-element.48.vector.third, bf16[2048,256]{1,0:T(8,128)(2,1)S(1)} %get-tuple-element.35.block_parts, bf16[768,384]{1,0:T(8,128)(2,1)S(1)} %get-tuple-element.36.lift_parts), custom_call_target="tpu_custom_call" | custom-call | tf_op jit(solution)/shard_map/pallas_call | solution.py:415
  33.9 0.0 collective-permute-done.5.from_pair
  33.9 0.7 shard_map.97
  34.6 1.9 %collective-permute-start.6 = (f32[8,1024]{1,0:T(8,128)S(1)}, f32[8,1024]{1,0:T(8,128)S(1)}, u32[]{:S(2)}, u32[]{:S(2)}) collective-permute-start(f32[8,1024]{1,0:T(8,128)S(1)} %get-tuple-element.52), channel_id=1, source_target_pairs={{1,2},{3,4},{5,6},{7,8},{9,10},{11,12},{13,14},{15,16},{17,18},{19... | collective-permute-start | bytes 98312 | tf_op jit(solution)/shard_map/ppermute | solution.py:382
  36.5 1.0 shard_map.98
  37.5 2.3 %collective-permute-done.6.message = f32[8,1024]{1,0:T(8,128)S(1)} collective-permute-done((f32[8,1024]{1,0:T(8,128)S(1)}, f32[8,1024]{1,0:T(8,128)S(1)}, u32[]{:S(2)}, u32[]{:S(2)}) %collective-permute-start.6) | collective-permute-done | bytes 32800 | tf_op jit(solution)/shard_map/ppermute | solution.py:382
  39.8 0.6 shard_map.99
  40.5 1.9 %collective-permute-start.7 = (f32[4,1024]{1,0:T(4,128)S(1)}, f32[4,1024]{1,0:T(4,128)S(1)}, u32[]{:S(2)}, u32[]{:S(2)}) collective-permute-start(f32[4,1024]{1,0:T(4,128)S(1)} %get-tuple-element.57), channel_id=1, source_target_pairs={{0,1},{2,3},{4,5},{6,7},{8,9},{10,11},{12,13},{14,15},{16,17},{18,... | collective-permute-start | bytes 49160 | tf_op jit(solution)/shard_map/ppermute | solution.py:382
  42.4 1.3 %shard_map.100 = (f32[32,1024]{1,0:T(8,128)S(1)}, bf16[16,2048]{1,0:T(8,128)(2,1)S(1)}, bf16[16,2048]{1,0:T(8,128)(2,1)S(1)}) custom-call(bf16[32,1024]{1,0:T(8,128)(2,1)S(1)} %copy-done, f32[32,1024]{1,0:T(8,128)S(1)} %get-tuple-element.54.vector, bf16[2048,256]{1,0:T(8,128)(2,1)S(1)} %get-tuple-element.35.block_parts, ...), custom_call_target="tpu_custom_call" | custom-call | tf_op jit(solution)/shard_map/pallas_call | solution.py:458
  43.7 0.0 collective-permute-done.7.from_pair
  43.8 1.2 %shard_map.101 = (bf16[16,2048]{1,0:T(8,128)(2,1)S(1)}, bf16[16,2048]{1,0:T(8,128)(2,1)S(1)}, f32[32,128]{1,0:T(8,128)S(1)}) custom-call(bf16[32,1024]{1,0:T(8,128)(2,1)S(1)} %copy-done, f32[32,1024]{1,0:T(8,128)S(1)} %get-tuple-element.56.own, f32[4,1024]{1,0:T(4,128)S(1)} %collective-permute-done.7.from_pair, ...), custom_call_target="tpu_custom_call" | custom-call | tf_op jit(solution)/shard_map/pallas_call | solution.py:461
  45.0 29.3 %all_to_all.10 = f32[32,16,128]{2,1,0:T(8,128)S(1)} all-to-all(f32[32,16,128]{2,1,0:T(8,128)S(1)} %bitcast.5), channel_id=1, replica_groups=mesh['outer'=4,'inner'=16,'narrow'=8] {'outer','narrow'}, dimensions={0} | all-to-all | bytes 524288 | tf_op jit(solution)/shard_map/all_to_all | solution.py:470
  74.4 16.6 %all_to_all.11 = f32[16,16,128]{2,1,0:T(8,128)S(1)} all-to-all(f32[16,16,128]{2,1,0:T(8,128)S(1)} %broadcast_in_dim.15), channel_id=1, replica_groups=mesh['outer'=4,'inner'=16,'narrow'=8] {'inner'}, dimensions={0} | all-to-all | bytes 262144 | tf_op jit(solution)/shard_map/all_to_all | solution.py:472
  91.0 4.9 %collective-permute-start.8 = (f32[16,128]{1,0:T(8,128)S(1)}, f32[16,128]{1,0:T(8,128)S(1)}, u32[]{:S(2)}, u32[]{:S(2)}) collective-permute-start(f32[16,128]{1,0:T(8,128)S(1)} %reduce_sum.19.mine), channel_id=1, source_target_pairs={{0,1},{2,3},{4,5},{6,7},{8,9},{10,11},{12,13},{14,15},{16,17},{18,... | collective-permute-start | bytes 24584 | tf_op jit(solution)/shard_map/ppermute | solution.py:382
  95.9 0.8 collective-permute-done.8.theirs
  96.7 3.8 %shard_map.102 = (f32[32,1024]{1,0:T(8,128)}, f32[32,1024]{1,0:T(8,128)}) custom-call(f32[16,128]{1,0:T(8,128)S(1)} %reduce_sum.19.mine, f32[16,128]{1,0:T(8,128)S(1)} %collective-permute-done.8.theirs, bf16[48,2048]{1,0:T(8,128)(2,1)S(1)} %get-tuple-element.58.high, bf16[48,2048]{1,0:T(8,128)(2,1)S(1)} %get-tuple-element.59.low, ...), custom_call_target="tpu_custom_call" | custom-call | tf_op jit(solution)/shard_map/pallas_call | solution.py:475
  (4 shorter events, 0.1 us)
Async XLA Ops:
  2.4 13.8 %collective-permute-start = (f32[8,1024]{1,0:T(8,128)}, f32[8,1024]{1,0:T(8,128)S(1)}, u32[]{:S(2)}, u32[]{:S(2)}) collective-permute-start(f32[8,1024]{1,0:T(8,128)} %get-tuple-element.37), channel_id=1, source_target_pairs={{1,2},{3,4},{5,6},{7,8},{9,10},{11,12},{13,14},{15,16},{17,18},{19... | collective-permute-start | bytes 98312 | tf_op jit(solution)/shard_map/ppermute | solution.py:382
  6.9 8.1 %copy-start = (bf16[32,1024]{1,0:T(8,128)(2,1)S(1)}, bf16[32,1024]{1,0:T(8,128)(2,1)}, u32[]{:S(2)}) copy-start(bf16[32,1024]{1,0:T(8,128)(2,1)} %get-tuple-element.34.choose) | copy-start | bytes 196612
  6.9 8.1 %copy-start.1 = (f32[32,1024]{1,0:T(8,128)S(1)}, f32[32,1024]{1,0:T(8,128)}, u32[]{:S(2)}) copy-start(f32[32,1024]{1,0:T(8,128)} %guess.3) | copy-start | bytes 393220
  6.9 9.3 %collective-permute-start.1 = (f32[4,1024]{1,0:T(4,128)}, f32[4,1024]{1,0:T(4,128)S(1)}, u32[]{:S(2)}, u32[]{:S(2)}) collective-permute-start(f32[4,1024]{1,0:T(4,128)} %get-tuple-element.38), channel_id=1, source_target_pairs={{0,1},{2,3},{4,5},{6,7},{8,9},{10,11},{12,13},{14,15},{16,17},{18,... | collective-permute-start | bytes 49160 | tf_op jit(solution)/shard_map/ppermute | solution.py:382
  12.0 1.0 %copy-start.2 = (f32[32,4096]{1,0:T(8,128)S(1)}, f32[32,4096]{1,0:T(8,128)}, u32[]{:S(2)}) copy-start(f32[32,4096]{1,0:T(8,128)} %blocks.1) | copy-start | bytes 1572868
  13.1 0.9 copy-start.3
  15.1 1.1 %copy-start.4 = (f32[32,1024]{1,0:T(8,128)S(1)}, f32[32,1024]{1,0:T(8,128)}, u32[]{:S(2)}) copy-start(f32[32,1024]{1,0:T(8,128)} %right.1) | copy-start | bytes 393220
  16.9 3.1 %collective-permute-start.2 = (f32[4,1024]{1,0:T(4,128)S(1)}, f32[4,1024]{1,0:T(4,128)S(1)}, u32[]{:S(2)}, u32[]{:S(2)}) collective-permute-start(f32[4,1024]{1,0:T(4,128)S(1)} %get-tuple-element.40), channel_id=1, source_target_pairs={{0,1},{2,3},{4,5},{6,7},{8,9},{10,11},{12,13},{14,15},{16,17},{18,... | collective-permute-start | bytes 49160 | tf_op jit(solution)/shard_map/ppermute | solution.py:382
  20.6 5.2 %collective-permute-start.3 = (f32[8,1024]{1,0:T(8,128)S(1)}, f32[8,1024]{1,0:T(8,128)S(1)}, u32[]{:S(2)}, u32[]{:S(2)}) collective-permute-start(f32[8,1024]{1,0:T(8,128)S(1)} %get-tuple-element.43), channel_id=1, source_target_pairs={{1,2},{3,4},{5,6},{7,8},{9,10},{11,12},{13,14},{15,16},{17,18},{19... | collective-permute-start | bytes 98312 | tf_op jit(solution)/shard_map/ppermute | solution.py:382
  26.5 3.3 %collective-permute-start.4 = (f32[4,1024]{1,0:T(4,128)S(1)}, f32[4,1024]{1,0:T(4,128)S(1)}, u32[]{:S(2)}, u32[]{:S(2)}) collective-permute-start(f32[4,1024]{1,0:T(4,128)S(1)} %get-tuple-element.47), channel_id=1, source_target_pairs={{0,1},{2,3},{4,5},{6,7},{8,9},{10,11},{12,13},{14,15},{16,17},{18,... | collective-permute-start | bytes 49160 | tf_op jit(solution)/shard_map/ppermute | solution.py:382
  30.4 3.5 %collective-permute-start.5 = (f32[4,1024]{1,0:T(4,128)S(1)}, f32[4,1024]{1,0:T(4,128)S(1)}, u32[]{:S(2)}, u32[]{:S(2)}) collective-permute-start(f32[4,1024]{1,0:T(4,128)S(1)} %get-tuple-element.49), channel_id=1, source_target_pairs={{0,1},{2,3},{4,5},{6,7},{8,9},{10,11},{12,13},{14,15},{16,17},{18,... | collective-permute-start | bytes 49160 | tf_op jit(solution)/shard_map/ppermute | solution.py:382
  34.6 5.2 %collective-permute-start.6 = (f32[8,1024]{1,0:T(8,128)S(1)}, f32[8,1024]{1,0:T(8,128)S(1)}, u32[]{:S(2)}, u32[]{:S(2)}) collective-permute-start(f32[8,1024]{1,0:T(8,128)S(1)} %get-tuple-element.52), channel_id=1, source_target_pairs={{1,2},{3,4},{5,6},{7,8},{9,10},{11,12},{13,14},{15,16},{17,18},{19... | collective-permute-start | bytes 98312 | tf_op jit(solution)/shard_map/ppermute | solution.py:382
  40.5 3.3 %collective-permute-start.7 = (f32[4,1024]{1,0:T(4,128)S(1)}, f32[4,1024]{1,0:T(4,128)S(1)}, u32[]{:S(2)}, u32[]{:S(2)}) collective-permute-start(f32[4,1024]{1,0:T(4,128)S(1)} %get-tuple-element.57), channel_id=1, source_target_pairs={{0,1},{2,3},{4,5},{6,7},{8,9},{10,11},{12,13},{14,15},{16,17},{18,... | collective-permute-start | bytes 49160 | tf_op jit(solution)/shard_map/ppermute | solution.py:382
  91.0 5.7 %collective-permute-start.8 = (f32[16,128]{1,0:T(8,128)S(1)}, f32[16,128]{1,0:T(8,128)S(1)}, u32[]{:S(2)}, u32[]{:S(2)}) collective-permute-start(f32[16,128]{1,0:T(8,128)S(1)} %reduce_sum.19.mine), channel_id=1, source_target_pairs={{0,1},{2,3},{4,5},{6,7},{8,9},{10,11},{12,13},{14,15},{16,17},{18,... | collective-permute-start | bytes 24584 | tf_op jit(solution)/shard_map/ppermute | solution.py:382

commit v4 on v3

--- a/solution.py
+++ b/solution.py
@@ -101,11 +101,10 @@
 def prep_kernel(blocks, lift, block_parts, lift_parts, spread_blocks):
     for f in range(FACES):
         upper = jnp.concatenate([lift[f], jnp.zeros((NODES, NODES), F32)], 1)
-        high, low = split(jnp.concatenate([upper, swap(upper)], 0))
-        rows = slice(f * 128, f * 128 + 128)
-        lift_parts[rows, :128] = high
-        lift_parts[rows, 128:256] = high
-        lift_parts[rows, 256:] = low
+        high, low = split(jnp.concatenate([upper, swap(upper)], 0).T)
+        lift_parts[:128, slab(f)] = high
+        lift_parts[128:256, slab(f)] = high
+        lift_parts[256:, slab(f)] = low
     mask = left_half((ELEMS, 128))
     for pair in range(NODES // 2):
         two = blocks[:, pair * 128 : pair * 128 + 128]
@@ -123,7 +122,8 @@
     count = vector.shape[0]
     rows = jnp.concatenate([vector[:, slab(t)] for t in range(8)], 0)
     high, low = split(rows)
-    moved = dot_nt(jnp.concatenate([high, low, high], 1), lift_parts[...])
+    both = jnp.concatenate([high, low, high], 1)
+    moved = jnp.dot(both, lift_parts[...], preferred_element_type=F32)
     moved = jnp.concatenate(
         [
             jnp.concatenate([moved[t * count : (t + 1) * count, slab(f)] for t in range(8)], 1)
@@ -161,7 +161,7 @@
     return jnp.concatenate([jnp.concatenate(upper, 1), jnp.concatenate(lower, 1)], 0)
 
 
-def own_part(vector, block_parts, lift_parts, choose, out, tiled, product, other=None):
+def own_part(vector, block_parts, lift_parts, choose, out, tiled, product):
     to_tiles(vector, tiled)
     value = tiled[...].reshape(ELEMS * 8, 128)
     mask = left_half((ELEMS * 8, 128))
@@ -188,8 +188,6 @@
             else:
                 product[group * 4 + part] = jnp.where(mask, swap(top), bottom)
     faces = face_sum(vector[...], lift_parts, choose[:, OWN[0] : OWN[1]])
-    if other is not None:
-        faces = faces + from_sides(choose, lift_parts, other=other[...])
     for t in range(8):
         out[:, slab(t)] = faces[:, slab(t)] + product[:, t, :]
 
@@ -203,14 +201,10 @@
     own_part(vector, block_parts, lift_parts, choose, out, tiled, product)
 
 
-def second_own_kernel(choose, vector, block_parts, lift_parts, other, out, tiled, product):
-    own_part(vector, block_parts, lift_parts, choose, out, tiled, product, other)
-
-
 def dense_own_kernel(
-    choose, vector, block_parts, lift_parts, other, out, high_out, low_out, tiled, product
-):
-    own_part(vector, block_parts, lift_parts, choose, out, tiled, product, other)
+    choose, vector, block_parts, lift_parts, out, high_out, low_out, tiled, product
+):
+    own_part(vector, block_parts, lift_parts, choose, out, tiled, product)
     high_out[...], low_out[...] = split(dense(tiled))
 
 
@@ -259,16 +253,16 @@
     next_other[...] = message[GHOST:] + missing[...]
 
 
-def second_pair_kernel(choose, own, from_pair, lift_parts, out, to_other, to_pair):
-    vector = GAIN * (own[...] + from_sides(choose, lift_parts, pair=from_pair[...]))
+def both_kernel(choose, own, from_other, from_pair, lift_parts, out, to_other, to_pair):
+    vector = GAIN * (own[...] + from_sides(choose, lift_parts, from_other[...], from_pair[...]))
     out[...] = vector
     to_other[...], to_pair[...] = sent_rows(vector, choose)
 
 
 def last_kernel(
-    choose, own, from_pair, lift_parts, high, low, high3, low3, gram, high4, low4, packed, newest, tiled,
-):
-    newest[...] = GAIN * (own[...] + from_sides(choose, lift_parts, pair=from_pair[...]))
+    choose, own, from_other, from_pair, lift_parts, high, low, high3, low3, gram, high4, low4, packed, newest, tiled,
+):
+    newest[...] = GAIN * (own[...] + from_sides(choose, lift_parts, from_other[...], from_pair[...]))
     to_tiles(newest, tiled)
     high4[...], low4[...] = split(dense(tiled))
     left_high = jnp.concatenate([high3[...], high4[...]], 0)
@@ -284,29 +278,28 @@
 
 
 def solve_spd(system):
-    size, block = 64, 8
-    row_id = lax.broadcasted_iota(jnp.int32, (size, 128), 0)
+    size, block = 64, 16
+    row_id = lax.broadcasted_iota(jnp.int32, (block, 128), 0)
     for start in range(0, size, block):
+        stop = start + block
         columns = [jnp.broadcast_to(system[:, start + j : start + j + 1], (size, 128)) for j in range(block)]
-        rows = [system[start + i : start + i + 1, :] for i in range(block)]
-        pivots = [[columns[j][start + i : start + i + 1, :] for j in range(block)] for i in range(block)]
+        pivots = [column[start:stop, :] for column in columns]
+        rows = system[start:stop, :]
         for j in range(block):
-            inverse = 1.0 / pivots[j][j]
-            rows[j] = rows[j] * inverse
+            here = row_id == j
+            inverse = 1.0 / pivots[j][j : j + 1, :]
+            factor = pivots[j]
             for l in range(j + 1, block):
-                pivots[j][l] = pivots[j][l] * inverse
-            for i in range(block):
-                if i != j:
-                    factor = pivots[i][j]
-                    rows[i] = rows[i] - factor * rows[j]
-                    for l in range(j + 1, block):
-                        pivots[i][l] = pivots[i][l] - factor * pivots[j][l]
-        update = system
-        for j in range(block):
-            update = update - columns[j] * rows[j]
-        for j in range(block):
-            update = jnp.where(row_id == start + j, rows[j], update)
-        system = update
+                scaled = pivots[l][j : j + 1, :] * inverse
+                pivots[l] = jnp.where(here, scaled, pivots[l] - factor * scaled)
+            scaled = rows[j : j + 1, :] * inverse
+            rows = jnp.where(here, scaled, rows - factor * scaled)
+        terms = [columns[j] * rows[j : j + 1, :] for j in range(block)]
+        while len(terms) > 1:
+            terms = [a + b for a, b in zip(terms[::2], terms[1::2])]
+        update = system - terms[0]
+        parts = [update[:start], rows, update[stop:]]
+        system = jnp.concatenate([part for part in parts if part.shape[0]], 0)
     return system
 
 
@@ -406,7 +399,7 @@
         prep_kernel,
         [
             jax.ShapeDtypeStruct((ELEMS * NODES, 256), BF16),
-            jax.ShapeDtypeStruct((FACES * 128, 384), BF16),
+            jax.ShapeDtypeStruct((384, FACES * 128), BF16),
         ],
         [pltpu.VMEM((ELEMS, NODES, 128), F32)],
         [VMEM] * 2,
@@ -447,23 +440,21 @@
         basis.append(vector)
         from_pair = swapped(to_pair, axes, 0)
         if half == 0:
-            own = call(second_own_kernel, [FIELD], [tile_scratch] * 2, [VMEM] * 5)(
-                choose, vector, block_parts, lift_parts, next_other
-            )[0]
-            vector, to_other, to_pair = call(second_pair_kernel, [FIELD, sent, sent], [], [VMEM] * 4)(
-                choose, own, from_pair, lift_parts
+            own = own_call(choose, vector, block_parts, lift_parts)
+            vector, to_other, to_pair = call(both_kernel, [FIELD, sent, sent], [], [VMEM] * 5)(
+                choose, own, next_other, from_pair, lift_parts
             )
             basis.append(vector)
         else:
             own, high3, low3 = call(
-                dense_own_kernel, [FIELD, stack(16), stack(16)], [tile_scratch] * 2, [VMEM] * 5
-            )(choose, vector, block_parts, lift_parts, next_other)
+                dense_own_kernel, [FIELD, stack(16), stack(16)], [tile_scratch] * 2, [VMEM] * 4
+            )(choose, vector, block_parts, lift_parts)
     high4, low4, packed = call(
         last_kernel,
         [stack(16), stack(16), jax.ShapeDtypeStruct((32, 128), F32)],
         [pltpu.VMEM((ELEMS, WIDTH), F32), tile_scratch],
-        [VMEM] * 9,
-    )(choose, own, from_pair, lift_parts, high, low, high3, low3, gram)
+        [VMEM] * 10,
+    )(choose, own, next_other, from_pair, lift_parts, high, low, high3, low3, gram)
     outer, inner, narrow = (lax.axis_size(axis) for axis in axes)
     halves = jnp.broadcast_to(packed.reshape(1, 2, 16, 128), (outer * narrow // 2, 2, 16, 128))
     halves = halves.reshape(outer * narrow, 16, 128)

time: 101 us -> 98.5 us (0.975)
  Pallas kernels: 19.1 us -> 16.3 us
    pallas_call x2 -> x1, Pallas kernels: 1.99 us -> 0.53 us  [local(): call(both_kernel, [FIELD, sent, sent], [], [VMEM] * 5)]
    pallas_call x3 -> x4, Pallas kernels: 3.31 us -> 4.29 us  [local(): call(first_own_kernel, [FIELD], [tile_scratch] * 2, [VMEM] * 4)(*args)[0]]
  transfers between devices with their start and end apart: 9 -> 9, of which waited for: 3 -> 6; matrix products, arithmetic and copies ran while one was open for 0% -> 0% of each run, Pallas kernels for 8% -> 8%
where the time goes in v4:
time: 98.5 us; the launch traced here: 98 us
  blocking collectives  45.9 us (47%)
  starting transfers between devices  26.4 us (27%)
  Pallas kernels  16.3 us (17%)
  waiting for transfers between devices  6.52 us (7%)
  local copies, waits for them, and re-layouts  2.07 us (2%)
    all_to_all x1, blocking collectives, local(): mine = lax.all_to_all(halves, (axes[0], axes[2]), 0, 0).sum(0)  29.2 us
    ppermute x9, starting transfers between devices, swapped(): lax.ppermute(block, axes, [(i, i + 1) for i in lower] + [(i + 1, i) for i...  26.4 us
    all_to_all x1, blocking collectives, local(): mine = lax.all_to_all(mine, axes[1], 0, 0).sum(0)  16.6 us
    ppermute x9, waiting for transfers between devices, swapped(): lax.ppermute(block, axes, [(i, i + 1) for i in lower] + [(i + 1, i) for i...  6.52 us
    pallas_call x4, Pallas kernels, local(): call(first_own_kernel, [FIELD], [tile_scratch] * 2, [VMEM] * 4)(*args)[0]  4.29 us
    pallas_call x1, Pallas kernels, local(): call(solve_kernel, [FIELD, FIELD], [pltpu.VMEM((128, 128), F32), pltpu.VM...  2.8 us
    unnamed x10, local copies, waits for them, and re-layouts  1.98 us
  transfers between devices with their start and end apart: 9, of which 6 were waited for; matrix products, arithmetic and copies ran while one was open for 0% of the time, Pallas kernels for 8%

profile of v4, /device:TPU:1, one launch (start us, length us, event | category | flops | bytes accessed | tf_op | source)
XLA Modules:
  0.0 98.0 jit_solution(15264056135529069264)
XLA Ops:
  0.6 1.8 %shard_map.86 = (f32[8,1024]{1,0:T(8,128)}, f32[4,1024]{1,0:T(4,128)}, bf16[32,1024]{1,0:T(8,128)(2,1)}) custom-call(s32[1,8]{1,0:T(1,128)} %send_in.1, f32[32,1024]{1,0:T(8,128)} %guess.3, s32[6,32]{1,0:T(8,128)} %bitcast.6, f32[6,32]{1,0:T(8,128)} %bitcast.7), custom_call_target="tpu_custom_call" | custom-call | tf_op jit(solution)/shard_map/pallas_call | solution.py:381
  2.4 4.5 %collective-permute-start = (f32[8,1024]{1,0:T(8,128)}, f32[8,1024]{1,0:T(8,128)S(1)}, u32[]{:S(2)}, u32[]{:S(2)}) collective-permute-start(f32[8,1024]{1,0:T(8,128)} %get-tuple-element.37), channel_id=1, source_target_pairs={{1,2},{3,4},{5,6},{7,8},{9,10},{11,12},{13,14},{15,16},{17,18},{19... | collective-permute-start | bytes 98312 | tf_op jit(solution)/shard_map/ppermute | solution.py:375
  6.9 0.0 copy-start
  6.9 0.0 copy-start.1
  6.9 5.1 %collective-permute-start.1 = (f32[4,1024]{1,0:T(4,128)}, f32[4,1024]{1,0:T(4,128)S(1)}, u32[]{:S(2)}, u32[]{:S(2)}) collective-permute-start(f32[4,1024]{1,0:T(4,128)} %get-tuple-element.38), channel_id=1, source_target_pairs={{0,1},{2,3},{4,5},{6,7},{8,9},{10,11},{12,13},{14,15},{16,17},{18,... | collective-permute-start | bytes 49160 | tf_op jit(solution)/shard_map/ppermute | solution.py:375
  12.0 0.0 copy-start.2
  12.0 1.0 %copy-done.2 = f32[32,4096]{1,0:T(8,128)S(1)} copy-done((f32[32,4096]{1,0:T(8,128)S(1)}, f32[32,4096]{1,0:T(8,128)}, u32[]{:S(2)}) %copy-start.2) | copy-done | bytes 524312
  13.1 0.0 copy-start.3
  13.1 0.9 copy-done.3
  14.0 1.2 %shard_map.87 = (bf16[2048,256]{1,0:T(8,128)(2,1)S(1)}, bf16[384,768]{1,0:T(8,128)(2,1)S(1)}) custom-call(f32[32,4096]{1,0:T(8,128)S(1)} %copy-done.2, f32[6,64,64]{2,1,0:T(8,128)S(1)} %copy-done.3), custom_call_target="tpu_custom_call" | custom-call | tf_op jit(solution)/shard_map/pallas_call | solution.py:398
  15.2 0.0 copy-done
  15.2 0.0 copy-done.1
  15.2 0.0 copy-start.4
  15.2 1.1 %shard_map.88.own = f32[32,1024]{1,0:T(8,128)S(1)} custom-call(bf16[32,1024]{1,0:T(8,128)(2,1)S(1)} %copy-done, f32[32,1024]{1,0:T(8,128)S(1)} %copy-done.1, bf16[2048,256]{1,0:T(8,128)(2,1)S(1)} %get-tuple-element.35.block_parts, bf16[384,768]{1,0:T(8,128)(2,1)S(1)} %get-tuple-element.36.lift_parts), custom_call_target="tpu_custom_call" | custom-call | tf_op jit(solution)/shard_map/pallas_call | solution.py:408
  16.3 0.0 collective-permute-done.1.from_pair
  16.3 0.0 collective-permute-done.from_other
  16.3 0.0 copy-done.4
  16.3 0.5 shard_map.89
  16.9 1.9 %collective-permute-start.2 = (f32[4,1024]{1,0:T(4,128)S(1)}, f32[4,1024]{1,0:T(4,128)S(1)}, u32[]{:S(2)}, u32[]{:S(2)}) collective-permute-start(f32[4,1024]{1,0:T(4,128)S(1)} %get-tuple-element.40), channel_id=1, source_target_pairs={{0,1},{2,3},{4,5},{6,7},{8,9},{10,11},{12,13},{14,15},{16,17},{18,... | collective-permute-start | bytes 49160 | tf_op jit(solution)/shard_map/ppermute | solution.py:375
  18.8 1.1 %shard_map.90.own = f32[32,1024]{1,0:T(8,128)S(1)} custom-call(bf16[32,1024]{1,0:T(8,128)(2,1)S(1)} %copy-done, f32[32,1024]{1,0:T(8,128)S(1)} %get-tuple-element.39.vector.first, bf16[2048,256]{1,0:T(8,128)(2,1)S(1)} %get-tuple-element.35.block_parts, bf16[384,768]{1,0:T(8,128)(2,1)S(1)} %get-tuple-element.36.lift_parts), custom_call_target="tpu_custom_call" | custom-call | tf_op jit(solution)/shard_map/pallas_call | solution.py:408
  19.9 0.1 collective-permute-done.2.from_pair
  19.9 0.5 shard_map.91
  20.5 1.9 %collective-permute-start.3 = (f32[8,1024]{1,0:T(8,128)S(1)}, f32[8,1024]{1,0:T(8,128)S(1)}, u32[]{:S(2)}, u32[]{:S(2)}) collective-permute-start(f32[8,1024]{1,0:T(8,128)S(1)} %get-tuple-element.43), channel_id=1, source_target_pairs={{1,2},{3,4},{5,6},{7,8},{9,10},{11,12},{13,14},{15,16},{17,18},{19... | collective-permute-start | bytes 98312 | tf_op jit(solution)/shard_map/ppermute | solution.py:375
  22.4 0.4 shard_map.92.missing
  22.8 2.9 %collective-permute-done.3.message = f32[8,1024]{1,0:T(8,128)S(1)} collective-permute-done((f32[8,1024]{1,0:T(8,128)S(1)}, f32[8,1024]{1,0:T(8,128)S(1)}, u32[]{:S(2)}, u32[]{:S(2)}) %collective-permute-start.3) | collective-permute-done | bytes 32800 | tf_op jit(solution)/shard_map/ppermute | solution.py:375
  25.7 0.5 shard_map.93
  26.2 1.9 %collective-permute-start.4 = (f32[4,1024]{1,0:T(4,128)S(1)}, f32[4,1024]{1,0:T(4,128)S(1)}, u32[]{:S(2)}, u32[]{:S(2)}) collective-permute-start(f32[4,1024]{1,0:T(4,128)S(1)} %get-tuple-element.47), channel_id=1, source_target_pairs={{0,1},{2,3},{4,5},{6,7},{8,9},{10,11},{12,13},{14,15},{16,17},{18,... | collective-permute-start | bytes 49160 | tf_op jit(solution)/shard_map/ppermute | solution.py:375
  28.2 1.1 %shard_map.94.own = f32[32,1024]{1,0:T(8,128)S(1)} custom-call(bf16[32,1024]{1,0:T(8,128)(2,1)S(1)} %copy-done, f32[32,1024]{1,0:T(8,128)S(1)} %get-tuple-element.45.vector.second, bf16[2048,256]{1,0:T(8,128)(2,1)S(1)} %get-tuple-element.35.block_parts, bf16[384,768]{1,0:T(8,128)(2,1)S(1)} %get-tuple-element.36.lift_parts), custom_call_target="tpu_custom_call" | custom-call | tf_op jit(solution)/shard_map/pallas_call | solution.py:408
  29.2 0.1 collective-permute-done.4.from_pair
  29.3 0.5 shard_map.95
  29.8 2.3 %collective-permute-start.5 = (f32[4,1024]{1,0:T(4,128)S(1)}, f32[4,1024]{1,0:T(4,128)S(1)}, u32[]{:S(2)}, u32[]{:S(2)}) collective-permute-start(f32[4,1024]{1,0:T(4,128)S(1)} %get-tuple-element.49), channel_id=1, source_target_pairs={{0,1},{2,3},{4,5},{6,7},{8,9},{10,11},{12,13},{14,15},{16,17},{18,... | collective-permute-start | bytes 49160 | tf_op jit(solution)/shard_map/ppermute | solution.py:375
  32.2 1.1 %shard_map.96.own = f32[32,1024]{1,0:T(8,128)S(1)} custom-call(bf16[32,1024]{1,0:T(8,128)(2,1)S(1)} %copy-done, f32[32,1024]{1,0:T(8,128)S(1)} %get-tuple-element.48.vector.third, bf16[2048,256]{1,0:T(8,128)(2,1)S(1)} %get-tuple-element.35.block_parts, bf16[384,768]{1,0:T(8,128)(2,1)S(1)} %get-tuple-element.36.lift_parts), custom_call_target="tpu_custom_call" | custom-call | tf_op jit(solution)/shard_map/pallas_call | solution.py:408
  33.3 0.0 collective-permute-done.5.from_pair
  33.3 0.5 shard_map.97
  33.8 1.9 %collective-permute-start.6 = (f32[8,1024]{1,0:T(8,128)S(1)}, f32[8,1024]{1,0:T(8,128)S(1)}, u32[]{:S(2)}, u32[]{:S(2)}) collective-permute-start(f32[8,1024]{1,0:T(8,128)S(1)} %get-tuple-element.52), channel_id=1, source_target_pairs={{1,2},{3,4},{5,6},{7,8},{9,10},{11,12},{13,14},{15,16},{17,18},{19... | collective-permute-start | bytes 98312 | tf_op jit(solution)/shard_map/ppermute | solution.py:375
  35.7 0.7 shard_map.98
  36.5 2.6 %collective-permute-done.6.message = f32[8,1024]{1,0:T(8,128)S(1)} collective-permute-done((f32[8,1024]{1,0:T(8,128)S(1)}, f32[8,1024]{1,0:T(8,128)S(1)}, u32[]{:S(2)}, u32[]{:S(2)}) %collective-permute-start.6) | collective-permute-done | bytes 32800 | tf_op jit(solution)/shard_map/ppermute | solution.py:375
  39.0 0.5 shard_map.99
  39.6 1.9 %collective-permute-start.7 = (f32[4,1024]{1,0:T(4,128)S(1)}, f32[4,1024]{1,0:T(4,128)S(1)}, u32[]{:S(2)}, u32[]{:S(2)}) collective-permute-start(f32[4,1024]{1,0:T(4,128)S(1)} %get-tuple-element.57), channel_id=1, source_target_pairs={{0,1},{2,3},{4,5},{6,7},{8,9},{10,11},{12,13},{14,15},{16,17},{18,... | collective-permute-start | bytes 49160 | tf_op jit(solution)/shard_map/ppermute | solution.py:375
  41.5 1.1 %shard_map.100 = (f32[32,1024]{1,0:T(8,128)S(1)}, bf16[16,2048]{1,0:T(8,128)(2,1)S(1)}, bf16[16,2048]{1,0:T(8,128)(2,1)S(1)}) custom-call(bf16[32,1024]{1,0:T(8,128)(2,1)S(1)} %copy-done, f32[32,1024]{1,0:T(8,128)S(1)} %get-tuple-element.54.vector, bf16[2048,256]{1,0:T(8,128)(2,1)S(1)} %get-tuple-element.35.block_parts, ...), custom_call_target="tpu_custom_call" | custom-call | tf_op jit(solution)/shard_map/pallas_call | solution.py:449
  42.6 0.1 collective-permute-done.7.from_pair
  42.6 0.9 shard_map.101
  43.5 0.1 broadcast_in_dim.14
  43.6 29.2 %all_to_all.10 = f32[32,16,128]{2,1,0:T(8,128)S(1)} all-to-all(f32[32,16,128]{2,1,0:T(8,128)S(1)} %bitcast.5), channel_id=1, replica_groups=mesh['outer'=4,'inner'=16,'narrow'=8] {'outer','narrow'}, dimensions={0} | all-to-all | bytes 524288 | tf_op jit(solution)/shard_map/all_to_all | solution.py:461
  72.9 16.6 %all_to_all.11 = f32[16,16,128]{2,1,0:T(8,128)S(1)} all-to-all(f32[16,16,128]{2,1,0:T(8,128)S(1)} %broadcast_in_dim.15), channel_id=1, replica_groups=mesh['outer'=4,'inner'=16,'narrow'=8] {'inner'}, dimensions={0} | all-to-all | bytes 262144 | tf_op jit(solution)/shard_map/all_to_all | solution.py:463
  89.6 4.9 %collective-permute-start.8 = (f32[16,128]{1,0:T(8,128)S(1)}, f32[16,128]{1,0:T(8,128)S(1)}, u32[]{:S(2)}, u32[]{:S(2)}) collective-permute-start(f32[16,128]{1,0:T(8,128)S(1)} %reduce_sum.19.mine), channel_id=1, source_target_pairs={{0,1},{2,3},{4,5},{6,7},{8,9},{10,11},{12,13},{14,15},{16,17},{18,... | collective-permute-start | bytes 24584 | tf_op jit(solution)/shard_map/ppermute | solution.py:375
  94.4 0.8 collective-permute-done.8.theirs
  95.2 2.8 %shard_map.102 = (f32[32,1024]{1,0:T(8,128)}, f32[32,1024]{1,0:T(8,128)}) custom-call(f32[16,128]{1,0:T(8,128)S(1)} %reduce_sum.19.mine, f32[16,128]{1,0:T(8,128)S(1)} %collective-permute-done.8.theirs, bf16[48,2048]{1,0:T(8,128)(2,1)S(1)} %get-tuple-element.58.high, bf16[48,2048]{1,0:T(8,128)(2,1)S(1)} %get-tuple-element.59.low, ...), custom_call_target="tpu_custom_call" | custom-call | tf_op jit(solution)/shard_map/pallas_call | solution.py:466
  (3 shorter events, 0.1 us)
Async XLA Ops:
  2.4 13.9 %collective-permute-start = (f32[8,1024]{1,0:T(8,128)}, f32[8,1024]{1,0:T(8,128)S(1)}, u32[]{:S(2)}, u32[]{:S(2)}) collective-permute-start(f32[8,1024]{1,0:T(8,128)} %get-tuple-element.37), channel_id=1, source_target_pairs={{1,2},{3,4},{5,6},{7,8},{9,10},{11,12},{13,14},{15,16},{17,18},{19... | collective-permute-start | bytes 98312 | tf_op jit(solution)/shard_map/ppermute | solution.py:375
  6.9 8.3 %copy-start = (bf16[32,1024]{1,0:T(8,128)(2,1)S(1)}, bf16[32,1024]{1,0:T(8,128)(2,1)}, u32[]{:S(2)}) copy-start(bf16[32,1024]{1,0:T(8,128)(2,1)} %get-tuple-element.34.choose) | copy-start | bytes 196612
  6.9 8.3 %copy-start.1 = (f32[32,1024]{1,0:T(8,128)S(1)}, f32[32,1024]{1,0:T(8,128)}, u32[]{:S(2)}) copy-start(f32[32,1024]{1,0:T(8,128)} %guess.3) | copy-start | bytes 393220
  6.9 9.4 %collective-permute-start.1 = (f32[4,1024]{1,0:T(4,128)}, f32[4,1024]{1,0:T(4,128)S(1)}, u32[]{:S(2)}, u32[]{:S(2)}) collective-permute-start(f32[4,1024]{1,0:T(4,128)} %get-tuple-element.38), channel_id=1, source_target_pairs={{0,1},{2,3},{4,5},{6,7},{8,9},{10,11},{12,13},{14,15},{16,17},{18,... | collective-permute-start | bytes 49160 | tf_op jit(solution)/shard_map/ppermute | solution.py:375
  12.0 1.0 %copy-start.2 = (f32[32,4096]{1,0:T(8,128)S(1)}, f32[32,4096]{1,0:T(8,128)}, u32[]{:S(2)}) copy-start(f32[32,4096]{1,0:T(8,128)} %blocks.1) | copy-start | bytes 1572868
  13.1 0.9 copy-start.3
  15.2 1.1 %copy-start.4 = (f32[32,1024]{1,0:T(8,128)S(1)}, f32[32,1024]{1,0:T(8,128)}, u32[]{:S(2)}) copy-start(f32[32,1024]{1,0:T(8,128)} %right.1) | copy-start | bytes 393220
  16.9 3.1 %collective-permute-start.2 = (f32[4,1024]{1,0:T(4,128)S(1)}, f32[4,1024]{1,0:T(4,128)S(1)}, u32[]{:S(2)}, u32[]{:S(2)}) collective-permute-start(f32[4,1024]{1,0:T(4,128)S(1)} %get-tuple-element.40), channel_id=1, source_target_pairs={{0,1},{2,3},{4,5},{6,7},{8,9},{10,11},{12,13},{14,15},{16,17},{18,... | collective-permute-start | bytes 49160 | tf_op jit(solution)/shard_map/ppermute | solution.py:375
  20.5 5.2 %collective-permute-start.3 = (f32[8,1024]{1,0:T(8,128)S(1)}, f32[8,1024]{1,0:T(8,128)S(1)}, u32[]{:S(2)}, u32[]{:S(2)}) collective-permute-start(f32[8,1024]{1,0:T(8,128)S(1)} %get-tuple-element.43), channel_id=1, source_target_pairs={{1,2},{3,4},{5,6},{7,8},{9,10},{11,12},{13,14},{15,16},{17,18},{19... | collective-permute-start | bytes 98312 | tf_op jit(solution)/shard_map/ppermute | solution.py:375
  26.2 3.1 %collective-permute-start.4 = (f32[4,1024]{1,0:T(4,128)S(1)}, f32[4,1024]{1,0:T(4,128)S(1)}, u32[]{:S(2)}, u32[]{:S(2)}) collective-permute-start(f32[4,1024]{1,0:T(4,128)S(1)} %get-tuple-element.47), channel_id=1, source_target_pairs={{0,1},{2,3},{4,5},{6,7},{8,9},{10,11},{12,13},{14,15},{16,17},{18,... | collective-permute-start | bytes 49160 | tf_op jit(solution)/shard_map/ppermute | solution.py:375
  29.8 3.4 %collective-permute-start.5 = (f32[4,1024]{1,0:T(4,128)S(1)}, f32[4,1024]{1,0:T(4,128)S(1)}, u32[]{:S(2)}, u32[]{:S(2)}) collective-permute-start(f32[4,1024]{1,0:T(4,128)S(1)} %get-tuple-element.49), channel_id=1, source_target_pairs={{0,1},{2,3},{4,5},{6,7},{8,9},{10,11},{12,13},{14,15},{16,17},{18,... | collective-permute-start | bytes 49160 | tf_op jit(solution)/shard_map/ppermute | solution.py:375
  33.8 5.2 %collective-permute-start.6 = (f32[8,1024]{1,0:T(8,128)S(1)}, f32[8,1024]{1,0:T(8,128)S(1)}, u32[]{:S(2)}, u32[]{:S(2)}) collective-permute-start(f32[8,1024]{1,0:T(8,128)S(1)} %get-tuple-element.52), channel_id=1, source_target_pairs={{1,2},{3,4},{5,6},{7,8},{9,10},{11,12},{13,14},{15,16},{17,18},{19... | collective-permute-start | bytes 98312 | tf_op jit(solution)/shard_map/ppermute | solution.py:375
  39.6 3.1 %collective-permute-start.7 = (f32[4,1024]{1,0:T(4,128)S(1)}, f32[4,1024]{1,0:T(4,128)S(1)}, u32[]{:S(2)}, u32[]{:S(2)}) collective-permute-start(f32[4,1024]{1,0:T(4,128)S(1)} %get-tuple-element.57), channel_id=1, source_target_pairs={{0,1},{2,3},{4,5},{6,7},{8,9},{10,11},{12,13},{14,15},{16,17},{18,... | collective-permute-start | bytes 49160 | tf_op jit(solution)/shard_map/ppermute | solution.py:375
  89.6 5.7 %collective-permute-start.8 = (f32[16,128]{1,0:T(8,128)S(1)}, f32[16,128]{1,0:T(8,128)S(1)}, u32[]{:S(2)}, u32[]{:S(2)}) collective-permute-start(f32[16,128]{1,0:T(8,128)S(1)} %reduce_sum.19.mine), channel_id=1, source_target_pairs={{0,1},{2,3},{4,5},{6,7},{8,9},{10,11},{12,13},{14,15},{16,17},{18,... | collective-permute-start | bytes 24584 | tf_op jit(solution)/shard_map/ppermute | solution.py:375

commit v5 on v4

--- a/solution.py
+++ b/solution.py
@@ -85,12 +85,12 @@
     choose[:, FROM[0] : FROM[1]] = three_parts(ghosts, 0).T.astype(BF16)
     terms[...] = jnp.zeros((ELEMS, 128), F32)
     terms[:, : FACES * 2 * GHOST] = ghosts.T
-    to_other[GHOST:, :] = jnp.zeros((GHOST, WIDTH), F32)
-    for k in range(GHOST):
-        row = send[0, GHOST * odd + k]
-        to_other[k : k + 1, :] = guess[pl.ds(row, 1), :]
-        to_other[GHOST + k : GHOST + k + 1, :128] = terms[pl.ds(row, 1), :]
-        to_pair[k : k + 1, :] = guess[pl.ds(send[0, GHOST * (1 - odd) + k], 1), :]
+    for out, first in ((to_other, GHOST * odd), (to_pair, GHOST * (1 - odd))):
+        out[GHOST:, :] = jnp.zeros((GHOST, WIDTH), F32)
+        for k in range(GHOST):
+            row = send[0, first + k]
+            out[k : k + 1, :] = guess[pl.ds(row, 1), :]
+            out[GHOST + k : GHOST + k + 1, :128] = terms[pl.ds(row, 1), :]
     row = send_row[...]
     row = jnp.where(odd == 1, jnp.concatenate([row[:, GHOST:], row[:, :GHOST]], 1), row)
     rows = (lax.broadcasted_iota(jnp.int32, (ELEMS, 2 * GHOST), 0) == row).astype(F32)
@@ -209,14 +209,17 @@
 
 
 def first_ghost_kernel(
-    choose, own, from_other, from_pair, lift_parts, right, guess, out, to_other, to_pair, terms
-):
-    faces = from_sides(choose, lift_parts, from_other[:GHOST], from_pair[...])
+    choose, own, from_other, from_pair, lift_parts, right, guess,
+    out, to_other, to_pair, terms, pair_terms,
+):
+    faces = from_sides(choose, lift_parts, from_other[:GHOST], from_pair[:GHOST])
     vector = right[...] - (guess[...] + (own[...] + faces))
     out[...] = vector
     to_other[...], to_pair[...] = sent_rows(vector, choose)
-    partner = three_parts(from_other[GHOST:, : FACES * 2 * GHOST], 1)
-    terms[...] = jnp.concatenate([partner, jnp.zeros((16 - GHOST, partner.shape[1]), F32)], 0).astype(BF16)
+    for sent, out in ((from_other, terms), (from_pair, pair_terms)):
+        theirs = three_parts(sent[GHOST:, : FACES * 2 * GHOST], 1)
+        empty = jnp.zeros((16 - GHOST, theirs.shape[1]), F32)
+        out[...] = jnp.concatenate([theirs, empty], 0).astype(BF16)
 
 
 def pair_kernel(choose, own, from_pair, lift_parts, to_other, partial, message):
@@ -243,6 +246,39 @@
         to_tiles(vector, tiled)
         high[16 * a : 16 * a + 16], low[16 * a : 16 * a + 16] = split(dense(tiled))
     gram[...] = gram_of(high[...], low[...], high[...], low[...])
+
+
+def other_own_kernel(
+    choose, partial, message, missing, block_parts, lift_parts, out, own, to_pair, outgoing, tiled, product
+):
+    vector = GAIN * (partial[...] + from_sides(choose, lift_parts, other=message[:GHOST]))
+    out[...] = vector
+    own_part(out, block_parts, lift_parts, choose, own, tiled, product)
+    total = own[...] + from_sides(choose, lift_parts, other=message[GHOST:] + missing[...])
+    own[...] = total
+    rows = sent_rows(vector, choose)[1]
+    to_pair[...] = rows
+    outgoing[:GHOST] = rows
+    outgoing[GHOST:] = sent_rows(GAIN * total, choose)[1]
+
+
+def pair_flight_kernel(terms, lift_parts, to_pair, missing):
+    rows = jnp.concatenate([jnp.zeros((GHOST, WIDTH), F32), to_pair[...]], 0)
+    missing[...] = GAIN * face_sum(rows, lift_parts, terms[...])[:GHOST]
+
+
+def pair_own_kernel(
+    choose, own, message, missing, block_parts, lift_parts, out, partial, to_other, outgoing, tiled, product
+):
+    vector = GAIN * (own[...] + from_sides(choose, lift_parts, pair=message[:GHOST]))
+    out[...] = vector
+    own_part(out, block_parts, lift_parts, choose, partial, tiled, product)
+    total = partial[...] + from_sides(choose, lift_parts, pair=message[GHOST:] + missing[...])
+    partial[...] = total
+    rows = sent_rows(vector, choose)[0]
+    to_other[...] = rows
+    outgoing[:GHOST] = rows
+    outgoing[GHOST:] = sent_rows(GAIN * total, choose)[0]
 
 
 def other_kernel(choose, partial, message, missing, lift_parts, out, to_pair, next_other):
@@ -251,12 +287,6 @@
     out[...] = vector
     to_pair[...] = sent_rows(vector, choose)[1]
     next_other[...] = message[GHOST:] + missing[...]
-
-
-def both_kernel(choose, own, from_other, from_pair, lift_parts, out, to_other, to_pair):
-    vector = GAIN * (own[...] + from_sides(choose, lift_parts, from_other[...], from_pair[...]))
-    out[...] = vector
-    to_other[...], to_pair[...] = sent_rows(vector, choose)
 
 
 def last_kernel(
@@ -380,7 +410,7 @@
     message = jax.ShapeDtypeStruct((2 * GHOST, WIDTH), F32)
     to_other, to_pair, choose = call(
         pack_kernel,
-        [message, sent, jax.ShapeDtypeStruct((ELEMS, 1024), BF16)],
+        [message, message, jax.ShapeDtypeStruct((ELEMS, 1024), BF16)],
         [
             pltpu.VMEM((ELEMS, WIDTH), F32),
             pltpu.VMEM((FACES, ELEMS), jnp.int32),
@@ -409,46 +439,46 @@
         first_own_kernel, [FIELD], [tile_scratch] * 2, [VMEM] * 4
     )(*args)[0]
     own = own_call(choose, start_guess, block_parts, lift_parts)
-    basis = []
-    vector, to_other, to_pair, terms = call(
+    vector, to_other, to_pair, terms, pair_terms = call(
         first_ghost_kernel,
-        [FIELD, sent, sent, jax.ShapeDtypeStruct((16, 3 * FACES * 2 * GHOST), BF16)],
+        [FIELD, sent, sent] + [jax.ShapeDtypeStruct((16, 3 * FACES * 2 * GHOST), BF16)] * 2,
         [],
         [VMEM] * 7,
     )(choose, own, from_other, from_pair, lift_parts, right_side, start_guess)
+    basis = [vector]
+    stack = lambda rows: jax.ShapeDtypeStruct((rows, ELEMS * NODES), BF16)
+    from_pair = swapped(to_pair, axes, 0)
+    own = own_call(choose, vector, block_parts, lift_parts)
+    partial, outgoing = call(pair_kernel, [FIELD, message], [], [VMEM] * 5)(
+        choose, own, from_pair, lift_parts, to_other
+    )
+    incoming = swapped(outgoing, axes, 1)
+    missing = call(flight_kernel, [sent], [], [VMEM] * 3)(terms, lift_parts, to_other)[0]
+    joint = [FIELD, FIELD, sent, message], [tile_scratch] * 2, [VMEM] * 6
+    vector, own, to_pair, outgoing = call(other_own_kernel, *joint)(
+        choose, partial, incoming, missing, block_parts, lift_parts
+    )
     basis.append(vector)
-    stack = lambda rows: jax.ShapeDtypeStruct((rows, ELEMS * NODES), BF16)
-    for half in range(2):
-        from_pair = swapped(to_pair, axes, 0)
-        own = own_call(choose, vector, block_parts, lift_parts)
-        partial, outgoing = call(pair_kernel, [FIELD, message], [], [VMEM] * 5)(
-            choose, own, from_pair, lift_parts, to_other
-        )
-        incoming = swapped(outgoing, axes, 1)
-        if half == 0:
-            missing = call(flight_kernel, [sent], [], [VMEM] * 3)(terms, lift_parts, to_other)[0]
-        else:
-            missing, high, low, gram = call(
-                gram_flight_kernel,
-                [sent, stack(48), stack(48), jax.ShapeDtypeStruct((48, 48), F32)],
-                [tile_scratch],
-                [VMEM] * 6,
-            )(terms, lift_parts, to_other, *basis)
-        vector, to_pair, next_other = call(other_kernel, [FIELD, sent, sent], [], [VMEM] * 5)(
-            choose, partial, incoming, missing, lift_parts
-        )
-        basis.append(vector)
-        from_pair = swapped(to_pair, axes, 0)
-        if half == 0:
-            own = own_call(choose, vector, block_parts, lift_parts)
-            vector, to_other, to_pair = call(both_kernel, [FIELD, sent, sent], [], [VMEM] * 5)(
-                choose, own, next_other, from_pair, lift_parts
-            )
-            basis.append(vector)
-        else:
-            own, high3, low3 = call(
-                dense_own_kernel, [FIELD, stack(16), stack(16)], [tile_scratch] * 2, [VMEM] * 4
-            )(choose, vector, block_parts, lift_parts)
+    incoming = swapped(outgoing, axes, 0)
+    missing = call(pair_flight_kernel, [sent], [], [VMEM] * 3)(pair_terms, lift_parts, to_pair)[0]
+    vector, partial, to_other, outgoing = call(pair_own_kernel, *joint)(
+        choose, own, incoming, missing, block_parts, lift_parts
+    )
+    basis.append(vector)
+    incoming = swapped(outgoing, axes, 1)
+    missing, high, low, gram = call(
+        gram_flight_kernel,
+        [sent, stack(48), stack(48), jax.ShapeDtypeStruct((48, 48), F32)],
+        [tile_scratch],
+        [VMEM] * 6,
+    )(terms, lift_parts, to_other, *basis)
+    vector, to_pair, next_other = call(other_kernel, [FIELD, sent, sent], [], [VMEM] * 5)(
+        choose, partial, incoming, missing, lift_parts
+    )
+    from_pair = swapped(to_pair, axes, 0)
+    own, high3, low3 = call(
+        dense_own_kernel, [FIELD, stack(16), stack(16)], [tile_scratch] * 2, [VMEM] * 4
+    )(choose, vector, block_parts, lift_parts)
     high4, low4, packed = call(
         last_kernel,
         [stack(16), stack(16), jax.ShapeDtypeStruct((32, 128), F32)],

time: 98.5 us -> 97.3 us (0.988)
  starting transfers between devices: 26.4 us -> 24 us
    pallas_call x3 -> x5, Pallas kernels: 2.82 us -> 6.44 us  [the longest x1 1.88 us: local(): call(pair_own_kernel, *joint)]
    ppermute x9 -> x8, starting transfers between devices: 26.4 us -> 24 us  [swapped(): lax.ppermute(block, axes, [(i, i + 1) for i in lower] + [(i + 1, i) for i...]
    pallas_call x4 -> x2, Pallas kernels: 4.29 us -> 2.16 us  [local(): call(first_own_kernel, [FIELD], [tile_scratch] * 2, [VMEM] * 4)(*args)[0]]
    ppermute x9 -> x8, waiting for transfers between devices: 6.52 us -> 7.22 us  [swapped(): lax.ppermute(block, axes, [(i, i + 1) for i in lower] + [(i + 1, i) for i...]
  transfers between devices with their start and end apart: 9 -> 8, of which waited for: 6 -> 6; matrix products, arithmetic and copies ran while one was open for 0% -> 0% of each run, Pallas kernels for 8% -> 6%
where the time goes in v5:
time: 97.3 us; the launch traced here: 96.8 us
  blocking collectives  45.9 us (47%)
  starting transfers between devices  24 us (25%)
  Pallas kernels  16.7 us (17%)
  waiting for transfers between devices  7.22 us (7%)
  local copies, waits for them, and re-layouts  2.07 us (2%)
    all_to_all x1, blocking collectives, local(): mine = lax.all_to_all(halves, (axes[0], axes[2]), 0, 0).sum(0)  29.2 us
    ppermute x8, starting transfers between devices, swapped(): lax.ppermute(block, axes, [(i, i + 1) for i in lower] + [(i + 1, i) for i...  24 us
    all_to_all x1, blocking collectives, local(): mine = lax.all_to_all(mine, axes[1], 0, 0).sum(0)  16.7 us
    ppermute x8, waiting for transfers between devices, swapped(): lax.ppermute(block, axes, [(i, i + 1) for i in lower] + [(i + 1, i) for i...  7.22 us
    pallas_call x1, Pallas kernels, local(): call(solve_kernel, [FIELD, FIELD], [pltpu.VMEM((128, 128), F32), pltpu.VM...  2.8 us
    pallas_call x2, Pallas kernels, local(): call(first_own_kernel, [FIELD], [tile_scratch] * 2, [VMEM] * 4)(*args)[0]  2.16 us
    unnamed x10, local copies, waits for them, and re-layouts  1.98 us
  transfers between devices with their start and end apart: 8, of which 6 were waited for; matrix products, arithmetic and copies ran while one was open for 0% of the time, Pallas kernels for 6%

profile of v5, /device:TPU:1, one launch (start us, length us, event | category | flops | bytes accessed | tf_op | source)
XLA Modules:
  0.0 96.8 jit_solution(617335677363226445)
XLA Ops:
  0.6 1.8 %shard_map.86 = (f32[8,1024]{1,0:T(8,128)}, f32[8,1024]{1,0:T(8,128)}, bf16[32,1024]{1,0:T(8,128)(2,1)}) custom-call(s32[1,8]{1,0:T(1,128)} %send_in.1, f32[32,1024]{1,0:T(8,128)} %guess.3, s32[6,32]{1,0:T(8,128)} %bitcast.6, f32[6,32]{1,0:T(8,128)} %bitcast.7), custom_call_target="tpu_custom_call" | custom-call | tf_op jit(solution)/shard_map/pallas_call | solution.py:411
  2.4 4.5 %collective-permute-start = (f32[8,1024]{1,0:T(8,128)}, f32[8,1024]{1,0:T(8,128)S(1)}, u32[]{:S(2)}, u32[]{:S(2)}) collective-permute-start(f32[8,1024]{1,0:T(8,128)} %get-tuple-element.38), channel_id=1, source_target_pairs={{1,2},{3,4},{5,6},{7,8},{9,10},{11,12},{13,14},{15,16},{17,18},{19... | collective-permute-start | bytes 98312 | tf_op jit(solution)/shard_map/ppermute | solution.py:405
  6.9 0.0 copy-start
  6.9 0.0 copy-start.1
  6.9 5.1 %collective-permute-start.1 = (f32[8,1024]{1,0:T(8,128)}, f32[8,1024]{1,0:T(8,128)S(1)}, u32[]{:S(2)}, u32[]{:S(2)}) collective-permute-start(f32[8,1024]{1,0:T(8,128)} %get-tuple-element.39), channel_id=1, source_target_pairs={{0,1},{2,3},{4,5},{6,7},{8,9},{10,11},{12,13},{14,15},{16,17},{18,... | collective-permute-start | bytes 98312 | tf_op jit(solution)/shard_map/ppermute | solution.py:405
  12.0 0.0 copy-start.2
  12.0 1.0 %copy-done.2 = f32[32,4096]{1,0:T(8,128)S(1)} copy-done((f32[32,4096]{1,0:T(8,128)S(1)}, f32[32,4096]{1,0:T(8,128)}, u32[]{:S(2)}) %copy-start.2) | copy-done | bytes 524312
  13.1 0.0 copy-start.3
  13.1 0.9 copy-done.3
  14.0 1.2 %shard_map.87 = (bf16[2048,256]{1,0:T(8,128)(2,1)S(1)}, bf16[384,768]{1,0:T(8,128)(2,1)S(1)}) custom-call(f32[32,4096]{1,0:T(8,128)S(1)} %copy-done.2, f32[6,64,64]{2,1,0:T(8,128)S(1)} %copy-done.3), custom_call_target="tpu_custom_call" | custom-call | tf_op jit(solution)/shard_map/pallas_call | solution.py:428
  15.2 0.0 copy-done
  15.2 0.0 copy-done.1
  15.2 0.0 copy-start.4
  15.2 1.1 %shard_map.88.own = f32[32,1024]{1,0:T(8,128)S(1)} custom-call(bf16[32,1024]{1,0:T(8,128)(2,1)S(1)} %copy-done, f32[32,1024]{1,0:T(8,128)S(1)} %copy-done.1, bf16[2048,256]{1,0:T(8,128)(2,1)S(1)} %get-tuple-element.36.block_parts, bf16[384,768]{1,0:T(8,128)(2,1)S(1)} %get-tuple-element.37.lift_parts), custom_call_target="tpu_custom_call" | custom-call | tf_op jit(solution)/shard_map/pallas_call | solution.py:438
  16.3 0.0 collective-permute-done.from_other
  16.3 0.0 collective-permute-done.1.from_pair
  16.3 0.0 copy-done.4
  16.3 0.5 shard_map.89
  16.9 1.9 %collective-permute-start.2 = (f32[4,1024]{1,0:T(4,128)S(1)}, f32[4,1024]{1,0:T(4,128)S(1)}, u32[]{:S(2)}, u32[]{:S(2)}) collective-permute-start(f32[4,1024]{1,0:T(4,128)S(1)} %get-tuple-element.41), channel_id=1, source_target_pairs={{0,1},{2,3},{4,5},{6,7},{8,9},{10,11},{12,13},{14,15},{16,17},{18,... | collective-permute-start | bytes 49160 | tf_op jit(solution)/shard_map/ppermute | solution.py:405
  18.8 1.1 %shard_map.90.own = f32[32,1024]{1,0:T(8,128)S(1)} custom-call(bf16[32,1024]{1,0:T(8,128)(2,1)S(1)} %copy-done, f32[32,1024]{1,0:T(8,128)S(1)} %get-tuple-element.40.vector.first, bf16[2048,256]{1,0:T(8,128)(2,1)S(1)} %get-tuple-element.36.block_parts, bf16[384,768]{1,0:T(8,128)(2,1)S(1)} %get-tuple-element.37.lift_parts), custom_call_target="tpu_custom_call" | custom-call | tf_op jit(solution)/shard_map/pallas_call | solution.py:438
  19.9 0.1 collective-permute-done.2.from_pair
  19.9 0.5 shard_map.91
  20.5 1.9 %collective-permute-start.3 = (f32[8,1024]{1,0:T(8,128)S(1)}, f32[8,1024]{1,0:T(8,128)S(1)}, u32[]{:S(2)}, u32[]{:S(2)}) collective-permute-start(f32[8,1024]{1,0:T(8,128)S(1)} %get-tuple-element.44), channel_id=1, source_target_pairs={{1,2},{3,4},{5,6},{7,8},{9,10},{11,12},{13,14},{15,16},{17,18},{19... | collective-permute-start | bytes 98312 | tf_op jit(solution)/shard_map/ppermute | solution.py:405
  22.4 0.4 shard_map.92.missing
  22.8 2.9 %collective-permute-done.3.message = f32[8,1024]{1,0:T(8,128)S(1)} collective-permute-done((f32[8,1024]{1,0:T(8,128)S(1)}, f32[8,1024]{1,0:T(8,128)S(1)}, u32[]{:S(2)}, u32[]{:S(2)}) %collective-permute-start.3) | collective-permute-done | bytes 32800 | tf_op jit(solution)/shard_map/ppermute | solution.py:405
  25.7 1.9 %shard_map.93 = (f32[32,1024]{1,0:T(8,128)S(1)}, f32[32,1024]{1,0:T(8,128)S(1)}, f32[4,1024]{1,0:T(4,128)S(1)}, f32[8,1024]{1,0:T(8,128)S(1)}) custom-call(bf16[32,1024]{1,0:T(8,128)(2,1)S(1)} %copy-done, f32[32,1024]{1,0:T(8,128)S(1)} %get-tuple-element.43.partial, f32[8,1024]{1,0:T(8,128)S(1)} %collective-permute-done.3.message, ...), custom_call_target="tpu_custom_call" | custom-call | tf_op jit(solution)/shard_map/pallas_call | solution.py:458
  27.6 1.9 %collective-permute-start.4 = (f32[8,1024]{1,0:T(8,128)S(1)}, f32[8,1024]{1,0:T(8,128)S(1)}, u32[]{:S(2)}, u32[]{:S(2)}) collective-permute-start(f32[8,1024]{1,0:T(8,128)S(1)} %get-tuple-element.47), channel_id=1, source_target_pairs={{0,1},{2,3},{4,5},{6,7},{8,9},{10,11},{12,13},{14,15},{16,17},{18,... | collective-permute-start | bytes 98312 | tf_op jit(solution)/shard_map/ppermute | solution.py:405
  29.5 0.4 shard_map.94.missing
  29.9 0.8 collective-permute-done.4.message
  30.7 1.9 %shard_map.95 = (f32[32,1024]{1,0:T(8,128)S(1)}, f32[32,1024]{1,0:T(8,128)S(1)}, f32[4,1024]{1,0:T(4,128)S(1)}, f32[8,1024]{1,0:T(8,128)S(1)}) custom-call(bf16[32,1024]{1,0:T(8,128)(2,1)S(1)} %copy-done, f32[32,1024]{1,0:T(8,128)S(1)} %get-tuple-element.46.own, f32[8,1024]{1,0:T(8,128)S(1)} %collective-permute-done.4.message, ...), custom_call_target="tpu_custom_call" | custom-call | tf_op jit(solution)/shard_map/pallas_call | solution.py:464
  32.6 1.9 %collective-permute-start.5 = (f32[8,1024]{1,0:T(8,128)S(1)}, f32[8,1024]{1,0:T(8,128)S(1)}, u32[]{:S(2)}, u32[]{:S(2)}) collective-permute-start(f32[8,1024]{1,0:T(8,128)S(1)} %get-tuple-element.51), channel_id=1, source_target_pairs={{1,2},{3,4},{5,6},{7,8},{9,10},{11,12},{13,14},{15,16},{17,18},{19... | collective-permute-start | bytes 98312 | tf_op jit(solution)/shard_map/ppermute | solution.py:405
  34.5 0.7 shard_map.96
  35.2 2.6 %collective-permute-done.5.message = f32[8,1024]{1,0:T(8,128)S(1)} collective-permute-done((f32[8,1024]{1,0:T(8,128)S(1)}, f32[8,1024]{1,0:T(8,128)S(1)}, u32[]{:S(2)}, u32[]{:S(2)}) %collective-permute-start.5) | collective-permute-done | bytes 32800 | tf_op jit(solution)/shard_map/ppermute | solution.py:405
  37.8 0.5 shard_map.97
  38.3 1.9 %collective-permute-start.6 = (f32[4,1024]{1,0:T(4,128)S(1)}, f32[4,1024]{1,0:T(4,128)S(1)}, u32[]{:S(2)}, u32[]{:S(2)}) collective-permute-start(f32[4,1024]{1,0:T(4,128)S(1)} %get-tuple-element.59), channel_id=1, source_target_pairs={{0,1},{2,3},{4,5},{6,7},{8,9},{10,11},{12,13},{14,15},{16,17},{18,... | collective-permute-start | bytes 49160 | tf_op jit(solution)/shard_map/ppermute | solution.py:405
  40.2 1.1 %shard_map.98 = (f32[32,1024]{1,0:T(8,128)S(1)}, bf16[16,2048]{1,0:T(8,128)(2,1)S(1)}, bf16[16,2048]{1,0:T(8,128)(2,1)S(1)}) custom-call(bf16[32,1024]{1,0:T(8,128)(2,1)S(1)} %copy-done, f32[32,1024]{1,0:T(8,128)S(1)} %get-tuple-element.56.vector, bf16[2048,256]{1,0:T(8,128)(2,1)S(1)} %get-tuple-element.36.block_parts, ...), custom_call_target="tpu_custom_call" | custom-call | tf_op jit(solution)/shard_map/pallas_call | solution.py:479
  41.3 0.1 collective-permute-done.6.from_pair
  41.4 0.9 shard_map.99
  42.3 0.1 broadcast_in_dim.14
  42.4 29.2 %all_to_all.10 = f32[32,16,128]{2,1,0:T(8,128)S(1)} all-to-all(f32[32,16,128]{2,1,0:T(8,128)S(1)} %bitcast.5), channel_id=1, replica_groups=mesh['outer'=4,'inner'=16,'narrow'=8] {'outer','narrow'}, dimensions={0} | all-to-all | bytes 524288 | tf_op jit(solution)/shard_map/all_to_all | solution.py:491
  71.7 16.7 %all_to_all.11 = f32[16,16,128]{2,1,0:T(8,128)S(1)} all-to-all(f32[16,16,128]{2,1,0:T(8,128)S(1)} %broadcast_in_dim.15), channel_id=1, replica_groups=mesh['outer'=4,'inner'=16,'narrow'=8] {'inner'}, dimensions={0} | all-to-all | bytes 262144 | tf_op jit(solution)/shard_map/all_to_all | solution.py:493
  88.3 4.9 %collective-permute-start.7 = (f32[16,128]{1,0:T(8,128)S(1)}, f32[16,128]{1,0:T(8,128)S(1)}, u32[]{:S(2)}, u32[]{:S(2)}) collective-permute-start(f32[16,128]{1,0:T(8,128)S(1)} %reduce_sum.19.mine), channel_id=1, source_target_pairs={{0,1},{2,3},{4,5},{6,7},{8,9},{10,11},{12,13},{14,15},{16,17},{18,... | collective-permute-start | bytes 24584 | tf_op jit(solution)/shard_map/ppermute | solution.py:405
  93.2 0.8 collective-permute-done.7.theirs
  94.0 2.8 %shard_map.100 = (f32[32,1024]{1,0:T(8,128)}, f32[32,1024]{1,0:T(8,128)}) custom-call(f32[16,128]{1,0:T(8,128)S(1)} %reduce_sum.19.mine, f32[16,128]{1,0:T(8,128)S(1)} %collective-permute-done.7.theirs, bf16[48,2048]{1,0:T(8,128)(2,1)S(1)} %get-tuple-element.60.high, bf16[48,2048]{1,0:T(8,128)(2,1)S(1)} %get-tuple-element.61.low, ...), custom_call_target="tpu_custom_call" | custom-call | tf_op jit(solution)/shard_map/pallas_call | solution.py:496
  (3 shorter events, 0.1 us)
Async XLA Ops:
  2.4 13.9 %collective-permute-start = (f32[8,1024]{1,0:T(8,128)}, f32[8,1024]{1,0:T(8,128)S(1)}, u32[]{:S(2)}, u32[]{:S(2)}) collective-permute-start(f32[8,1024]{1,0:T(8,128)} %get-tuple-element.38), channel_id=1, source_target_pairs={{1,2},{3,4},{5,6},{7,8},{9,10},{11,12},{13,14},{15,16},{17,18},{19... | collective-permute-start | bytes 98312 | tf_op jit(solution)/shard_map/ppermute | solution.py:405
  6.9 8.3 %copy-start = (bf16[32,1024]{1,0:T(8,128)(2,1)S(1)}, bf16[32,1024]{1,0:T(8,128)(2,1)}, u32[]{:S(2)}) copy-start(bf16[32,1024]{1,0:T(8,128)(2,1)} %get-tuple-element.35.choose) | copy-start | bytes 196612
  6.9 8.3 %copy-start.1 = (f32[32,1024]{1,0:T(8,128)S(1)}, f32[32,1024]{1,0:T(8,128)}, u32[]{:S(2)}) copy-start(f32[32,1024]{1,0:T(8,128)} %guess.3) | copy-start | bytes 393220
  6.9 9.4 %collective-permute-start.1 = (f32[8,1024]{1,0:T(8,128)}, f32[8,1024]{1,0:T(8,128)S(1)}, u32[]{:S(2)}, u32[]{:S(2)}) collective-permute-start(f32[8,1024]{1,0:T(8,128)} %get-tuple-element.39), channel_id=1, source_target_pairs={{0,1},{2,3},{4,5},{6,7},{8,9},{10,11},{12,13},{14,15},{16,17},{18,... | collective-permute-start | bytes 98312 | tf_op jit(solution)/shard_map/ppermute | solution.py:405
  12.0 1.0 %copy-start.2 = (f32[32,4096]{1,0:T(8,128)S(1)}, f32[32,4096]{1,0:T(8,128)}, u32[]{:S(2)}) copy-start(f32[32,4096]{1,0:T(8,128)} %blocks.1) | copy-start | bytes 1572868
  13.1 0.9 copy-start.3
  15.2 1.1 %copy-start.4 = (f32[32,1024]{1,0:T(8,128)S(1)}, f32[32,1024]{1,0:T(8,128)}, u32[]{:S(2)}) copy-start(f32[32,1024]{1,0:T(8,128)} %right.1) | copy-start | bytes 393220
  16.9 3.1 %collective-permute-start.2 = (f32[4,1024]{1,0:T(4,128)S(1)}, f32[4,1024]{1,0:T(4,128)S(1)}, u32[]{:S(2)}, u32[]{:S(2)}) collective-permute-start(f32[4,1024]{1,0:T(4,128)S(1)} %get-tuple-element.41), channel_id=1, source_target_pairs={{0,1},{2,3},{4,5},{6,7},{8,9},{10,11},{12,13},{14,15},{16,17},{18,... | collective-permute-start | bytes 49160 | tf_op jit(solution)/shard_map/ppermute | solution.py:405
  20.5 5.2 %collective-permute-start.3 = (f32[8,1024]{1,0:T(8,128)S(1)}, f32[8,1024]{1,0:T(8,128)S(1)}, u32[]{:S(2)}, u32[]{:S(2)}) collective-permute-start(f32[8,1024]{1,0:T(8,128)S(1)} %get-tuple-element.44), channel_id=1, source_target_pairs={{1,2},{3,4},{5,6},{7,8},{9,10},{11,12},{13,14},{15,16},{17,18},{19... | collective-permute-start | bytes 98312 | tf_op jit(solution)/shard_map/ppermute | solution.py:405
  27.6 3.1 %collective-permute-start.4 = (f32[8,1024]{1,0:T(8,128)S(1)}, f32[8,1024]{1,0:T(8,128)S(1)}, u32[]{:S(2)}, u32[]{:S(2)}) collective-permute-start(f32[8,1024]{1,0:T(8,128)S(1)} %get-tuple-element.47), channel_id=1, source_target_pairs={{0,1},{2,3},{4,5},{6,7},{8,9},{10,11},{12,13},{14,15},{16,17},{18,... | collective-permute-start | bytes 98312 | tf_op jit(solution)/shard_map/ppermute | solution.py:405
  32.6 5.2 %collective-permute-start.5 = (f32[8,1024]{1,0:T(8,128)S(1)}, f32[8,1024]{1,0:T(8,128)S(1)}, u32[]{:S(2)}, u32[]{:S(2)}) collective-permute-start(f32[8,1024]{1,0:T(8,128)S(1)} %get-tuple-element.51), channel_id=1, source_target_pairs={{1,2},{3,4},{5,6},{7,8},{9,10},{11,12},{13,14},{15,16},{17,18},{19... | collective-permute-start | bytes 98312 | tf_op jit(solution)/shard_map/ppermute | solution.py:405
  38.3 3.1 %collective-permute-start.6 = (f32[4,1024]{1,0:T(4,128)S(1)}, f32[4,1024]{1,0:T(4,128)S(1)}, u32[]{:S(2)}, u32[]{:S(2)}) collective-permute-start(f32[4,1024]{1,0:T(4,128)S(1)} %get-tuple-element.59), channel_id=1, source_target_pairs={{0,1},{2,3},{4,5},{6,7},{8,9},{10,11},{12,13},{14,15},{16,17},{18,... | collective-permute-start | bytes 49160 | tf_op jit(solution)/shard_map/ppermute | solution.py:405
  88.3 5.7 %collective-permute-start.7 = (f32[16,128]{1,0:T(8,128)S(1)}, f32[16,128]{1,0:T(8,128)S(1)}, u32[]{:S(2)}, u32[]{:S(2)}) collective-permute-start(f32[16,128]{1,0:T(8,128)S(1)} %reduce_sum.19.mine), channel_id=1, source_target_pairs={{0,1},{2,3},{4,5},{6,7},{8,9},{10,11},{12,13},{14,15},{16,17},{18,... | collective-permute-start | bytes 24584 | tf_op jit(solution)/shard_map/ppermute | solution.py:405

commit v6 on v5

--- a/solution.py
+++ b/solution.py
@@ -98,13 +98,21 @@
     choose[:, SEND[0] : SEND[1]] = jnp.concatenate([rows, rows, rows], 0).T.astype(BF16)
 
 
-def prep_kernel(blocks, lift, block_parts, lift_parts, spread_blocks):
+def prep_kernel(blocks_in, lift_in, block_parts, lift_parts, blocks, lift, spread_blocks, done):
+    copies = [
+        pltpu.make_async_copy(lift_in, lift, done.at[0]),
+        pltpu.make_async_copy(blocks_in, blocks, done.at[1]),
+    ]
+    for copy in copies:
+        copy.start()
+    copies[0].wait()
     for f in range(FACES):
         upper = jnp.concatenate([lift[f], jnp.zeros((NODES, NODES), F32)], 1)
         high, low = split(jnp.concatenate([upper, swap(upper)], 0).T)
         lift_parts[:128, slab(f)] = high
         lift_parts[128:256, slab(f)] = high
         lift_parts[256:, slab(f)] = low
+    copies[1].wait()
     mask = left_half((ELEMS, 128))
     for pair in range(NODES // 2):
         two = blocks[:, pair * 128 : pair * 128 + 128]
@@ -400,6 +408,10 @@
     )
 
 
+def in_hbm(array):
+    return pltpu.with_memory_space_constraint(array, pltpu.HBM)
+
+
 def swapped(block, axes, first):
     lower = range(first, lax.axis_size(axes) - 1, 2)
     return lax.ppermute(block, axes, [(i, i + 1) for i in lower] + [(i + 1, i) for i in lower])
@@ -421,8 +433,7 @@
             pltpu.SemaphoreType.DMA((5,)),
         ],
         [HBM] * 4,
-        60 * 1024,
-    )(ghost_send, start_guess, neighbors.T, face_scale.T)
+    )(*map(in_hbm, (ghost_send, start_guess, neighbors.T, face_scale.T)))
     from_other = swapped(to_other, axes, 1)
     from_pair = swapped(to_pair, axes, 0)
     block_parts, lift_parts = call(
@@ -431,9 +442,14 @@
             jax.ShapeDtypeStruct((ELEMS * NODES, 256), BF16),
             jax.ShapeDtypeStruct((384, FACES * 128), BF16),
         ],
-        [pltpu.VMEM((ELEMS, NODES, 128), F32)],
-        [VMEM] * 2,
-    )(block_diag, face_lift)
+        [
+            pltpu.VMEM((ELEMS, NODES * NODES), F32),
+            pltpu.VMEM((FACES, NODES, NODES), F32),
+            pltpu.VMEM((ELEMS, NODES, 128), F32),
+            pltpu.SemaphoreType.DMA((2,)),
+        ],
+        [HBM] * 2,
+    )(in_hbm(block_diag), in_hbm(face_lift))
     tile_scratch = pltpu.VMEM((ELEMS, 8, 128), F32)
     own_call = lambda *args: call(
         first_own_kernel, [FIELD], [tile_scratch] * 2, [VMEM] * 4

time: 97.3 us -> 95.6 us (0.983)
  local copies, waits for them, and re-layouts: 2.07 us -> 0.1 us
    unnamed x10 -> x4, local copies, waits for them, and re-layouts: 1.98 us -> 0.01 us
    pallas_call x1, Pallas kernels: 1.18 us -> 2.2 us  [local(): call(prep_kernel, [jax.ShapeDtypeStruct((ELEMS * NODES, 256), BF16), jax....]
  transfers between devices with their start and end apart: 8 -> 8, of which waited for: 6 -> 6; matrix products, arithmetic and copies ran while one was open for 0% -> 0% of each run, Pallas kernels for 6% -> 7%
where the time goes in v6:
time: 95.6 us; the launch traced here: 95.2 us
  blocking collectives  45.9 us (48%)
  starting transfers between devices  24 us (25%)
  Pallas kernels  17.1 us (18%)
  waiting for transfers between devices  7.22 us (8%)
    all_to_all x1, blocking collectives, local(): mine = lax.all_to_all(halves, (axes[0], axes[2]), 0, 0).sum(0)  29.2 us
    ppermute x8, starting transfers between devices, swapped(): lax.ppermute(block, axes, [(i, i + 1) for i in lower] + [(i + 1, i) for i...  24 us
    all_to_all x1, blocking collectives, local(): mine = lax.all_to_all(mine, axes[1], 0, 0).sum(0)  16.6 us
    ppermute x8, waiting for transfers between devices, swapped(): lax.ppermute(block, axes, [(i, i + 1) for i in lower] + [(i + 1, i) for i...  7.22 us
    pallas_call x1, Pallas kernels, local(): call(solve_kernel, [FIELD, FIELD], [pltpu.VMEM((128, 128), F32), pltpu.VM...  2.8 us
    pallas_call x1, Pallas kernels, local(): call(prep_kernel, [jax.ShapeDtypeStruct((ELEMS * NODES, 256), BF16), jax....  2.2 us
    pallas_call x2, Pallas kernels, local(): call(first_own_kernel, [FIELD], [tile_scratch] * 2, [VMEM] * 4)(*args)[0]  2.15 us
  transfers between devices with their start and end apart: 8, of which 6 were waited for; matrix products, arithmetic and copies ran while one was open for 0% of the time, Pallas kernels for 7%

profile of v6, /device:TPU:1, one launch (start us, length us, event | category | flops | bytes accessed | tf_op | source)
XLA Modules:
  0.0 95.2 jit_solution(9303688671985919912)
XLA Ops:
  0.6 1.1 %shard_map.86 = (f32[8,1024]{1,0:T(8,128)S(1)}, f32[8,1024]{1,0:T(8,128)S(1)}, bf16[32,1024]{1,0:T(8,128)(2,1)S(1)}) custom-call(s32[1,8]{1,0:T(1,128)} %send_in.1, f32[32,1024]{1,0:T(8,128)} %guess.3, s32[6,32]{1,0:T(8,128)} %bitcast.6, f32[6,32]{1,0:T(8,128)} %bitcast.7), custom_call_target="tpu_custom_call" | custom-call | tf_op jit(solution)/shard_map/pallas_call | solution.py:423
  1.8 4.5 %collective-permute-start = (f32[8,1024]{1,0:T(8,128)S(1)}, f32[8,1024]{1,0:T(8,128)S(1)}, u32[]{:S(2)}, u32[]{:S(2)}) collective-permute-start(f32[8,1024]{1,0:T(8,128)S(1)} %get-tuple-element.38), channel_id=1, source_target_pairs={{1,2},{3,4},{5,6},{7,8},{9,10},{11,12},{13,14},{15,16},{17,18},{19... | collective-permute-start | bytes 98312 | tf_op jit(solution)/shard_map/ppermute | solution.py:417
  6.3 0.0 copy-start
  6.3 5.1 %collective-permute-start.1 = (f32[8,1024]{1,0:T(8,128)S(1)}, f32[8,1024]{1,0:T(8,128)S(1)}, u32[]{:S(2)}, u32[]{:S(2)}) collective-permute-start(f32[8,1024]{1,0:T(8,128)S(1)} %get-tuple-element.39), channel_id=1, source_target_pairs={{0,1},{2,3},{4,5},{6,7},{8,9},{10,11},{12,13},{14,15},{16,17},{18,... | collective-permute-start | bytes 98312 | tf_op jit(solution)/shard_map/ppermute | solution.py:417
  11.4 2.2 %shard_map.87 = (bf16[2048,256]{1,0:T(8,128)(2,1)S(1)}, bf16[384,768]{1,0:T(8,128)(2,1)S(1)}) custom-call(f32[32,4096]{1,0:T(8,128)} %blocks_in.1, f32[6,64,64]{2,1,0:T(8,128)} %lift_in.1), custom_call_target="tpu_custom_call" | custom-call | tf_op jit(solution)/shard_map/pallas_call | solution.py:439
  13.6 0.0 copy-done
  13.6 0.0 copy-start.1
  13.6 1.1 %shard_map.88.own = f32[32,1024]{1,0:T(8,128)S(1)} custom-call(bf16[32,1024]{1,0:T(8,128)(2,1)S(1)} %get-tuple-element.35.choose, f32[32,1024]{1,0:T(8,128)S(1)} %copy-done, bf16[2048,256]{1,0:T(8,128)(2,1)S(1)} %get-tuple-element.36.block_parts, bf16[384,768]{1,0:T(8,128)(2,1)S(1)} %get-tuple-element.37.lift_parts), custom_call_target="tpu_custom_call" | custom-call | tf_op jit(solution)/shard_map/pallas_call | solution.py:454
  14.7 0.0 collective-permute-done.from_other
  14.7 0.0 collective-permute-done.1.from_pair
  14.7 0.0 copy-done.1
  14.7 0.5 shard_map.89
  15.2 1.9 %collective-permute-start.2 = (f32[4,1024]{1,0:T(4,128)S(1)}, f32[4,1024]{1,0:T(4,128)S(1)}, u32[]{:S(2)}, u32[]{:S(2)}) collective-permute-start(f32[4,1024]{1,0:T(4,128)S(1)} %get-tuple-element.41), channel_id=1, source_target_pairs={{0,1},{2,3},{4,5},{6,7},{8,9},{10,11},{12,13},{14,15},{16,17},{18,... | collective-permute-start | bytes 49160 | tf_op jit(solution)/shard_map/ppermute | solution.py:417
  17.2 1.1 %shard_map.90.own = f32[32,1024]{1,0:T(8,128)S(1)} custom-call(bf16[32,1024]{1,0:T(8,128)(2,1)S(1)} %get-tuple-element.35.choose, f32[32,1024]{1,0:T(8,128)S(1)} %get-tuple-element.40.vector.first, bf16[2048,256]{1,0:T(8,128)(2,1)S(1)} %get-tuple-element.36.block_parts, bf16[384,768]{1,0:T(8,128)(2,1)S(1)} %get-tuple-element.37.lift_parts), custom_call_target="tpu_custom_call" | custom-call | tf_op jit(solution)/shard_map/pallas_call | solution.py:454
  18.2 0.1 collective-permute-done.2.from_pair
  18.3 0.5 shard_map.91
  18.9 1.9 %collective-permute-start.3 = (f32[8,1024]{1,0:T(8,128)S(1)}, f32[8,1024]{1,0:T(8,128)S(1)}, u32[]{:S(2)}, u32[]{:S(2)}) collective-permute-start(f32[8,1024]{1,0:T(8,128)S(1)} %get-tuple-element.44), channel_id=1, source_target_pairs={{1,2},{3,4},{5,6},{7,8},{9,10},{11,12},{13,14},{15,16},{17,18},{19... | collective-permute-start | bytes 98312 | tf_op jit(solution)/shard_map/ppermute | solution.py:417
  20.8 0.4 shard_map.92.missing
  21.2 2.9 %collective-permute-done.3.message = f32[8,1024]{1,0:T(8,128)S(1)} collective-permute-done((f32[8,1024]{1,0:T(8,128)S(1)}, f32[8,1024]{1,0:T(8,128)S(1)}, u32[]{:S(2)}, u32[]{:S(2)}) %collective-permute-start.3) | collective-permute-done | bytes 32800 | tf_op jit(solution)/shard_map/ppermute | solution.py:417
  24.1 1.9 %shard_map.93 = (f32[32,1024]{1,0:T(8,128)S(1)}, f32[32,1024]{1,0:T(8,128)S(1)}, f32[4,1024]{1,0:T(4,128)S(1)}, f32[8,1024]{1,0:T(8,128)S(1)}) custom-call(bf16[32,1024]{1,0:T(8,128)(2,1)S(1)} %get-tuple-element.35.choose, f32[32,1024]{1,0:T(8,128)S(1)} %get-tuple-element.43.partial, f32[8,1024]{1,0:T(8,128)S(1)} %collective-permute-done.3.message, ...), custom_call_target="tpu_custom_call" | custom-call | tf_op jit(solution)/shard_map/pallas_call | solution.py:474
  26.0 1.9 %collective-permute-start.4 = (f32[8,1024]{1,0:T(8,128)S(1)}, f32[8,1024]{1,0:T(8,128)S(1)}, u32[]{:S(2)}, u32[]{:S(2)}) collective-permute-start(f32[8,1024]{1,0:T(8,128)S(1)} %get-tuple-element.47), channel_id=1, source_target_pairs={{0,1},{2,3},{4,5},{6,7},{8,9},{10,11},{12,13},{14,15},{16,17},{18,... | collective-permute-start | bytes 98312 | tf_op jit(solution)/shard_map/ppermute | solution.py:417
  27.9 0.4 shard_map.94.missing
  28.3 0.8 collective-permute-done.4.message
  29.1 1.9 %shard_map.95 = (f32[32,1024]{1,0:T(8,128)S(1)}, f32[32,1024]{1,0:T(8,128)S(1)}, f32[4,1024]{1,0:T(4,128)S(1)}, f32[8,1024]{1,0:T(8,128)S(1)}) custom-call(bf16[32,1024]{1,0:T(8,128)(2,1)S(1)} %get-tuple-element.35.choose, f32[32,1024]{1,0:T(8,128)S(1)} %get-tuple-element.46.own, f32[8,1024]{1,0:T(8,128)S(1)} %collective-permute-done.4.message, ...), custom_call_target="tpu_custom_call" | custom-call | tf_op jit(solution)/shard_map/pallas_call | solution.py:480
  30.9 1.9 %collective-permute-start.5 = (f32[8,1024]{1,0:T(8,128)S(1)}, f32[8,1024]{1,0:T(8,128)S(1)}, u32[]{:S(2)}, u32[]{:S(2)}) collective-permute-start(f32[8,1024]{1,0:T(8,128)S(1)} %get-tuple-element.51), channel_id=1, source_target_pairs={{1,2},{3,4},{5,6},{7,8},{9,10},{11,12},{13,14},{15,16},{17,18},{19... | collective-permute-start | bytes 98312 | tf_op jit(solution)/shard_map/ppermute | solution.py:417
  32.9 0.7 shard_map.96
  33.6 2.6 %collective-permute-done.5.message = f32[8,1024]{1,0:T(8,128)S(1)} collective-permute-done((f32[8,1024]{1,0:T(8,128)S(1)}, f32[8,1024]{1,0:T(8,128)S(1)}, u32[]{:S(2)}, u32[]{:S(2)}) %collective-permute-start.5) | collective-permute-done | bytes 32800 | tf_op jit(solution)/shard_map/ppermute | solution.py:417
  36.2 0.5 shard_map.97
  36.7 1.9 %collective-permute-start.6 = (f32[4,1024]{1,0:T(4,128)S(1)}, f32[4,1024]{1,0:T(4,128)S(1)}, u32[]{:S(2)}, u32[]{:S(2)}) collective-permute-start(f32[4,1024]{1,0:T(4,128)S(1)} %get-tuple-element.59), channel_id=1, source_target_pairs={{0,1},{2,3},{4,5},{6,7},{8,9},{10,11},{12,13},{14,15},{16,17},{18,... | collective-permute-start | bytes 49160 | tf_op jit(solution)/shard_map/ppermute | solution.py:417
  38.6 1.1 %shard_map.98 = (f32[32,1024]{1,0:T(8,128)S(1)}, bf16[16,2048]{1,0:T(8,128)(2,1)S(1)}, bf16[16,2048]{1,0:T(8,128)(2,1)S(1)}) custom-call(bf16[32,1024]{1,0:T(8,128)(2,1)S(1)} %get-tuple-element.35.choose, f32[32,1024]{1,0:T(8,128)S(1)} %get-tuple-element.56.vector, bf16[2048,256]{1,0:T(8,128)(2,1)S(1)} %get-tuple-element.36.block_parts, ...), custom_call_target="tpu_custom_call" | custom-call | tf_op jit(solution)/shard_map/pallas_call | solution.py:495
  39.7 0.1 collective-permute-done.6.from_pair
  39.8 0.9 shard_map.99
  40.7 0.1 broadcast_in_dim.14
  40.8 29.2 %all_to_all.10 = f32[32,16,128]{2,1,0:T(8,128)S(1)} all-to-all(f32[32,16,128]{2,1,0:T(8,128)S(1)} %bitcast.5), channel_id=1, replica_groups=mesh['outer'=4,'inner'=16,'narrow'=8] {'outer','narrow'}, dimensions={0} | all-to-all | bytes 524288 | tf_op jit(solution)/shard_map/all_to_all | solution.py:507
  70.1 16.6 %all_to_all.11 = f32[16,16,128]{2,1,0:T(8,128)S(1)} all-to-all(f32[16,16,128]{2,1,0:T(8,128)S(1)} %broadcast_in_dim.15), channel_id=1, replica_groups=mesh['outer'=4,'inner'=16,'narrow'=8] {'inner'}, dimensions={0} | all-to-all | bytes 262144 | tf_op jit(solution)/shard_map/all_to_all | solution.py:509
  86.7 4.9 %collective-permute-start.7 = (f32[16,128]{1,0:T(8,128)S(1)}, f32[16,128]{1,0:T(8,128)S(1)}, u32[]{:S(2)}, u32[]{:S(2)}) collective-permute-start(f32[16,128]{1,0:T(8,128)S(1)} %reduce_sum.19.mine), channel_id=1, source_target_pairs={{0,1},{2,3},{4,5},{6,7},{8,9},{10,11},{12,13},{14,15},{16,17},{18,... | collective-permute-start | bytes 24584 | tf_op jit(solution)/shard_map/ppermute | solution.py:417
  91.6 0.8 collective-permute-done.7.theirs
  92.4 2.8 %shard_map.100 = (f32[32,1024]{1,0:T(8,128)}, f32[32,1024]{1,0:T(8,128)}) custom-call(f32[16,128]{1,0:T(8,128)S(1)} %reduce_sum.19.mine, f32[16,128]{1,0:T(8,128)S(1)} %collective-permute-done.7.theirs, bf16[48,2048]{1,0:T(8,128)(2,1)S(1)} %get-tuple-element.60.high, bf16[48,2048]{1,0:T(8,128)(2,1)S(1)} %get-tuple-element.61.low, ...), custom_call_target="tpu_custom_call" | custom-call | tf_op jit(solution)/shard_map/pallas_call | solution.py:512
  (3 shorter events, 0.1 us)
Async XLA Ops:
  1.8 12.9 %collective-permute-start = (f32[8,1024]{1,0:T(8,128)S(1)}, f32[8,1024]{1,0:T(8,128)S(1)}, u32[]{:S(2)}, u32[]{:S(2)}) collective-permute-start(f32[8,1024]{1,0:T(8,128)S(1)} %get-tuple-element.38), channel_id=1, source_target_pairs={{1,2},{3,4},{5,6},{7,8},{9,10},{11,12},{13,14},{15,16},{17,18},{19... | collective-permute-start | bytes 98312 | tf_op jit(solution)/shard_map/ppermute | solution.py:417
  6.3 7.3 %copy-start = (f32[32,1024]{1,0:T(8,128)S(1)}, f32[32,1024]{1,0:T(8,128)}, u32[]{:S(2)}) copy-start(f32[32,1024]{1,0:T(8,128)} %guess.3) | copy-start | bytes 393220
  6.3 8.4 %collective-permute-start.1 = (f32[8,1024]{1,0:T(8,128)S(1)}, f32[8,1024]{1,0:T(8,128)S(1)}, u32[]{:S(2)}, u32[]{:S(2)}) collective-permute-start(f32[8,1024]{1,0:T(8,128)S(1)} %get-tuple-element.39), channel_id=1, source_target_pairs={{0,1},{2,3},{4,5},{6,7},{8,9},{10,11},{12,13},{14,15},{16,17},{18,... | collective-permute-start | bytes 98312 | tf_op jit(solution)/shard_map/ppermute | solution.py:417
  13.6 1.1 %copy-start.1 = (f32[32,1024]{1,0:T(8,128)S(1)}, f32[32,1024]{1,0:T(8,128)}, u32[]{:S(2)}) copy-start(f32[32,1024]{1,0:T(8,128)} %right.1) | copy-start | bytes 393220
  15.2 3.1 %collective-permute-start.2 = (f32[4,1024]{1,0:T(4,128)S(1)}, f32[4,1024]{1,0:T(4,128)S(1)}, u32[]{:S(2)}, u32[]{:S(2)}) collective-permute-start(f32[4,1024]{1,0:T(4,128)S(1)} %get-tuple-element.41), channel_id=1, source_target_pairs={{0,1},{2,3},{4,5},{6,7},{8,9},{10,11},{12,13},{14,15},{16,17},{18,... | collective-permute-start | bytes 49160 | tf_op jit(solution)/shard_map/ppermute | solution.py:417
  18.9 5.2 %collective-permute-start.3 = (f32[8,1024]{1,0:T(8,128)S(1)}, f32[8,1024]{1,0:T(8,128)S(1)}, u32[]{:S(2)}, u32[]{:S(2)}) collective-permute-start(f32[8,1024]{1,0:T(8,128)S(1)} %get-tuple-element.44), channel_id=1, source_target_pairs={{1,2},{3,4},{5,6},{7,8},{9,10},{11,12},{13,14},{15,16},{17,18},{19... | collective-permute-start | bytes 98312 | tf_op jit(solution)/shard_map/ppermute | solution.py:417
  26.0 3.1 %collective-permute-start.4 = (f32[8,1024]{1,0:T(8,128)S(1)}, f32[8,1024]{1,0:T(8,128)S(1)}, u32[]{:S(2)}, u32[]{:S(2)}) collective-permute-start(f32[8,1024]{1,0:T(8,128)S(1)} %get-tuple-element.47), channel_id=1, source_target_pairs={{0,1},{2,3},{4,5},{6,7},{8,9},{10,11},{12,13},{14,15},{16,17},{18,... | collective-permute-start | bytes 98312 | tf_op jit(solution)/shard_map/ppermute | solution.py:417
  30.9 5.2 %collective-permute-start.5 = (f32[8,1024]{1,0:T(8,128)S(1)}, f32[8,1024]{1,0:T(8,128)S(1)}, u32[]{:S(2)}, u32[]{:S(2)}) collective-permute-start(f32[8,1024]{1,0:T(8,128)S(1)} %get-tuple-element.51), channel_id=1, source_target_pairs={{1,2},{3,4},{5,6},{7,8},{9,10},{11,12},{13,14},{15,16},{17,18},{19... | collective-permute-start | bytes 98312 | tf_op jit(solution)/shard_map/ppermute | solution.py:417
  36.7 3.1 %collective-permute-start.6 = (f32[4,1024]{1,0:T(4,128)S(1)}, f32[4,1024]{1,0:T(4,128)S(1)}, u32[]{:S(2)}, u32[]{:S(2)}) collective-permute-start(f32[4,1024]{1,0:T(4,128)S(1)} %get-tuple-element.59), channel_id=1, source_target_pairs={{0,1},{2,3},{4,5},{6,7},{8,9},{10,11},{12,13},{14,15},{16,17},{18,... | collective-permute-start | bytes 49160 | tf_op jit(solution)/shard_map/ppermute | solution.py:417
  86.7 5.7 %collective-permute-start.7 = (f32[16,128]{1,0:T(8,128)S(1)}, f32[16,128]{1,0:T(8,128)S(1)}, u32[]{:S(2)}, u32[]{:S(2)}) collective-permute-start(f32[16,128]{1,0:T(8,128)S(1)} %reduce_sum.19.mine), channel_id=1, source_target_pairs={{0,1},{2,3},{4,5},{6,7},{8,9},{10,11},{12,13},{14,15},{16,17},{18,... | collective-permute-start | bytes 24584 | tf_op jit(solution)/shard_map/ppermute | solution.py:417

commit v7 on v6

--- a/solution.py
+++ b/solution.py
@@ -119,11 +119,10 @@
         turned = swap(two)
         spread_blocks[:, 2 * pair, :] = jnp.where(mask, two, turned)
         spread_blocks[:, 2 * pair + 1, :] = jnp.where(mask, turned, two)
-    for element in range(ELEMS):
-        high, low = split(spread_blocks[element])
-        rows = slice(element * NODES, (element + 1) * NODES)
-        block_parts[rows, :128] = high
-        block_parts[rows, 128:] = low
+    for pair in range(ELEMS // 2):
+        high, low = split(spread_blocks[2 * pair : 2 * pair + 2].reshape(128, 128).T)
+        block_parts[:128, slab(pair)] = high
+        block_parts[128:, slab(pair)] = low
 
 
 def face_sum(vector, lift_parts, chosen):
@@ -170,12 +169,14 @@
 
 
 def own_part(vector, block_parts, lift_parts, choose, out, tiled, product):
+    faces = face_sum(vector[...], lift_parts, choose[:, OWN[0] : OWN[1]])
     to_tiles(vector, tiled)
     value = tiled[...].reshape(ELEMS * 8, 128)
     mask = left_half((ELEMS * 8, 128))
     high, low = split(value)
     high, low = high.astype(F32), low.astype(F32)
-    turned_high, turned_low = swap(high), swap(low)
+    turned_high, turned_low = split(swap(value))
+    turned_high, turned_low = turned_high.astype(F32), turned_low.astype(F32)
     first = jnp.where(mask, low, turned_high).astype(BF16)
     second = jnp.where(mask, turned_low, high).astype(BF16)
     first_rest = jnp.where(mask, high, 0.0).astype(BF16)
@@ -186,7 +187,8 @@
     for group in range(ELEMS // 4):
         rows = slice(group * 32, (group + 1) * 32)
         both = jnp.concatenate([first[rows], second[rows]], 0)
-        result = dot_nt(both, block_parts[group * 256 : (group + 1) * 256, :])
+        columns = block_parts[:, group * 256 : (group + 1) * 256]
+        result = jnp.dot(both, columns, preferred_element_type=F32)
         for part in range(4):
             lanes = slab(part // 2)
             top = result[part * 8 : part * 8 + 8, lanes]
@@ -195,14 +197,14 @@
                 product[group * 4 + part] = jnp.where(mask, top, swap(bottom))
             else:
                 product[group * 4 + part] = jnp.where(mask, swap(top), bottom)
-    faces = face_sum(vector[...], lift_parts, choose[:, OWN[0] : OWN[1]])
     for t in range(8):
         out[:, slab(t)] = faces[:, slab(t)] + product[:, t, :]
 
 
 def gram_of(left_high, left_low, high, low):
-    left = jnp.concatenate([left_high, left_high, left_low], 1)
-    return dot_nt(left, jnp.concatenate([high, low, high], 1))
+    count = left_high.shape[0]
+    both = dot_nt(jnp.concatenate([left_high, left_low], 0), high)
+    return both[:count] + both[count:] + dot_nt(left_high, low)
 
 
 def first_own_kernel(choose, vector, block_parts, lift_parts, out, tiled, product):
@@ -439,7 +441,7 @@
     block_parts, lift_parts = call(
         prep_kernel,
         [
-            jax.ShapeDtypeStruct((ELEMS * NODES, 256), BF16),
+            jax.ShapeDtypeStruct((256, ELEMS * NODES), BF16),
             jax.ShapeDtypeStruct((384, FACES * 128), BF16),
         ],
         [

time: 95.6 us -> 95 us (level)
  no operation moved by 1% of the time
where the time goes in v7:
time: 95 us; the launch traced here: 94.6 us
  blocking collectives  45.9 us (48%)
  starting transfers between devices  24.1 us (25%)
  Pallas kernels  16.6 us (17%)
  waiting for transfers between devices  7.18 us (8%)
    all_to_all x1, blocking collectives, local(): mine = lax.all_to_all(halves, (axes[0], axes[2]), 0, 0).sum(0)  29.2 us
    ppermute x8, starting transfers between devices, swapped(): lax.ppermute(block, axes, [(i, i + 1) for i in lower] + [(i + 1, i) for i...  24.1 us
    all_to_all x1, blocking collectives, local(): mine = lax.all_to_all(mine, axes[1], 0, 0).sum(0)  16.6 us
    ppermute x8, waiting for transfers between devices, swapped(): lax.ppermute(block, axes, [(i, i + 1) for i in lower] + [(i + 1, i) for i...  7.18 us
    pallas_call x1, Pallas kernels, local(): call(solve_kernel, [FIELD, FIELD], [pltpu.VMEM((128, 128), F32), pltpu.VM...  2.8 us
    pallas_call x1, Pallas kernels, local(): call(prep_kernel, [jax.ShapeDtypeStruct((256, ELEMS * NODES), BF16), jax....  2.16 us
    pallas_call x2, Pallas kernels, local(): call(first_own_kernel, [FIELD], [tile_scratch] * 2, [VMEM] * 4)(*args)[0]  2.12 us
  transfers between devices with their start and end apart: 8, of which 6 were waited for; matrix products, arithmetic and copies ran while one was open for 0% of the time, Pallas kernels for 7%

profile of v7, /device:TPU:1, one launch (start us, length us, event | category | flops | bytes accessed | tf_op | source)
XLA Modules:
  0.0 94.6 jit_solution(16198957701698249309)
XLA Ops:
  0.6 1.1 %shard_map.86 = (f32[8,1024]{1,0:T(8,128)S(1)}, f32[8,1024]{1,0:T(8,128)S(1)}, bf16[32,1024]{1,0:T(8,128)(2,1)S(1)}) custom-call(s32[1,8]{1,0:T(1,128)} %send_in.1, f32[32,1024]{1,0:T(8,128)} %guess.3, s32[6,32]{1,0:T(8,128)} %bitcast.6, f32[6,32]{1,0:T(8,128)} %bitcast.7), custom_call_target="tpu_custom_call" | custom-call | tf_op jit(solution)/shard_map/pallas_call | solution.py:425
  1.8 4.5 %collective-permute-start = (f32[8,1024]{1,0:T(8,128)S(1)}, f32[8,1024]{1,0:T(8,128)S(1)}, u32[]{:S(2)}, u32[]{:S(2)}) collective-permute-start(f32[8,1024]{1,0:T(8,128)S(1)} %get-tuple-element.38), channel_id=1, source_target_pairs={{1,2},{3,4},{5,6},{7,8},{9,10},{11,12},{13,14},{15,16},{17,18},{19... | collective-permute-start | bytes 98312 | tf_op jit(solution)/shard_map/ppermute | solution.py:419
  6.3 0.0 copy-start
  6.3 5.1 %collective-permute-start.1 = (f32[8,1024]{1,0:T(8,128)S(1)}, f32[8,1024]{1,0:T(8,128)S(1)}, u32[]{:S(2)}, u32[]{:S(2)}) collective-permute-start(f32[8,1024]{1,0:T(8,128)S(1)} %get-tuple-element.39), channel_id=1, source_target_pairs={{0,1},{2,3},{4,5},{6,7},{8,9},{10,11},{12,13},{14,15},{16,17},{18,... | collective-permute-start | bytes 98312 | tf_op jit(solution)/shard_map/ppermute | solution.py:419
  11.4 2.2 %shard_map.87 = (bf16[256,2048]{1,0:T(8,128)(2,1)S(1)}, bf16[384,768]{1,0:T(8,128)(2,1)S(1)}) custom-call(f32[32,4096]{1,0:T(8,128)} %blocks_in.1, f32[6,64,64]{2,1,0:T(8,128)} %lift_in.1), custom_call_target="tpu_custom_call" | custom-call | tf_op jit(solution)/shard_map/pallas_call | solution.py:441
  13.5 0.0 copy-done
  13.6 0.0 copy-start.1
  13.6 1.1 %shard_map.88.own = f32[32,1024]{1,0:T(8,128)S(1)} custom-call(bf16[32,1024]{1,0:T(8,128)(2,1)S(1)} %get-tuple-element.35.choose, f32[32,1024]{1,0:T(8,128)S(1)} %copy-done, bf16[256,2048]{1,0:T(8,128)(2,1)S(1)} %get-tuple-element.36.block_parts, bf16[384,768]{1,0:T(8,128)(2,1)S(1)} %get-tuple-element.37.lift_parts), custom_call_target="tpu_custom_call" | custom-call | tf_op jit(solution)/shard_map/pallas_call | solution.py:456
  14.6 0.0 collective-permute-done.from_other
  14.6 0.0 collective-permute-done.1.from_pair
  14.7 0.0 copy-done.1
  14.7 0.5 shard_map.89
  15.2 1.9 %collective-permute-start.2 = (f32[4,1024]{1,0:T(4,128)S(1)}, f32[4,1024]{1,0:T(4,128)S(1)}, u32[]{:S(2)}, u32[]{:S(2)}) collective-permute-start(f32[4,1024]{1,0:T(4,128)S(1)} %get-tuple-element.41), channel_id=1, source_target_pairs={{0,1},{2,3},{4,5},{6,7},{8,9},{10,11},{12,13},{14,15},{16,17},{18,... | collective-permute-start | bytes 49160 | tf_op jit(solution)/shard_map/ppermute | solution.py:419
  17.1 1.1 %shard_map.90.own = f32[32,1024]{1,0:T(8,128)S(1)} custom-call(bf16[32,1024]{1,0:T(8,128)(2,1)S(1)} %get-tuple-element.35.choose, f32[32,1024]{1,0:T(8,128)S(1)} %get-tuple-element.40.vector.first, bf16[256,2048]{1,0:T(8,128)(2,1)S(1)} %get-tuple-element.36.block_parts, bf16[384,768]{1,0:T(8,128)(2,1)S(1)} %get-tuple-element.37.lift_parts), custom_call_target="tpu_custom_call" | custom-call | tf_op jit(solution)/shard_map/pallas_call | solution.py:456
  18.2 0.1 collective-permute-done.2.from_pair
  18.3 0.5 shard_map.91
  18.8 1.9 %collective-permute-start.3 = (f32[8,1024]{1,0:T(8,128)S(1)}, f32[8,1024]{1,0:T(8,128)S(1)}, u32[]{:S(2)}, u32[]{:S(2)}) collective-permute-start(f32[8,1024]{1,0:T(8,128)S(1)} %get-tuple-element.44), channel_id=1, source_target_pairs={{1,2},{3,4},{5,6},{7,8},{9,10},{11,12},{13,14},{15,16},{17,18},{19... | collective-permute-start | bytes 98312 | tf_op jit(solution)/shard_map/ppermute | solution.py:419
  20.7 0.4 shard_map.92.missing
  21.1 2.9 %collective-permute-done.3.message = f32[8,1024]{1,0:T(8,128)S(1)} collective-permute-done((f32[8,1024]{1,0:T(8,128)S(1)}, f32[8,1024]{1,0:T(8,128)S(1)}, u32[]{:S(2)}, u32[]{:S(2)}) %collective-permute-start.3) | collective-permute-done | bytes 32800 | tf_op jit(solution)/shard_map/ppermute | solution.py:419
  24.0 1.7 %shard_map.93 = (f32[32,1024]{1,0:T(8,128)S(1)}, f32[32,1024]{1,0:T(8,128)S(1)}, f32[4,1024]{1,0:T(4,128)S(1)}, f32[8,1024]{1,0:T(8,128)S(1)}) custom-call(bf16[32,1024]{1,0:T(8,128)(2,1)S(1)} %get-tuple-element.35.choose, f32[32,1024]{1,0:T(8,128)S(1)} %get-tuple-element.43.partial, f32[8,1024]{1,0:T(8,128)S(1)} %collective-permute-done.3.message, ...), custom_call_target="tpu_custom_call" | custom-call | tf_op jit(solution)/shard_map/pallas_call | solution.py:476
  25.7 1.9 %collective-permute-start.4 = (f32[8,1024]{1,0:T(8,128)S(1)}, f32[8,1024]{1,0:T(8,128)S(1)}, u32[]{:S(2)}, u32[]{:S(2)}) collective-permute-start(f32[8,1024]{1,0:T(8,128)S(1)} %get-tuple-element.47), channel_id=1, source_target_pairs={{0,1},{2,3},{4,5},{6,7},{8,9},{10,11},{12,13},{14,15},{16,17},{18,... | collective-permute-start | bytes 98312 | tf_op jit(solution)/shard_map/ppermute | solution.py:419
  27.6 0.4 shard_map.94.missing
  28.0 0.8 collective-permute-done.4.message
  28.8 1.7 %shard_map.95 = (f32[32,1024]{1,0:T(8,128)S(1)}, f32[32,1024]{1,0:T(8,128)S(1)}, f32[4,1024]{1,0:T(4,128)S(1)}, f32[8,1024]{1,0:T(8,128)S(1)}) custom-call(bf16[32,1024]{1,0:T(8,128)(2,1)S(1)} %get-tuple-element.35.choose, f32[32,1024]{1,0:T(8,128)S(1)} %get-tuple-element.46.own, f32[8,1024]{1,0:T(8,128)S(1)} %collective-permute-done.4.message, ...), custom_call_target="tpu_custom_call" | custom-call | tf_op jit(solution)/shard_map/pallas_call | solution.py:482
  30.5 1.9 %collective-permute-start.5 = (f32[8,1024]{1,0:T(8,128)S(1)}, f32[8,1024]{1,0:T(8,128)S(1)}, u32[]{:S(2)}, u32[]{:S(2)}) collective-permute-start(f32[8,1024]{1,0:T(8,128)S(1)} %get-tuple-element.51), channel_id=1, source_target_pairs={{1,2},{3,4},{5,6},{7,8},{9,10},{11,12},{13,14},{15,16},{17,18},{19... | collective-permute-start | bytes 98312 | tf_op jit(solution)/shard_map/ppermute | solution.py:419
  32.4 0.8 shard_map.96
  33.2 2.5 %collective-permute-done.5.message = f32[8,1024]{1,0:T(8,128)S(1)} collective-permute-done((f32[8,1024]{1,0:T(8,128)S(1)}, f32[8,1024]{1,0:T(8,128)S(1)}, u32[]{:S(2)}, u32[]{:S(2)}) %collective-permute-start.5) | collective-permute-done | bytes 32800 | tf_op jit(solution)/shard_map/ppermute | solution.py:419
  35.7 0.5 shard_map.97
  36.2 1.9 %collective-permute-start.6 = (f32[4,1024]{1,0:T(4,128)S(1)}, f32[4,1024]{1,0:T(4,128)S(1)}, u32[]{:S(2)}, u32[]{:S(2)}) collective-permute-start(f32[4,1024]{1,0:T(4,128)S(1)} %get-tuple-element.59), channel_id=1, source_target_pairs={{0,1},{2,3},{4,5},{6,7},{8,9},{10,11},{12,13},{14,15},{16,17},{18,... | collective-permute-start | bytes 49160 | tf_op jit(solution)/shard_map/ppermute | solution.py:419
  38.2 1.1 %shard_map.98 = (f32[32,1024]{1,0:T(8,128)S(1)}, bf16[16,2048]{1,0:T(8,128)(2,1)S(1)}, bf16[16,2048]{1,0:T(8,128)(2,1)S(1)}) custom-call(bf16[32,1024]{1,0:T(8,128)(2,1)S(1)} %get-tuple-element.35.choose, f32[32,1024]{1,0:T(8,128)S(1)} %get-tuple-element.56.vector, bf16[256,2048]{1,0:T(8,128)(2,1)S(1)} %get-tuple-element.36.block_parts, ...), custom_call_target="tpu_custom_call" | custom-call | tf_op jit(solution)/shard_map/pallas_call | solution.py:497
  39.2 0.1 collective-permute-done.6.from_pair
  39.3 0.9 shard_map.99
  40.2 29.2 %all_to_all.10 = f32[32,16,128]{2,1,0:T(8,128)S(1)} all-to-all(f32[32,16,128]{2,1,0:T(8,128)S(1)} %bitcast.5), channel_id=1, replica_groups=mesh['outer'=4,'inner'=16,'narrow'=8] {'outer','narrow'}, dimensions={0} | all-to-all | bytes 524288 | tf_op jit(solution)/shard_map/all_to_all | solution.py:509
  69.5 16.6 %all_to_all.11 = f32[16,16,128]{2,1,0:T(8,128)S(1)} all-to-all(f32[16,16,128]{2,1,0:T(8,128)S(1)} %broadcast_in_dim.15), channel_id=1, replica_groups=mesh['outer'=4,'inner'=16,'narrow'=8] {'inner'}, dimensions={0} | all-to-all | bytes 262144 | tf_op jit(solution)/shard_map/all_to_all | solution.py:511
  86.2 4.9 %collective-permute-start.7 = (f32[16,128]{1,0:T(8,128)S(1)}, f32[16,128]{1,0:T(8,128)S(1)}, u32[]{:S(2)}, u32[]{:S(2)}) collective-permute-start(f32[16,128]{1,0:T(8,128)S(1)} %reduce_sum.19.mine), channel_id=1, source_target_pairs={{0,1},{2,3},{4,5},{6,7},{8,9},{10,11},{12,13},{14,15},{16,17},{18,... | collective-permute-start | bytes 24584 | tf_op jit(solution)/shard_map/ppermute | solution.py:419
  91.0 0.8 collective-permute-done.7.theirs
  91.8 2.8 %shard_map.100 = (f32[32,1024]{1,0:T(8,128)}, f32[32,1024]{1,0:T(8,128)}) custom-call(f32[16,128]{1,0:T(8,128)S(1)} %reduce_sum.19.mine, f32[16,128]{1,0:T(8,128)S(1)} %collective-permute-done.7.theirs, bf16[48,2048]{1,0:T(8,128)(2,1)S(1)} %get-tuple-element.60.high, bf16[48,2048]{1,0:T(8,128)(2,1)S(1)} %get-tuple-element.61.low, ...), custom_call_target="tpu_custom_call" | custom-call | tf_op jit(solution)/shard_map/pallas_call | solution.py:514
  (4 shorter events, 0.1 us)
Async XLA Ops:
  1.8 12.9 %collective-permute-start = (f32[8,1024]{1,0:T(8,128)S(1)}, f32[8,1024]{1,0:T(8,128)S(1)}, u32[]{:S(2)}, u32[]{:S(2)}) collective-permute-start(f32[8,1024]{1,0:T(8,128)S(1)} %get-tuple-element.38), channel_id=1, source_target_pairs={{1,2},{3,4},{5,6},{7,8},{9,10},{11,12},{13,14},{15,16},{17,18},{19... | collective-permute-start | bytes 98312 | tf_op jit(solution)/shard_map/ppermute | solution.py:419
  6.3 7.3 %copy-start = (f32[32,1024]{1,0:T(8,128)S(1)}, f32[32,1024]{1,0:T(8,128)}, u32[]{:S(2)}) copy-start(f32[32,1024]{1,0:T(8,128)} %guess.3) | copy-start | bytes 393220
  6.3 8.3 %collective-permute-start.1 = (f32[8,1024]{1,0:T(8,128)S(1)}, f32[8,1024]{1,0:T(8,128)S(1)}, u32[]{:S(2)}, u32[]{:S(2)}) collective-permute-start(f32[8,1024]{1,0:T(8,128)S(1)} %get-tuple-element.39), channel_id=1, source_target_pairs={{0,1},{2,3},{4,5},{6,7},{8,9},{10,11},{12,13},{14,15},{16,17},{18,... | collective-permute-start | bytes 98312 | tf_op jit(solution)/shard_map/ppermute | solution.py:419
  13.6 1.1 %copy-start.1 = (f32[32,1024]{1,0:T(8,128)S(1)}, f32[32,1024]{1,0:T(8,128)}, u32[]{:S(2)}) copy-start(f32[32,1024]{1,0:T(8,128)} %right.1) | copy-start | bytes 393220
  15.2 3.1 %collective-permute-start.2 = (f32[4,1024]{1,0:T(4,128)S(1)}, f32[4,1024]{1,0:T(4,128)S(1)}, u32[]{:S(2)}, u32[]{:S(2)}) collective-permute-start(f32[4,1024]{1,0:T(4,128)S(1)} %get-tuple-element.41), channel_id=1, source_target_pairs={{0,1},{2,3},{4,5},{6,7},{8,9},{10,11},{12,13},{14,15},{16,17},{18,... | collective-permute-start | bytes 49160 | tf_op jit(solution)/shard_map/ppermute | solution.py:419
  18.8 5.2 %collective-permute-start.3 = (f32[8,1024]{1,0:T(8,128)S(1)}, f32[8,1024]{1,0:T(8,128)S(1)}, u32[]{:S(2)}, u32[]{:S(2)}) collective-permute-start(f32[8,1024]{1,0:T(8,128)S(1)} %get-tuple-element.44), channel_id=1, source_target_pairs={{1,2},{3,4},{5,6},{7,8},{9,10},{11,12},{13,14},{15,16},{17,18},{19... | collective-permute-start | bytes 98312 | tf_op jit(solution)/shard_map/ppermute | solution.py:419
  25.7 3.1 %collective-permute-start.4 = (f32[8,1024]{1,0:T(8,128)S(1)}, f32[8,1024]{1,0:T(8,128)S(1)}, u32[]{:S(2)}, u32[]{:S(2)}) collective-permute-start(f32[8,1024]{1,0:T(8,128)S(1)} %get-tuple-element.47), channel_id=1, source_target_pairs={{0,1},{2,3},{4,5},{6,7},{8,9},{10,11},{12,13},{14,15},{16,17},{18,... | collective-permute-start | bytes 98312 | tf_op jit(solution)/shard_map/ppermute | solution.py:419
  30.5 5.2 %collective-permute-start.5 = (f32[8,1024]{1,0:T(8,128)S(1)}, f32[8,1024]{1,0:T(8,128)S(1)}, u32[]{:S(2)}, u32[]{:S(2)}) collective-permute-start(f32[8,1024]{1,0:T(8,128)S(1)} %get-tuple-element.51), channel_id=1, source_target_pairs={{1,2},{3,4},{5,6},{7,8},{9,10},{11,12},{13,14},{15,16},{17,18},{19... | collective-permute-start | bytes 98312 | tf_op jit(solution)/shard_map/ppermute | solution.py:419
  36.2 3.1 %collective-permute-start.6 = (f32[4,1024]{1,0:T(4,128)S(1)}, f32[4,1024]{1,0:T(4,128)S(1)}, u32[]{:S(2)}, u32[]{:S(2)}) collective-permute-start(f32[4,1024]{1,0:T(4,128)S(1)} %get-tuple-element.59), channel_id=1, source_target_pairs={{0,1},{2,3},{4,5},{6,7},{8,9},{10,11},{12,13},{14,15},{16,17},{18,... | collective-permute-start | bytes 49160 | tf_op jit(solution)/shard_map/ppermute | solution.py:419
  86.2 5.7 %collective-permute-start.7 = (f32[16,128]{1,0:T(8,128)S(1)}, f32[16,128]{1,0:T(8,128)S(1)}, u32[]{:S(2)}, u32[]{:S(2)}) collective-permute-start(f32[16,128]{1,0:T(8,128)S(1)} %reduce_sum.19.mine), channel_id=1, source_target_pairs={{0,1},{2,3},{4,5},{6,7},{8,9},{10,11},{12,13},{14,15},{16,17},{18,... | collective-permute-start | bytes 24584 | tf_op jit(solution)/shard_map/ppermute | solution.py:419

commit v8 on v7

--- a/solution.py
+++ b/solution.py
@@ -299,8 +299,29 @@
     next_other[...] = message[GHOST:] + missing[...]
 
 
+def fold(blocks):
+    lane = lax.broadcasted_iota(jnp.int32, (1, 128), 1)
+    rows = []
+    for k in range(14):
+        part = pltpu.roll(blocks[14 + k // 7 : 15 + k // 7, :], (112 - 16 * (k % 7)) % 128, 1)
+        rows.append(jnp.where(lane < 112, blocks[k : k + 1, :], part))
+    return rows
+
+
+def unfold(rows):
+    lane = lax.broadcasted_iota(jnp.int32, (1, 128), 1) // 16
+    ends = []
+    for half in range(2):
+        total = jnp.zeros((1, 128), F32)
+        for b in range(7):
+            part = pltpu.roll(rows[7 * half + b], 16 * b + 16, 1)
+            total = jnp.where(lane == b, part, total)
+        ends.append(total)
+    return jnp.concatenate(rows + ends, 0)
+
+
 def last_kernel(
-    choose, own, from_other, from_pair, lift_parts, high, low, high3, low3, gram, high4, low4, packed, newest, tiled,
+    choose, own, from_other, from_pair, lift_parts, high, low, high3, low3, gram, high4, low4, packed, newest, tiled, gram_low,
 ):
     newest[...] = GAIN * (own[...] + from_sides(choose, lift_parts, from_other[...], from_pair[...]))
     to_tiles(newest, tiled)
@@ -313,8 +334,28 @@
         jnp.concatenate([high[...], left_high], 0),
         jnp.concatenate([low[...], left_low], 0),
     )
-    packed[0:16] = jnp.concatenate([rows[16:], gram[16:32, :32], gram[:16, :16]], 1)
-    packed[16:32] = jnp.concatenate([rows[:16, :64], gram[32:, :], jnp.zeros((16, 16), F32)], 1)
+    gram_low[...] = jnp.zeros((128, 128), F32)
+    gram_low[0:48, 0:48] = gram[...]
+    gram_low[48:80, 0:80] = rows
+    known = gram_low[...]
+    row = lax.broadcasted_iota(jnp.int32, (128, 128), 0) // 16
+    column = lax.broadcasted_iota(jnp.int32, (128, 128), 1) // 16
+    full = jnp.where(row >= column, known, known.T)
+    weighted = full[:64] + full[16:80] * (1.0 / GAIN)
+    normal = weighted + pltpu.roll(weighted, 112, 1) * (1.0 / GAIN)
+    lane = lax.broadcasted_iota(jnp.int32, (16, 128), 1)
+    joined = []
+    for a in range(STEPS):
+        part = slice(16 * a, 16 * a + 16)
+        width = 16 * (a + 1)
+        right = pltpu.roll(weighted[part], width, 1)
+        joined.append(jnp.where(lane < width, normal[part], right))
+    first = jnp.where(lane < 80, joined[3], pltpu.roll(joined[0], 80, 1))
+    second = jnp.where(lane < 64, joined[2], pltpu.roll(joined[1], 64, 1))
+    for half, blocks in enumerate((first, second)):
+        folded = fold(blocks)
+        for k in range(7):
+            packed[half, k] = jnp.concatenate(folded[2 * k : 2 * k + 2], 0)
 
 
 def solve_spd(system):
@@ -350,28 +391,22 @@
     high = jnp.concatenate([high[...], high3[...], high4[...]], 0)
     low = jnp.concatenate([low[...], low3[...], low4[...]], 0)
     odd = lax.rem(lax.axis_index("narrow"), 2) == 1
-    upper = jnp.where(odd, theirs[...], mine[...])
-    lower = jnp.where(odd, mine[...], theirs[...])
+    halves = []
+    for one, two in ((mine, theirs), (theirs, mine)):
+        pairs = [jnp.where(odd, two[k], one[k]) for k in range(7)]
+        halves.append(unfold([pair[i : i + 1, :] for pair in pairs for i in range(2)]))
     lane = lax.broadcasted_iota(jnp.int32, (16, 128), 1)
-    pieces = [
-        (pltpu.roll(upper, 16, 1), 16),
-        (pltpu.roll(upper, 48, 1), 32),
-        (pltpu.roll(lower, 64, 1), 48),
-        (lower, 64),
-        (upper, 80),
-    ]
-    for a, (piece, width) in enumerate(pieces):
-        gram_low[16 * a : 16 * a + 16, :] = jnp.where(lane < width, piece, 0.0)
-    gram_low[80:, :] = jnp.zeros((48, 128), F32)
-    lower_part = gram_low[...]
-    row = lax.broadcasted_iota(jnp.int32, (128, 128), 0) // 16
-    column = lax.broadcasted_iota(jnp.int32, (128, 128), 1) // 16
-    gram = jnp.where(row >= column, lower_part, lower_part.T)
-    weighted = gram[:64] + gram[16:80] * (1.0 / GAIN)
-    lane = lax.broadcasted_iota(jnp.int32, (64, 128), 1)
-    normal = weighted + pltpu.roll(weighted, 112, 1) * (1.0 / GAIN)
-    system = jnp.where(lane < 64, normal, pltpu.roll(weighted, 64, 1))
-    system = jnp.where(lane < 80, system, 0.0)
+    joined = [pltpu.roll(halves[0], 48, 1), pltpu.roll(halves[1], 64, 1), halves[1], halves[0]]
+    for a, part in enumerate(joined):
+        width = 16 * (a + 1)
+        right = pltpu.roll(part, (64 - width) % 128, 1)
+        right = jnp.where((lane >= 64) & (lane < 80), right, 0.0)
+        gram_low[16 * a : 16 * a + 16, :] = jnp.where(lane < width, part, right)
+    gram_low[64:, :] = jnp.zeros((64, 128), F32)
+    known = gram_low[...]
+    row = lax.broadcasted_iota(jnp.int32, (64, 128), 0) // 16
+    column = lax.broadcasted_iota(jnp.int32, (64, 128), 1) // 16
+    system = jnp.where((row >= column) | (column >= 4), known[:64], known.T[:64])
     coeffs = pltpu.roll(solve_spd(system), 64, 1)
     empty = jnp.zeros((16, 128), F32)
     padded = jnp.concatenate([coeffs, empty], 0)
@@ -499,15 +534,15 @@
     )(choose, vector, block_parts, lift_parts)
     high4, low4, packed = call(
         last_kernel,
-        [stack(16), stack(16), jax.ShapeDtypeStruct((32, 128), F32)],
-        [pltpu.VMEM((ELEMS, WIDTH), F32), tile_scratch],
+        [stack(16), stack(16), jax.ShapeDtypeStruct((2, 7, 2, 128), F32)],
+        [pltpu.VMEM((ELEMS, WIDTH), F32), tile_scratch, pltpu.VMEM((128, 128), F32)],
         [VMEM] * 10,
     )(choose, own, next_other, from_pair, lift_parts, high, low, high3, low3, gram)
     outer, inner, narrow = (lax.axis_size(axis) for axis in axes)
-    halves = jnp.broadcast_to(packed.reshape(1, 2, 16, 128), (outer * narrow // 2, 2, 16, 128))
-    halves = halves.reshape(outer * narrow, 16, 128)
+    halves = jnp.broadcast_to(packed[None], (outer * narrow // 2, 2, 7, 2, 128))
+    halves = halves.reshape(outer * narrow, 7, 2, 128)
     mine = lax.all_to_all(halves, (axes[0], axes[2]), 0, 0).sum(0)
-    mine = jnp.broadcast_to(mine[None], (inner, 16, 128))
+    mine = jnp.broadcast_to(mine[None], (inner, 7, 2, 128))
     mine = lax.all_to_all(mine, axes[1], 0, 0).sum(0)
     theirs = swapped(mine, axes, 0)
     return tuple(

time: 95 us -> 94.8 us (level)
  no operation moved by 1% of the time
where the time goes in v8:
time: 94.8 us; the launch traced here: 94.4 us
  blocking collectives  45.4 us (48%)
  starting transfers between devices  23.8 us (25%)
  Pallas kernels  17 us (18%)
  waiting for transfers between devices  7.18 us (8%)
    all_to_all x1, blocking collectives, local(): mine = lax.all_to_all(halves, (axes[0], axes[2]), 0, 0).sum(0)  28.9 us
    ppermute x8, starting transfers between devices, swapped(): lax.ppermute(block, axes, [(i, i + 1) for i in lower] + [(i + 1, i) for i...  23.8 us
    all_to_all x1, blocking collectives, local(): mine = lax.all_to_all(mine, axes[1], 0, 0).sum(0)  16.5 us
    ppermute x8, waiting for transfers between devices, swapped(): lax.ppermute(block, axes, [(i, i + 1) for i in lower] + [(i + 1, i) for i...  7.18 us
    pallas_call x1, Pallas kernels, local(): call(solve_kernel, [FIELD, FIELD], [pltpu.VMEM((128, 128), F32), pltpu.VM...  2.84 us
    pallas_call x1, Pallas kernels, local(): call(prep_kernel, [jax.ShapeDtypeStruct((256, ELEMS * NODES), BF16), jax....  2.16 us
    pallas_call x2, Pallas kernels, local(): call(first_own_kernel, [FIELD], [tile_scratch] * 2, [VMEM] * 4)(*args)[0]  2.12 us
  transfers between devices with their start and end apart: 8, of which 6 were waited for; matrix products, arithmetic and copies ran while one was open for 0% of the time, Pallas kernels for 7%

profile of v8, /device:TPU:1, one launch (start us, length us, event | category | flops | bytes accessed | tf_op | source)
XLA Modules:
  0.0 94.4 jit_solution(7851725071435362529)
XLA Ops:
  0.6 1.1 %shard_map.86 = (f32[8,1024]{1,0:T(8,128)S(1)}, f32[8,1024]{1,0:T(8,128)S(1)}, bf16[32,1024]{1,0:T(8,128)(2,1)S(1)}) custom-call(s32[1,8]{1,0:T(1,128)} %send_in.1, f32[32,1024]{1,0:T(8,128)} %guess.3, s32[6,32]{1,0:T(8,128)} %bitcast.4, f32[6,32]{1,0:T(8,128)} %bitcast.5), custom_call_target="tpu_custom_call" | custom-call | tf_op jit(solution)/shard_map/pallas_call | solution.py:460
  1.8 4.5 %collective-permute-start = (f32[8,1024]{1,0:T(8,128)S(1)}, f32[8,1024]{1,0:T(8,128)S(1)}, u32[]{:S(2)}, u32[]{:S(2)}) collective-permute-start(f32[8,1024]{1,0:T(8,128)S(1)} %get-tuple-element.38), channel_id=1, source_target_pairs={{1,2},{3,4},{5,6},{7,8},{9,10},{11,12},{13,14},{15,16},{17,18},{19... | collective-permute-start | bytes 98312 | tf_op jit(solution)/shard_map/ppermute | solution.py:454
  6.3 0.0 copy-start
  6.3 5.1 %collective-permute-start.1 = (f32[8,1024]{1,0:T(8,128)S(1)}, f32[8,1024]{1,0:T(8,128)S(1)}, u32[]{:S(2)}, u32[]{:S(2)}) collective-permute-start(f32[8,1024]{1,0:T(8,128)S(1)} %get-tuple-element.39), channel_id=1, source_target_pairs={{0,1},{2,3},{4,5},{6,7},{8,9},{10,11},{12,13},{14,15},{16,17},{18,... | collective-permute-start | bytes 98312 | tf_op jit(solution)/shard_map/ppermute | solution.py:454
  11.4 2.2 %shard_map.87 = (bf16[256,2048]{1,0:T(8,128)(2,1)S(1)}, bf16[384,768]{1,0:T(8,128)(2,1)S(1)}) custom-call(f32[32,4096]{1,0:T(8,128)} %blocks_in.1, f32[6,64,64]{2,1,0:T(8,128)} %lift_in.1), custom_call_target="tpu_custom_call" | custom-call | tf_op jit(solution)/shard_map/pallas_call | solution.py:476
  13.5 0.0 copy-done
  13.6 0.0 copy-start.1
  13.6 1.1 %shard_map.88.own = f32[32,1024]{1,0:T(8,128)S(1)} custom-call(bf16[32,1024]{1,0:T(8,128)(2,1)S(1)} %get-tuple-element.35.choose, f32[32,1024]{1,0:T(8,128)S(1)} %copy-done, bf16[256,2048]{1,0:T(8,128)(2,1)S(1)} %get-tuple-element.36.block_parts, bf16[384,768]{1,0:T(8,128)(2,1)S(1)} %get-tuple-element.37.lift_parts), custom_call_target="tpu_custom_call" | custom-call | tf_op jit(solution)/shard_map/pallas_call | solution.py:491
  14.6 0.0 collective-permute-done.from_other
  14.6 0.0 collective-permute-done.1.from_pair
  14.7 0.0 copy-done.1
  14.7 0.5 shard_map.89
  15.2 1.9 %collective-permute-start.2 = (f32[4,1024]{1,0:T(4,128)S(1)}, f32[4,1024]{1,0:T(4,128)S(1)}, u32[]{:S(2)}, u32[]{:S(2)}) collective-permute-start(f32[4,1024]{1,0:T(4,128)S(1)} %get-tuple-element.41), channel_id=1, source_target_pairs={{0,1},{2,3},{4,5},{6,7},{8,9},{10,11},{12,13},{14,15},{16,17},{18,... | collective-permute-start | bytes 49160 | tf_op jit(solution)/shard_map/ppermute | solution.py:454
  17.1 1.1 %shard_map.90.own = f32[32,1024]{1,0:T(8,128)S(1)} custom-call(bf16[32,1024]{1,0:T(8,128)(2,1)S(1)} %get-tuple-element.35.choose, f32[32,1024]{1,0:T(8,128)S(1)} %get-tuple-element.40.vector.first, bf16[256,2048]{1,0:T(8,128)(2,1)S(1)} %get-tuple-element.36.block_parts, bf16[384,768]{1,0:T(8,128)(2,1)S(1)} %get-tuple-element.37.lift_parts), custom_call_target="tpu_custom_call" | custom-call | tf_op jit(solution)/shard_map/pallas_call | solution.py:491
  18.2 0.1 collective-permute-done.2.from_pair
  18.3 0.5 shard_map.91
  18.8 1.9 %collective-permute-start.3 = (f32[8,1024]{1,0:T(8,128)S(1)}, f32[8,1024]{1,0:T(8,128)S(1)}, u32[]{:S(2)}, u32[]{:S(2)}) collective-permute-start(f32[8,1024]{1,0:T(8,128)S(1)} %get-tuple-element.44), channel_id=1, source_target_pairs={{1,2},{3,4},{5,6},{7,8},{9,10},{11,12},{13,14},{15,16},{17,18},{19... | collective-permute-start | bytes 98312 | tf_op jit(solution)/shard_map/ppermute | solution.py:454
  20.7 0.4 shard_map.92.missing
  21.1 2.9 %collective-permute-done.3.message = f32[8,1024]{1,0:T(8,128)S(1)} collective-permute-done((f32[8,1024]{1,0:T(8,128)S(1)}, f32[8,1024]{1,0:T(8,128)S(1)}, u32[]{:S(2)}, u32[]{:S(2)}) %collective-permute-start.3) | collective-permute-done | bytes 32800 | tf_op jit(solution)/shard_map/ppermute | solution.py:454
  24.0 1.7 %shard_map.93 = (f32[32,1024]{1,0:T(8,128)S(1)}, f32[32,1024]{1,0:T(8,128)S(1)}, f32[4,1024]{1,0:T(4,128)S(1)}, f32[8,1024]{1,0:T(8,128)S(1)}) custom-call(bf16[32,1024]{1,0:T(8,128)(2,1)S(1)} %get-tuple-element.35.choose, f32[32,1024]{1,0:T(8,128)S(1)} %get-tuple-element.43.partial, f32[8,1024]{1,0:T(8,128)S(1)} %collective-permute-done.3.message, ...), custom_call_target="tpu_custom_call" | custom-call | tf_op jit(solution)/shard_map/pallas_call | solution.py:511
  25.7 1.9 %collective-permute-start.4 = (f32[8,1024]{1,0:T(8,128)S(1)}, f32[8,1024]{1,0:T(8,128)S(1)}, u32[]{:S(2)}, u32[]{:S(2)}) collective-permute-start(f32[8,1024]{1,0:T(8,128)S(1)} %get-tuple-element.47), channel_id=1, source_target_pairs={{0,1},{2,3},{4,5},{6,7},{8,9},{10,11},{12,13},{14,15},{16,17},{18,... | collective-permute-start | bytes 98312 | tf_op jit(solution)/shard_map/ppermute | solution.py:454
  27.6 0.4 shard_map.94.missing
  28.0 0.8 collective-permute-done.4.message
  28.8 1.7 %shard_map.95 = (f32[32,1024]{1,0:T(8,128)S(1)}, f32[32,1024]{1,0:T(8,128)S(1)}, f32[4,1024]{1,0:T(4,128)S(1)}, f32[8,1024]{1,0:T(8,128)S(1)}) custom-call(bf16[32,1024]{1,0:T(8,128)(2,1)S(1)} %get-tuple-element.35.choose, f32[32,1024]{1,0:T(8,128)S(1)} %get-tuple-element.46.own, f32[8,1024]{1,0:T(8,128)S(1)} %collective-permute-done.4.message, ...), custom_call_target="tpu_custom_call" | custom-call | tf_op jit(solution)/shard_map/pallas_call | solution.py:517
  30.5 1.9 %collective-permute-start.5 = (f32[8,1024]{1,0:T(8,128)S(1)}, f32[8,1024]{1,0:T(8,128)S(1)}, u32[]{:S(2)}, u32[]{:S(2)}) collective-permute-start(f32[8,1024]{1,0:T(8,128)S(1)} %get-tuple-element.51), channel_id=1, source_target_pairs={{1,2},{3,4},{5,6},{7,8},{9,10},{11,12},{13,14},{15,16},{17,18},{19... | collective-permute-start | bytes 98312 | tf_op jit(solution)/shard_map/ppermute | solution.py:454
  32.4 0.8 shard_map.96
  33.2 2.5 %collective-permute-done.5.message = f32[8,1024]{1,0:T(8,128)S(1)} collective-permute-done((f32[8,1024]{1,0:T(8,128)S(1)}, f32[8,1024]{1,0:T(8,128)S(1)}, u32[]{:S(2)}, u32[]{:S(2)}) %collective-permute-start.5) | collective-permute-done | bytes 32800 | tf_op jit(solution)/shard_map/ppermute | solution.py:454
  35.7 0.5 shard_map.97
  36.2 1.9 %collective-permute-start.6 = (f32[4,1024]{1,0:T(4,128)S(1)}, f32[4,1024]{1,0:T(4,128)S(1)}, u32[]{:S(2)}, u32[]{:S(2)}) collective-permute-start(f32[4,1024]{1,0:T(4,128)S(1)} %get-tuple-element.59), channel_id=1, source_target_pairs={{0,1},{2,3},{4,5},{6,7},{8,9},{10,11},{12,13},{14,15},{16,17},{18,... | collective-permute-start | bytes 49160 | tf_op jit(solution)/shard_map/ppermute | solution.py:454
  38.2 1.1 %shard_map.98 = (f32[32,1024]{1,0:T(8,128)S(1)}, bf16[16,2048]{1,0:T(8,128)(2,1)S(1)}, bf16[16,2048]{1,0:T(8,128)(2,1)S(1)}) custom-call(bf16[32,1024]{1,0:T(8,128)(2,1)S(1)} %get-tuple-element.35.choose, f32[32,1024]{1,0:T(8,128)S(1)} %get-tuple-element.56.vector, bf16[256,2048]{1,0:T(8,128)(2,1)S(1)} %get-tuple-element.36.block_parts, ...), custom_call_target="tpu_custom_call" | custom-call | tf_op jit(solution)/shard_map/pallas_call | solution.py:532
  39.2 0.1 collective-permute-done.6.from_pair
  39.3 1.2 %shard_map.99 = (bf16[16,2048]{1,0:T(8,128)(2,1)S(1)}, bf16[16,2048]{1,0:T(8,128)(2,1)S(1)}, f32[2,7,2,128]{3,2,1,0:T(2,128)S(1)}) custom-call(bf16[32,1024]{1,0:T(8,128)(2,1)S(1)} %get-tuple-element.35.choose, f32[32,1024]{1,0:T(8,128)S(1)} %get-tuple-element.57.own, f32[4,1024]{1,0:T(4,128)S(1)} %get-tuple-element.58.from_other, ...), custom_call_target="tpu_custom_call" | custom-call | tf_op jit(solution)/shard_map/pallas_call | solution.py:535
  40.5 0.1 broadcast_in_dim.4
  40.6 28.9 %all_to_all.10 = f32[32,7,2,128]{3,2,1,0:T(2,128)S(1)} all-to-all(f32[32,7,2,128]{3,2,1,0:T(2,128)S(1)} %bitcast.3), channel_id=1, replica_groups=mesh['outer'=4,'inner'=16,'narrow'=8] {'outer','narrow'}, dimensions={0} | all-to-all | bytes 458752 | tf_op jit(solution)/shard_map/all_to_all | solution.py:544
  69.5 0.1 reduce_sum.18
  69.6 16.5 %all_to_all.11 = f32[16,7,2,128]{3,2,1,0:T(2,128)S(1)} all-to-all(f32[16,7,2,128]{3,2,1,0:T(2,128)S(1)} %broadcast_in_dim.5), channel_id=1, replica_groups=mesh['outer'=4,'inner'=16,'narrow'=8] {'inner'}, dimensions={0} | all-to-all | bytes 229376 | tf_op jit(solution)/shard_map/all_to_all | solution.py:546
  86.1 0.1 reduce_sum.19.mine
  86.2 4.6 %collective-permute-start.7 = (f32[7,2,128]{2,1,0:T(2,128)S(1)}, f32[7,2,128]{2,1,0:T(2,128)S(1)}, u32[]{:S(2)}, u32[]{:S(2)}) collective-permute-start(f32[7,2,128]{2,1,0:T(2,128)S(1)} %reduce_sum.19.mine), channel_id=1, source_target_pairs={{0,1},{2,3},{4,5},{6,7},{8,9},{10,11},{12,13},{14,15},{16,17},{18,... | collective-permute-start | bytes 21512 | tf_op jit(solution)/shard_map/ppermute | solution.py:454
  90.8 0.8 collective-permute-done.7.theirs
  91.6 2.8 %shard_map.100 = (f32[32,1024]{1,0:T(8,128)}, f32[32,1024]{1,0:T(8,128)}) custom-call(f32[7,2,128]{2,1,0:T(2,128)S(1)} %reduce_sum.19.mine, f32[7,2,128]{2,1,0:T(2,128)S(1)} %collective-permute-done.7.theirs, bf16[48,2048]{1,0:T(8,128)(2,1)S(1)} %get-tuple-element.60.high, bf16[48,2048]{1,0:T(8,128)(2,1)S(1)} %get-tuple-element.61.low, ...), custom_call_target="tpu_custom_call" | custom-call | tf_op jit(solution)/shard_map/pallas_call | solution.py:549
  (1 shorter events, 0.0 us)
Async XLA Ops:
  1.8 12.9 %collective-permute-start = (f32[8,1024]{1,0:T(8,128)S(1)}, f32[8,1024]{1,0:T(8,128)S(1)}, u32[]{:S(2)}, u32[]{:S(2)}) collective-permute-start(f32[8,1024]{1,0:T(8,128)S(1)} %get-tuple-element.38), channel_id=1, source_target_pairs={{1,2},{3,4},{5,6},{7,8},{9,10},{11,12},{13,14},{15,16},{17,18},{19... | collective-permute-start | bytes 98312 | tf_op jit(solution)/shard_map/ppermute | solution.py:454
  6.3 7.3 %copy-start = (f32[32,1024]{1,0:T(8,128)S(1)}, f32[32,1024]{1,0:T(8,128)}, u32[]{:S(2)}) copy-start(f32[32,1024]{1,0:T(8,128)} %guess.3) | copy-start | bytes 393220
  6.3 8.3 %collective-permute-start.1 = (f32[8,1024]{1,0:T(8,128)S(1)}, f32[8,1024]{1,0:T(8,128)S(1)}, u32[]{:S(2)}, u32[]{:S(2)}) collective-permute-start(f32[8,1024]{1,0:T(8,128)S(1)} %get-tuple-element.39), channel_id=1, source_target_pairs={{0,1},{2,3},{4,5},{6,7},{8,9},{10,11},{12,13},{14,15},{16,17},{18,... | collective-permute-start | bytes 98312 | tf_op jit(solution)/shard_map/ppermute | solution.py:454
  13.6 1.1 %copy-start.1 = (f32[32,1024]{1,0:T(8,128)S(1)}, f32[32,1024]{1,0:T(8,128)}, u32[]{:S(2)}) copy-start(f32[32,1024]{1,0:T(8,128)} %right.1) | copy-start | bytes 393220
  15.2 3.1 %collective-permute-start.2 = (f32[4,1024]{1,0:T(4,128)S(1)}, f32[4,1024]{1,0:T(4,128)S(1)}, u32[]{:S(2)}, u32[]{:S(2)}) collective-permute-start(f32[4,1024]{1,0:T(4,128)S(1)} %get-tuple-element.41), channel_id=1, source_target_pairs={{0,1},{2,3},{4,5},{6,7},{8,9},{10,11},{12,13},{14,15},{16,17},{18,... | collective-permute-start | bytes 49160 | tf_op jit(solution)/shard_map/ppermute | solution.py:454
  18.8 5.2 %collective-permute-start.3 = (f32[8,1024]{1,0:T(8,128)S(1)}, f32[8,1024]{1,0:T(8,128)S(1)}, u32[]{:S(2)}, u32[]{:S(2)}) collective-permute-start(f32[8,1024]{1,0:T(8,128)S(1)} %get-tuple-element.44), channel_id=1, source_target_pairs={{1,2},{3,4},{5,6},{7,8},{9,10},{11,12},{13,14},{15,16},{17,18},{19... | collective-permute-start | bytes 98312 | tf_op jit(solution)/shard_map/ppermute | solution.py:454
  25.7 3.1 %collective-permute-start.4 = (f32[8,1024]{1,0:T(8,128)S(1)}, f32[8,1024]{1,0:T(8,128)S(1)}, u32[]{:S(2)}, u32[]{:S(2)}) collective-permute-start(f32[8,1024]{1,0:T(8,128)S(1)} %get-tuple-element.47), channel_id=1, source_target_pairs={{0,1},{2,3},{4,5},{6,7},{8,9},{10,11},{12,13},{14,15},{16,17},{18,... | collective-permute-start | bytes 98312 | tf_op jit(solution)/shard_map/ppermute | solution.py:454
  30.5 5.2 %collective-permute-start.5 = (f32[8,1024]{1,0:T(8,128)S(1)}, f32[8,1024]{1,0:T(8,128)S(1)}, u32[]{:S(2)}, u32[]{:S(2)}) collective-permute-start(f32[8,1024]{1,0:T(8,128)S(1)} %get-tuple-element.51), channel_id=1, source_target_pairs={{1,2},{3,4},{5,6},{7,8},{9,10},{11,12},{13,14},{15,16},{17,18},{19... | collective-permute-start | bytes 98312 | tf_op jit(solution)/shard_map/ppermute | solution.py:454
  36.2 3.1 %collective-permute-start.6 = (f32[4,1024]{1,0:T(4,128)S(1)}, f32[4,1024]{1,0:T(4,128)S(1)}, u32[]{:S(2)}, u32[]{:S(2)}) collective-permute-start(f32[4,1024]{1,0:T(4,128)S(1)} %get-tuple-element.59), channel_id=1, source_target_pairs={{0,1},{2,3},{4,5},{6,7},{8,9},{10,11},{12,13},{14,15},{16,17},{18,... | collective-permute-start | bytes 49160 | tf_op jit(solution)/shard_map/ppermute | solution.py:454
  86.2 5.4 %collective-permute-start.7 = (f32[7,2,128]{2,1,0:T(2,128)S(1)}, f32[7,2,128]{2,1,0:T(2,128)S(1)}, u32[]{:S(2)}, u32[]{:S(2)}) collective-permute-start(f32[7,2,128]{2,1,0:T(2,128)S(1)} %reduce_sum.19.mine), channel_id=1, source_target_pairs={{0,1},{2,3},{4,5},{6,7},{8,9},{10,11},{12,13},{14,15},{16,17},{18,... | collective-permute-start | bytes 21512 | tf_op jit(solution)/shard_map/ppermute | solution.py:454

commit v9 on v8

--- a/solution.py
+++ b/solution.py
@@ -67,22 +67,22 @@
     return jnp.concatenate([high, high, chosen - high], axis)
 
 
+def ghost_selection(near, scale, odd):
+    place = lambda m: ELEMS + lax.rem(m + GHOST * odd, 2 * GHOST)
+    return selection(near, scale, place, 2 * GHOST)
+
+
 def pack_kernel(
-    send_in, guess_in, near_in, scale_in, to_other, to_pair, choose,
-    guess, near, scale, send_row, terms, send, done,
-):
-    pairs = [(send_in, send), (guess_in, guess), (near_in, near), (scale_in, scale), (send_in, send_row)]
+    send_in, guess_in, near_in, scale_in, to_other, to_pair, guess, near, scale, terms, send, done
+):
+    pairs = [(send_in, send), (guess_in, guess), (near_in, near), (scale_in, scale)]
     copies = [pltpu.make_async_copy(a, b, done.at[i]) for i, (a, b) in enumerate(pairs)]
     for copy in copies:
         copy.start()
     for copy in copies:
         copy.wait()
     odd = lax.rem(lax.axis_index("narrow"), 2)
-    choose[...] = jnp.zeros((ELEMS, 1024), BF16)
-    own = selection(near, scale, lambda n: n, ELEMS)
-    choose[:, OWN[0] : OWN[1]] = three_parts(own, 0).T.astype(BF16)
-    ghosts = selection(near, scale, lambda m: ELEMS + lax.rem(m + GHOST * odd, 2 * GHOST), 2 * GHOST)
-    choose[:, FROM[0] : FROM[1]] = three_parts(ghosts, 0).T.astype(BF16)
+    ghosts = ghost_selection(near, scale, odd)
     terms[...] = jnp.zeros((ELEMS, 128), F32)
     terms[:, : FACES * 2 * GHOST] = ghosts.T
     for out, first in ((to_other, GHOST * odd), (to_pair, GHOST * (1 - odd))):
@@ -91,28 +91,36 @@
             row = send[0, first + k]
             out[k : k + 1, :] = guess[pl.ds(row, 1), :]
             out[GHOST + k : GHOST + k + 1, :128] = terms[pl.ds(row, 1), :]
+
+
+def prep_kernel(
+    send_in, near_in, scale_in, lift_in, blocks_in, choose, block_parts, lift_parts,
+    send_row, near, scale, lift, blocks, spread_blocks, done,
+):
+    pairs = [(send_in, send_row), (near_in, near), (scale_in, scale), (lift_in, lift), (blocks_in, blocks)]
+    copies = [pltpu.make_async_copy(a, b, done.at[i]) for i, (a, b) in enumerate(pairs)]
+    for copy in copies:
+        copy.start()
+    for copy in copies[:3]:
+        copy.wait()
+    odd = lax.rem(lax.axis_index("narrow"), 2)
+    choose[...] = jnp.zeros((ELEMS, 1024), BF16)
+    own = selection(near, scale, lambda n: n, ELEMS)
+    choose[:, OWN[0] : OWN[1]] = three_parts(own, 0).T.astype(BF16)
+    choose[:, FROM[0] : FROM[1]] = three_parts(ghost_selection(near, scale, odd), 0).T.astype(BF16)
     row = send_row[...]
     row = jnp.where(odd == 1, jnp.concatenate([row[:, GHOST:], row[:, :GHOST]], 1), row)
     rows = (lax.broadcasted_iota(jnp.int32, (ELEMS, 2 * GHOST), 0) == row).astype(F32)
     rows = jnp.concatenate([rows, jnp.zeros((ELEMS, ELEMS - 2 * GHOST), F32)], 1)
     choose[:, SEND[0] : SEND[1]] = jnp.concatenate([rows, rows, rows], 0).T.astype(BF16)
-
-
-def prep_kernel(blocks_in, lift_in, block_parts, lift_parts, blocks, lift, spread_blocks, done):
-    copies = [
-        pltpu.make_async_copy(lift_in, lift, done.at[0]),
-        pltpu.make_async_copy(blocks_in, blocks, done.at[1]),
-    ]
-    for copy in copies:
-        copy.start()
-    copies[0].wait()
+    copies[3].wait()
     for f in range(FACES):
         upper = jnp.concatenate([lift[f], jnp.zeros((NODES, NODES), F32)], 1)
         high, low = split(jnp.concatenate([upper, swap(upper)], 0).T)
         lift_parts[:128, slab(f)] = high
         lift_parts[128:256, slab(f)] = high
         lift_parts[256:, slab(f)] = low
-    copies[1].wait()
+    copies[4].wait()
     mask = left_half((ELEMS, 128))
     for pair in range(NODES // 2):
         two = blocks[:, pair * 128 : pair * 128 + 128]
@@ -326,21 +334,16 @@
     newest[...] = GAIN * (own[...] + from_sides(choose, lift_parts, from_other[...], from_pair[...]))
     to_tiles(newest, tiled)
     high4[...], low4[...] = split(dense(tiled))
-    left_high = jnp.concatenate([high3[...], high4[...]], 0)
-    left_low = jnp.concatenate([low3[...], low4[...]], 0)
-    rows = gram_of(
-        left_high,
-        left_low,
-        jnp.concatenate([high[...], left_high], 0),
-        jnp.concatenate([low[...], left_low], 0),
-    )
+    stack_high = jnp.concatenate([high[...], high3[...], high4[...]], 0)
+    stack_low = jnp.concatenate([low[...], low3[...], low4[...]], 0)
+    between = gram_of(high[32:48, :], low[32:48, :], high3[...], low3[...])
+    rows = gram_of(stack_high[48:], stack_low[48:], stack_high, stack_low)
     gram_low[...] = jnp.zeros((128, 128), F32)
-    gram_low[0:48, 0:48] = gram[...]
+    gram_low[0:48, 0:64] = jnp.concatenate(
+        [gram[...], jnp.concatenate([jnp.zeros((32, 16), F32), between], 0)], 1
+    )
     gram_low[48:80, 0:80] = rows
-    known = gram_low[...]
-    row = lax.broadcasted_iota(jnp.int32, (128, 128), 0) // 16
-    column = lax.broadcasted_iota(jnp.int32, (128, 128), 1) // 16
-    full = jnp.where(row >= column, known, known.T)
+    full = gram_low[...]
     weighted = full[:64] + full[16:80] * (1.0 / GAIN)
     normal = weighted + pltpu.roll(weighted, 112, 1) * (1.0 / GAIN)
     lane = lax.broadcasted_iota(jnp.int32, (16, 128), 1)
@@ -457,36 +460,39 @@
 def local(right_side, start_guess, block_diag, face_lift, face_scale, neighbors, ghost_send, axes):
     sent = jax.ShapeDtypeStruct((GHOST, WIDTH), F32)
     message = jax.ShapeDtypeStruct((2 * GHOST, WIDTH), F32)
-    to_other, to_pair, choose = call(
+    send, near, scale = map(in_hbm, (ghost_send, neighbors.T, face_scale.T))
+    tables = [pltpu.VMEM((FACES, ELEMS), jnp.int32), pltpu.VMEM((FACES, ELEMS), F32)]
+    to_other, to_pair = call(
         pack_kernel,
-        [message, message, jax.ShapeDtypeStruct((ELEMS, 1024), BF16)],
-        [
-            pltpu.VMEM((ELEMS, WIDTH), F32),
-            pltpu.VMEM((FACES, ELEMS), jnp.int32),
-            pltpu.VMEM((FACES, ELEMS), F32),
-            pltpu.VMEM((1, 2 * GHOST), jnp.int32),
+        [message, message],
+        [pltpu.VMEM((ELEMS, WIDTH), F32)]
+        + tables
+        + [
             pltpu.VMEM((ELEMS, 128), F32),
             pltpu.SMEM((1, 2 * GHOST), jnp.int32),
-            pltpu.SemaphoreType.DMA((5,)),
+            pltpu.SemaphoreType.DMA((4,)),
         ],
         [HBM] * 4,
-    )(*map(in_hbm, (ghost_send, start_guess, neighbors.T, face_scale.T)))
+    )(send, in_hbm(start_guess), near, scale)
     from_other = swapped(to_other, axes, 1)
     from_pair = swapped(to_pair, axes, 0)
-    block_parts, lift_parts = call(
+    choose, block_parts, lift_parts = call(
         prep_kernel,
         [
+            jax.ShapeDtypeStruct((ELEMS, 1024), BF16),
             jax.ShapeDtypeStruct((256, ELEMS * NODES), BF16),
             jax.ShapeDtypeStruct((384, FACES * 128), BF16),
         ],
-        [
+        [pltpu.VMEM((1, 2 * GHOST), jnp.int32)]
+        + tables
+        + [
+            pltpu.VMEM((FACES, NODES, NODES), F32),
             pltpu.VMEM((ELEMS, NODES * NODES), F32),
-            pltpu.VMEM((FACES, NODES, NODES), F32),
             pltpu.VMEM((ELEMS, NODES, 128), F32),
-            pltpu.SemaphoreType.DMA((2,)),
+            pltpu.SemaphoreType.DMA((5,)),
         ],
-        [HBM] * 2,
-    )(in_hbm(block_diag), in_hbm(face_lift))
+        [HBM] * 5,
+    )(send, near, scale, in_hbm(face_lift), in_hbm(block_diag))
     tile_scratch = pltpu.VMEM((ELEMS, 8, 128), F32)
     own_call = lambda *args: call(
         first_own_kernel, [FIELD], [tile_scratch] * 2, [VMEM] * 4

time: 94.8 us -> 94.7 us (level)
  no operation moved by 1% of the time
where the time goes in v9:
time: 94.7 us; the launch traced here: 94.3 us
  blocking collectives  45.4 us (48%)
  starting transfers between devices  23.7 us (25%)
  Pallas kernels  16.9 us (18%)
  waiting for transfers between devices  7.19 us (8%)
    all_to_all x1, blocking collectives, local(): mine = lax.all_to_all(halves, (axes[0], axes[2]), 0, 0).sum(0)  28.9 us
    ppermute x8, starting transfers between devices, swapped(): lax.ppermute(block, axes, [(i, i + 1) for i in lower] + [(i + 1, i) for i...  23.7 us
    all_to_all x1, blocking collectives, local(): mine = lax.all_to_all(mine, axes[1], 0, 0).sum(0)  16.5 us
    ppermute x8, waiting for transfers between devices, swapped(): lax.ppermute(block, axes, [(i, i + 1) for i in lower] + [(i + 1, i) for i...  7.19 us
    pallas_call x1, Pallas kernels, local(): call(solve_kernel, [FIELD, FIELD], [pltpu.VMEM((128, 128), F32), pltpu.VM...  2.84 us
    pallas_call x1, Pallas kernels, local(): call(prep_kernel, [jax.ShapeDtypeStruct((ELEMS, 1024), BF16), jax.ShapeDt...  2.23 us
    pallas_call x2, Pallas kernels, local(): call(first_own_kernel, [FIELD], [tile_scratch] * 2, [VMEM] * 4)(*args)[0]  2.12 us
  transfers between devices with their start and end apart: 8, of which 6 were waited for; matrix products, arithmetic and copies ran while one was open for 0% of the time, Pallas kernels for 7%

profile of v9, /device:TPU:1, one launch (start us, length us, event | category | flops | bytes accessed | tf_op | source)
XLA Modules:
  0.0 94.3 jit_solution(9804816545835341535)
XLA Ops:
  0.6 1.0 %shard_map.88 = (f32[8,1024]{1,0:T(8,128)S(1)}, f32[8,1024]{1,0:T(8,128)S(1)}) custom-call(s32[1,8]{1,0:T(1,128)} %send_in.3, f32[32,1024]{1,0:T(8,128)} %guess.3, s32[6,32]{1,0:T(8,128)} %bitcast.4, f32[6,32]{1,0:T(8,128)} %bitcast.6), custom_call_target="tpu_custom_call" | custom-call | tf_op jit(solution)/shard_map/pallas_call | solution.py:465
  1.7 4.5 %collective-permute-start = (f32[8,1024]{1,0:T(8,128)S(1)}, f32[8,1024]{1,0:T(8,128)S(1)}, u32[]{:S(2)}, u32[]{:S(2)}) collective-permute-start(f32[8,1024]{1,0:T(8,128)S(1)} %get-tuple-element.38), channel_id=1, source_target_pairs={{1,2},{3,4},{5,6},{7,8},{9,10},{11,12},{13,14},{15,16},{17,18},{19... | collective-permute-start | bytes 98312 | tf_op jit(solution)/shard_map/ppermute | solution.py:457
  6.2 0.0 copy-start
  6.2 5.1 %collective-permute-start.1 = (f32[8,1024]{1,0:T(8,128)S(1)}, f32[8,1024]{1,0:T(8,128)S(1)}, u32[]{:S(2)}, u32[]{:S(2)}) collective-permute-start(f32[8,1024]{1,0:T(8,128)S(1)} %get-tuple-element.39), channel_id=1, source_target_pairs={{0,1},{2,3},{4,5},{6,7},{8,9},{10,11},{12,13},{14,15},{16,17},{18,... | collective-permute-start | bytes 98312 | tf_op jit(solution)/shard_map/ppermute | solution.py:457
  11.3 2.2 %shard_map.86 = (bf16[32,1024]{1,0:T(8,128)(2,1)S(1)}, bf16[256,2048]{1,0:T(8,128)(2,1)S(1)}, bf16[384,768]{1,0:T(8,128)(2,1)S(1)}) custom-call(s32[1,8]{1,0:T(1,128)} %send_in.3, s32[6,32]{1,0:T(8,128)} %bitcast.5, f32[6,32]{1,0:T(8,128)} %bitcast.7, f32[6,64,64]{2,1,0:T(8,128)} %lift_in.1, f32[32,4096]{1,0:T(8,128)} %blocks_in.1), custom_call_target="tpu_custom_call" | custom-call | tf_op jit(solution)/shard_map/pallas_call | solution.py:479
  13.5 0.0 copy-done
  13.5 0.0 copy-start.1
  13.6 1.1 %shard_map.87.own = f32[32,1024]{1,0:T(8,128)S(1)} custom-call(bf16[32,1024]{1,0:T(8,128)(2,1)S(1)} %get-tuple-element.35.choose, f32[32,1024]{1,0:T(8,128)S(1)} %copy-done, bf16[256,2048]{1,0:T(8,128)(2,1)S(1)} %get-tuple-element.36.block_parts, bf16[384,768]{1,0:T(8,128)(2,1)S(1)} %get-tuple-element.37.lift_parts), custom_call_target="tpu_custom_call" | custom-call | tf_op jit(solution)/shard_map/pallas_call | solution.py:497
  14.6 0.0 collective-permute-done.from_other
  14.6 0.0 collective-permute-done.1.from_pair
  14.6 0.0 copy-done.1
  14.7 0.5 shard_map.89
  15.2 1.9 %collective-permute-start.2 = (f32[4,1024]{1,0:T(4,128)S(1)}, f32[4,1024]{1,0:T(4,128)S(1)}, u32[]{:S(2)}, u32[]{:S(2)}) collective-permute-start(f32[4,1024]{1,0:T(4,128)S(1)} %get-tuple-element.41), channel_id=1, source_target_pairs={{0,1},{2,3},{4,5},{6,7},{8,9},{10,11},{12,13},{14,15},{16,17},{18,... | collective-permute-start | bytes 49160 | tf_op jit(solution)/shard_map/ppermute | solution.py:457
  17.1 1.1 %shard_map.90.own = f32[32,1024]{1,0:T(8,128)S(1)} custom-call(bf16[32,1024]{1,0:T(8,128)(2,1)S(1)} %get-tuple-element.35.choose, f32[32,1024]{1,0:T(8,128)S(1)} %get-tuple-element.40.vector.first, bf16[256,2048]{1,0:T(8,128)(2,1)S(1)} %get-tuple-element.36.block_parts, bf16[384,768]{1,0:T(8,128)(2,1)S(1)} %get-tuple-element.37.lift_parts), custom_call_target="tpu_custom_call" | custom-call | tf_op jit(solution)/shard_map/pallas_call | solution.py:497
  18.2 0.1 collective-permute-done.2.from_pair
  18.3 0.5 shard_map.91
  18.8 1.9 %collective-permute-start.3 = (f32[8,1024]{1,0:T(8,128)S(1)}, f32[8,1024]{1,0:T(8,128)S(1)}, u32[]{:S(2)}, u32[]{:S(2)}) collective-permute-start(f32[8,1024]{1,0:T(8,128)S(1)} %get-tuple-element.44), channel_id=1, source_target_pairs={{1,2},{3,4},{5,6},{7,8},{9,10},{11,12},{13,14},{15,16},{17,18},{19... | collective-permute-start | bytes 98312 | tf_op jit(solution)/shard_map/ppermute | solution.py:457
  20.7 0.4 shard_map.92.missing
  21.1 2.9 %collective-permute-done.3.message = f32[8,1024]{1,0:T(8,128)S(1)} collective-permute-done((f32[8,1024]{1,0:T(8,128)S(1)}, f32[8,1024]{1,0:T(8,128)S(1)}, u32[]{:S(2)}, u32[]{:S(2)}) %collective-permute-start.3) | collective-permute-done | bytes 32800 | tf_op jit(solution)/shard_map/ppermute | solution.py:457
  24.0 1.7 %shard_map.93 = (f32[32,1024]{1,0:T(8,128)S(1)}, f32[32,1024]{1,0:T(8,128)S(1)}, f32[4,1024]{1,0:T(4,128)S(1)}, f32[8,1024]{1,0:T(8,128)S(1)}) custom-call(bf16[32,1024]{1,0:T(8,128)(2,1)S(1)} %get-tuple-element.35.choose, f32[32,1024]{1,0:T(8,128)S(1)} %get-tuple-element.43.partial, f32[8,1024]{1,0:T(8,128)S(1)} %collective-permute-done.3.message, ...), custom_call_target="tpu_custom_call" | custom-call | tf_op jit(solution)/shard_map/pallas_call | solution.py:517
  25.7 1.9 %collective-permute-start.4 = (f32[8,1024]{1,0:T(8,128)S(1)}, f32[8,1024]{1,0:T(8,128)S(1)}, u32[]{:S(2)}, u32[]{:S(2)}) collective-permute-start(f32[8,1024]{1,0:T(8,128)S(1)} %get-tuple-element.47), channel_id=1, source_target_pairs={{0,1},{2,3},{4,5},{6,7},{8,9},{10,11},{12,13},{14,15},{16,17},{18,... | collective-permute-start | bytes 98312 | tf_op jit(solution)/shard_map/ppermute | solution.py:457
  27.6 0.4 shard_map.94.missing
  28.0 0.8 collective-permute-done.4.message
  28.8 1.7 %shard_map.95 = (f32[32,1024]{1,0:T(8,128)S(1)}, f32[32,1024]{1,0:T(8,128)S(1)}, f32[4,1024]{1,0:T(4,128)S(1)}, f32[8,1024]{1,0:T(8,128)S(1)}) custom-call(bf16[32,1024]{1,0:T(8,128)(2,1)S(1)} %get-tuple-element.35.choose, f32[32,1024]{1,0:T(8,128)S(1)} %get-tuple-element.46.own, f32[8,1024]{1,0:T(8,128)S(1)} %collective-permute-done.4.message, ...), custom_call_target="tpu_custom_call" | custom-call | tf_op jit(solution)/shard_map/pallas_call | solution.py:523
  30.5 1.9 %collective-permute-start.5 = (f32[8,1024]{1,0:T(8,128)S(1)}, f32[8,1024]{1,0:T(8,128)S(1)}, u32[]{:S(2)}, u32[]{:S(2)}) collective-permute-start(f32[8,1024]{1,0:T(8,128)S(1)} %get-tuple-element.51), channel_id=1, source_target_pairs={{1,2},{3,4},{5,6},{7,8},{9,10},{11,12},{13,14},{15,16},{17,18},{19... | collective-permute-start | bytes 98312 | tf_op jit(solution)/shard_map/ppermute | solution.py:457
  32.4 0.8 shard_map.96
  33.2 2.5 %collective-permute-done.5.message = f32[8,1024]{1,0:T(8,128)S(1)} collective-permute-done((f32[8,1024]{1,0:T(8,128)S(1)}, f32[8,1024]{1,0:T(8,128)S(1)}, u32[]{:S(2)}, u32[]{:S(2)}) %collective-permute-start.5) | collective-permute-done | bytes 32800 | tf_op jit(solution)/shard_map/ppermute | solution.py:457
  35.7 0.5 shard_map.97
  36.2 1.9 %collective-permute-start.6 = (f32[4,1024]{1,0:T(4,128)S(1)}, f32[4,1024]{1,0:T(4,128)S(1)}, u32[]{:S(2)}, u32[]{:S(2)}) collective-permute-start(f32[4,1024]{1,0:T(4,128)S(1)} %get-tuple-element.59), channel_id=1, source_target_pairs={{0,1},{2,3},{4,5},{6,7},{8,9},{10,11},{12,13},{14,15},{16,17},{18,... | collective-permute-start | bytes 49160 | tf_op jit(solution)/shard_map/ppermute | solution.py:457
  38.2 1.1 %shard_map.98 = (f32[32,1024]{1,0:T(8,128)S(1)}, bf16[16,2048]{1,0:T(8,128)(2,1)S(1)}, bf16[16,2048]{1,0:T(8,128)(2,1)S(1)}) custom-call(bf16[32,1024]{1,0:T(8,128)(2,1)S(1)} %get-tuple-element.35.choose, f32[32,1024]{1,0:T(8,128)S(1)} %get-tuple-element.56.vector, bf16[256,2048]{1,0:T(8,128)(2,1)S(1)} %get-tuple-element.36.block_parts, ...), custom_call_target="tpu_custom_call" | custom-call | tf_op jit(solution)/shard_map/pallas_call | solution.py:538
  39.2 0.1 collective-permute-done.6.from_pair
  39.3 1.1 %shard_map.99 = (bf16[16,2048]{1,0:T(8,128)(2,1)S(1)}, bf16[16,2048]{1,0:T(8,128)(2,1)S(1)}, f32[2,7,2,128]{3,2,1,0:T(2,128)S(1)}) custom-call(bf16[32,1024]{1,0:T(8,128)(2,1)S(1)} %get-tuple-element.35.choose, f32[32,1024]{1,0:T(8,128)S(1)} %get-tuple-element.57.own, f32[4,1024]{1,0:T(4,128)S(1)} %get-tuple-element.58.from_other, ...), custom_call_target="tpu_custom_call" | custom-call | tf_op jit(solution)/shard_map/pallas_call | solution.py:541
  40.4 0.1 broadcast_in_dim.4
  40.5 28.9 %all_to_all.10 = f32[32,7,2,128]{3,2,1,0:T(2,128)S(1)} all-to-all(f32[32,7,2,128]{3,2,1,0:T(2,128)S(1)} %bitcast.3), channel_id=1, replica_groups=mesh['outer'=4,'inner'=16,'narrow'=8] {'outer','narrow'}, dimensions={0} | all-to-all | bytes 458752 | tf_op jit(solution)/shard_map/all_to_all | solution.py:550
  69.4 0.1 reduce_sum.18
  69.5 16.5 %all_to_all.11 = f32[16,7,2,128]{3,2,1,0:T(2,128)S(1)} all-to-all(f32[16,7,2,128]{3,2,1,0:T(2,128)S(1)} %broadcast_in_dim.5), channel_id=1, replica_groups=mesh['outer'=4,'inner'=16,'narrow'=8] {'inner'}, dimensions={0} | all-to-all | bytes 229376 | tf_op jit(solution)/shard_map/all_to_all | solution.py:552
  86.0 0.1 reduce_sum.19.mine
  86.1 4.6 %collective-permute-start.7 = (f32[7,2,128]{2,1,0:T(2,128)S(1)}, f32[7,2,128]{2,1,0:T(2,128)S(1)}, u32[]{:S(2)}, u32[]{:S(2)}) collective-permute-start(f32[7,2,128]{2,1,0:T(2,128)S(1)} %reduce_sum.19.mine), channel_id=1, source_target_pairs={{0,1},{2,3},{4,5},{6,7},{8,9},{10,11},{12,13},{14,15},{16,17},{18,... | collective-permute-start | bytes 21512 | tf_op jit(solution)/shard_map/ppermute | solution.py:457
  90.6 0.8 collective-permute-done.7.theirs
  91.5 2.8 %shard_map.100 = (f32[32,1024]{1,0:T(8,128)}, f32[32,1024]{1,0:T(8,128)}) custom-call(f32[7,2,128]{2,1,0:T(2,128)S(1)} %reduce_sum.19.mine, f32[7,2,128]{2,1,0:T(2,128)S(1)} %collective-permute-done.7.theirs, bf16[48,2048]{1,0:T(8,128)(2,1)S(1)} %get-tuple-element.60.high, bf16[48,2048]{1,0:T(8,128)(2,1)S(1)} %get-tuple-element.61.low, ...), custom_call_target="tpu_custom_call" | custom-call | tf_op jit(solution)/shard_map/pallas_call | solution.py:555
  (1 shorter events, 0.0 us)
Async XLA Ops:
  1.7 12.9 %collective-permute-start = (f32[8,1024]{1,0:T(8,128)S(1)}, f32[8,1024]{1,0:T(8,128)S(1)}, u32[]{:S(2)}, u32[]{:S(2)}) collective-permute-start(f32[8,1024]{1,0:T(8,128)S(1)} %get-tuple-element.38), channel_id=1, source_target_pairs={{1,2},{3,4},{5,6},{7,8},{9,10},{11,12},{13,14},{15,16},{17,18},{19... | collective-permute-start | bytes 98312 | tf_op jit(solution)/shard_map/ppermute | solution.py:457
  6.2 7.3 %copy-start = (f32[32,1024]{1,0:T(8,128)S(1)}, f32[32,1024]{1,0:T(8,128)}, u32[]{:S(2)}) copy-start(f32[32,1024]{1,0:T(8,128)} %guess.3) | copy-start | bytes 393220
  6.2 8.4 %collective-permute-start.1 = (f32[8,1024]{1,0:T(8,128)S(1)}, f32[8,1024]{1,0:T(8,128)S(1)}, u32[]{:S(2)}, u32[]{:S(2)}) collective-permute-start(f32[8,1024]{1,0:T(8,128)S(1)} %get-tuple-element.39), channel_id=1, source_target_pairs={{0,1},{2,3},{4,5},{6,7},{8,9},{10,11},{12,13},{14,15},{16,17},{18,... | collective-permute-start | bytes 98312 | tf_op jit(solution)/shard_map/ppermute | solution.py:457
  13.5 1.1 %copy-start.1 = (f32[32,1024]{1,0:T(8,128)S(1)}, f32[32,1024]{1,0:T(8,128)}, u32[]{:S(2)}) copy-start(f32[32,1024]{1,0:T(8,128)} %right.1) | copy-start | bytes 393220
  15.2 3.1 %collective-permute-start.2 = (f32[4,1024]{1,0:T(4,128)S(1)}, f32[4,1024]{1,0:T(4,128)S(1)}, u32[]{:S(2)}, u32[]{:S(2)}) collective-permute-start(f32[4,1024]{1,0:T(4,128)S(1)} %get-tuple-element.41), channel_id=1, source_target_pairs={{0,1},{2,3},{4,5},{6,7},{8,9},{10,11},{12,13},{14,15},{16,17},{18,... | collective-permute-start | bytes 49160 | tf_op jit(solution)/shard_map/ppermute | solution.py:457
  18.8 5.2 %collective-permute-start.3 = (f32[8,1024]{1,0:T(8,128)S(1)}, f32[8,1024]{1,0:T(8,128)S(1)}, u32[]{:S(2)}, u32[]{:S(2)}) collective-permute-start(f32[8,1024]{1,0:T(8,128)S(1)} %get-tuple-element.44), channel_id=1, source_target_pairs={{1,2},{3,4},{5,6},{7,8},{9,10},{11,12},{13,14},{15,16},{17,18},{19... | collective-permute-start | bytes 98312 | tf_op jit(solution)/shard_map/ppermute | solution.py:457
  25.7 3.1 %collective-permute-start.4 = (f32[8,1024]{1,0:T(8,128)S(1)}, f32[8,1024]{1,0:T(8,128)S(1)}, u32[]{:S(2)}, u32[]{:S(2)}) collective-permute-start(f32[8,1024]{1,0:T(8,128)S(1)} %get-tuple-element.47), channel_id=1, source_target_pairs={{0,1},{2,3},{4,5},{6,7},{8,9},{10,11},{12,13},{14,15},{16,17},{18,... | collective-permute-start | bytes 98312 | tf_op jit(solution)/shard_map/ppermute | solution.py:457
  30.5 5.2 %collective-permute-start.5 = (f32[8,1024]{1,0:T(8,128)S(1)}, f32[8,1024]{1,0:T(8,128)S(1)}, u32[]{:S(2)}, u32[]{:S(2)}) collective-permute-start(f32[8,1024]{1,0:T(8,128)S(1)} %get-tuple-element.51), channel_id=1, source_target_pairs={{1,2},{3,4},{5,6},{7,8},{9,10},{11,12},{13,14},{15,16},{17,18},{19... | collective-permute-start | bytes 98312 | tf_op jit(solution)/shard_map/ppermute | solution.py:457
  36.2 3.1 %collective-permute-start.6 = (f32[4,1024]{1,0:T(4,128)S(1)}, f32[4,1024]{1,0:T(4,128)S(1)}, u32[]{:S(2)}, u32[]{:S(2)}) collective-permute-start(f32[4,1024]{1,0:T(4,128)S(1)} %get-tuple-element.59), channel_id=1, source_target_pairs={{0,1},{2,3},{4,5},{6,7},{8,9},{10,11},{12,13},{14,15},{16,17},{18,... | collective-permute-start | bytes 49160 | tf_op jit(solution)/shard_map/ppermute | solution.py:457
  86.1 5.4 %collective-permute-start.7 = (f32[7,2,128]{2,1,0:T(2,128)S(1)}, f32[7,2,128]{2,1,0:T(2,128)S(1)}, u32[]{:S(2)}, u32[]{:S(2)}) collective-permute-start(f32[7,2,128]{2,1,0:T(2,128)S(1)} %reduce_sum.19.mine), channel_id=1, source_target_pairs={{0,1},{2,3},{4,5},{6,7},{8,9},{10,11},{12,13},{14,15},{16,17},{18,... | collective-permute-start | bytes 21512 | tf_op jit(solution)/shard_map/ppermute | solution.py:457
